TPU v7x, 32 devices: a whole 2x2x4 slice. The times are simulated.
32 devices in a mesh: chan: 4 (over x, core), tm: 2 (over y), stat: 4 (over z).
Axes of the slice: x: 2, y: 2, z: 4, core: 2. Of those that a mesh axis runs over, the one named last changes fastest.
Arguments:
- voltages: bfloat16 [8, 2, 512, 4096], P('chan', None, 'stat', 'tm'), may hold values from -6 to 6
- ref_index: int32 [8], replicated, may hold values from 0 to 511
- positions: int32 [4096], P('tm'), may hold values from 0 to 255
- aperture_weight: float32 [256], replicated, may hold values from 0.25 to 4
Outputs:
- coefficients: float32 [512, 8, 8, 128], P(('stat', 'tm', 'chan'))
Inputs may be any that keep to these rules, and one draw needn't show every extreme that they name: Each entry of ref_index is a station number; entries may repeat. Each entry of positions is a raster cell index of the 16 x 16 raster.
All inputs are finite; a program needn't handle non-finite values.
Results may differ from a plain program's by a relative error of at most 0.0003.
Values may be sent and summed in bfloat16 or wider, within the bound.
No kernel may reach another device: no remote copies, remote signals or barrier semaphores. Data moves between devices by JAX's collectives and lax.ppermute only.
A program may use at most 128 MiB of HBM per device.

v0:
```python
import functools
import math

import jax
import jax.numpy as jnp
import numpy as np
from jax import lax
from jax.experimental import pallas as pl
from jax.experimental.pallas import tpu as pltpu
from jax.sharding import PartitionSpec as P

RASTER = 16
ZERN = 64
CELLS = RASTER * RASTER
HIGHEST = lax.Precision.HIGHEST
ROWS = (((1,), (1,)), ((), ()))


def zernike_rows():
    cell_ids = np.arange(CELLS)
    grid_x = ((cell_ids // RASTER - RASTER // 2) + 0.5) / (RASTER / 2.0)
    grid_y = ((cell_ids % RASTER - RASTER // 2) + 0.5) / (RASTER / 2.0)
    radius_sq = grid_x * grid_x + grid_y * grid_y
    in_disk = np.where(radius_sq <= 1.0, 1.0, 0.0)
    rows = []
    degree = 0
    while len(rows) < ZERN:
        for azimuth in range(-degree, degree + 1, 2):
            if len(rows) == ZERN:
                break
            order = abs(azimuth)
            power = (grid_x + 1j * grid_y) ** order
            radial = np.zeros_like(grid_x)
            for k in range((degree - order) // 2 + 1):
                weight = (
                    (-1) ** k
                    * math.factorial(degree - k)
                    / (
                        math.factorial(k)
                        * math.factorial((degree + order) // 2 - k)
                        * math.factorial((degree - order) // 2 - k)
                    )
                )
                radial = radial + weight * radius_sq ** ((degree - 2 * k - order) // 2)
            if azimuth > 0:
                row = radial * power.real * math.sqrt(2.0 * (degree + 1))
            elif azimuth < 0:
                row = radial * power.imag * math.sqrt(2.0 * (degree + 1))
            else:
                row = radial * math.sqrt(degree + 1.0)
            rows.append(row * in_disk)
        degree += 1
    return np.stack(rows).astype(np.float32)


def dft_rows():
    cell_ids = np.arange(CELLS)
    a = cell_ids // RASTER - RASTER // 2
    b = cell_ids % RASTER - RASTER // 2
    phases = (a[:, None] * a[None, :] + b[:, None] * b[None, :]) % RASTER
    angles = phases * (2.0 * math.pi / RASTER)
    return np.concatenate([np.cos(angles), -np.sin(angles)], axis=1).astype(np.float32)


def pick_kernel(index_ref, volt_ref, out_ref):
    stations = volt_ref.shape[2]
    refs = out_ref.shape[2]
    first = lax.axis_index("stat") * stations
    row = lax.broadcasted_iota(jnp.int32, (refs, stations), 0)
    lane = lax.broadcasted_iota(jnp.int32, (refs, stations), 1)
    wanted = jnp.zeros((refs, stations), jnp.int32)
    for r in range(refs):
        wanted = jnp.where(row == r, index_ref[r] - first, wanted)
    select = jnp.where(lane == wanted, 1.0, 0.0).astype(jnp.bfloat16)
    out_ref[0, 0] = jnp.dot(
        select, volt_ref[0, 0], preferred_element_type=jnp.float32
    ).astype(jnp.bfloat16)


def pick(ref_index, voltages):
    chans, parts, stations, times = voltages.shape
    refs = ref_index.shape[0]
    return pl.pallas_call(
        pick_kernel,
        grid=(chans, parts),
        in_specs=[
            pl.BlockSpec(memory_space=pltpu.SMEM),
            pl.BlockSpec((1, 1, stations, times), lambda c, k: (c, k, 0, 0)),
        ],
        out_specs=pl.BlockSpec((1, 1, refs, times), lambda c, k: (c, k, 0, 0)),
        out_shape=jax.ShapeDtypeStruct((chans, parts, refs, times), jnp.bfloat16),
        name="pick_references",
    )(ref_index, voltages)


def invert(gram):
    size = gram.shape[0]
    row = lax.broadcasted_iota(jnp.int32, (size, size), 0)
    lane = lax.broadcasted_iota(jnp.int32, (size, size), 1)
    work = jnp.concatenate([gram, jnp.where(row == lane, 1.0, 0.0)], axis=1)
    row = lax.broadcasted_iota(jnp.int32, work.shape, 0)
    for k in range(size):
        pivot = work[k : k + 1, :] / work[k : k + 1, k : k + 1]
        work = jnp.where(row == k, pivot, work - work[:, k : k + 1] * pivot)
    return work[:, size:]


def split(value, parts):
    pieces = []
    for _ in range(parts):
        piece = value.astype(jnp.bfloat16)
        pieces.append(piece)
        value = value - piece.astype(jnp.float32)
    return pieces


def tables_kernel(scale, weight_ref, zern_ref, dft_ref, pos_ref, out_ref):
    zern = zern_ref[...]
    weighted = zern * weight_ref[...]
    gram = lax.dot_general(weighted, zern, ROWS, precision=HIGHEST, preferred_element_type=jnp.float32)
    field = jnp.dot(weighted, dft_ref[...], precision=HIGHEST, preferred_element_type=jnp.float32)
    fit = jnp.dot(invert(gram), field, precision=HIGHEST, preferred_element_type=jnp.float32) * scale
    fit = jnp.concatenate([fit[:, :CELLS], fit[:, CELLS:]], axis=0)
    pieces = split(fit, 3)
    times = pos_ref.shape[1]
    step = 512
    cell = lax.broadcasted_iota(jnp.int32, (CELLS, step), 0)
    for begin in range(0, times, step):
        onehot = jnp.where(cell == pos_ref[:, begin : begin + step], 1.0, 0.0).astype(jnp.bfloat16)
        total = jnp.dot(pieces[0], onehot, preferred_element_type=jnp.float32)
        for piece in pieces[1:]:
            total = total + jnp.dot(piece, onehot, preferred_element_type=jnp.float32)
        out_ref[:, begin : begin + step] = total


def tables(weight, positions, scale):
    times = positions.shape[0]
    return pl.pallas_call(
        functools.partial(tables_kernel, scale),
        out_shape=jax.ShapeDtypeStruct((2 * ZERN, times), jnp.float32),
        name="fit_tables",
        cost_estimate=pl.CostEstimate(flops=4_000_000_000, bytes_accessed=2_000_000, transcendentals=0),
    )(weight.reshape(1, CELLS), jnp.asarray(zernike_rows()), jnp.asarray(dft_rows()), positions.reshape(1, times))


STEP = 512


def correlate_kernel(volt_ref, *rest):
    ref_parts = rest[:-6]
    table_ref, out_ref, refs_ref, left_a, left_b, total_ref = rest[-6:]
    chans, parts, stations, times = volt_ref.shape
    refs = refs_ref.shape[2]
    steps = times // STEP
    picked = ref_parts[0][...]
    for other in ref_parts[1:]:
        picked = picked + other[...]
    refs_ref[...] = picked.astype(jnp.float32)

    def produce(chan, step, left_ref):
        span = pl.ds(step * STEP, STEP)
        for r in range(refs):
            real = refs_ref[chan, 0, r : r + 1, span]
            imag = refs_ref[chan, 1, r : r + 1, span]
            for half in range(0, ZERN, 16):
                table_r = table_ref[half : half + 16, span]
                table_i = table_ref[ZERN + half : ZERN + half + 16, span]
                for at, value in (
                    (half, real * table_r + imag * table_i),
                    (ZERN + half, real * table_i - imag * table_r),
                ):
                    high, low = split(value, 2)
                    rows = pl.ds(r * 2 * ZERN + at, 16)
                    left_ref[rows, 0:STEP] = high
                    left_ref[rows, STEP : 2 * STEP] = low

    def consume(chan, step, left_ref):
        span = pl.ds(step * STEP, STEP)
        right = volt_ref[chan, :, :, span].reshape(parts * stations, STEP)
        right = jnp.concatenate([right, right], axis=1)
        product = lax.dot_general(left_ref[...], right, ROWS, preferred_element_type=jnp.float32)
        if step == 0:
            total_ref[...] = product
        else:
            total_ref[...] += product

    def finish(chan):
        for r in range(refs):
            top = total_ref[r * 2 * ZERN : r * 2 * ZERN + ZERN, :]
            low = total_ref[r * 2 * ZERN + ZERN : (r + 1) * 2 * ZERN, :]
            real = top[:, :stations] - low[:, stations:]
            imag = top[:, stations:] + low[:, :stations]
            both = jnp.concatenate([real, imag], axis=0).T
            out_ref[chan, pl.ds(r, stations, stride=refs), :] = both

    order = [(chan, step) for chan in range(chans) for step in range(steps)]
    buffers = (left_a, left_b)
    produce(*order[0], buffers[0])
    for i, (chan, step) in enumerate(order):
        if i + 1 < len(order):
            produce(*order[i + 1], buffers[(i + 1) % 2])
        consume(chan, step, buffers[i % 2])
        if step == steps - 1:
            finish(chan)


def correlate(voltages, ref_parts, table):
    chans, parts, stations, times = voltages.shape
    refs = ref_parts[0].shape[2]
    vmem = pl.BlockSpec(memory_space=pltpu.VMEM)
    return pl.pallas_call(
        correlate_kernel,
        in_specs=[vmem] * (2 + len(ref_parts)),
        out_specs=vmem,
        out_shape=jax.ShapeDtypeStruct((chans, stations * refs, 2 * ZERN), jnp.float32),
        scratch_shapes=[
            pltpu.VMEM((chans, parts, refs, times), jnp.float32),
            pltpu.VMEM((refs * 2 * ZERN, 2 * STEP), jnp.bfloat16),
            pltpu.VMEM((refs * 2 * ZERN, 2 * STEP), jnp.bfloat16),
            pltpu.VMEM((refs * 2 * ZERN, parts * stations), jnp.float32),
        ],
        compiler_params=pltpu.CompilerParams(vmem_limit_bytes=40 * 2**20),
        cost_estimate=pl.CostEstimate(flops=8_600_000_000, bytes_accessed=5_000_000, transcendentals=0),
        name="correlate",
    )(voltages, *ref_parts, table)


def collect_kernel(*refs):
    *ins, out_ref = refs
    chan = lax.axis_index("chan")
    chan_count = lax.axis_size("chan")
    tm_count = len(ins) // chan_count
    for dc in range(chan_count):
        total = ins[dc][...]
        for dt in range(1, tm_count):
            total = total + ins[dt * chan_count + dc][...]
        source = jnp.bitwise_xor(chan, dc)
        for c in range(total.shape[0]):
            out_ref[:, source * total.shape[0] + c] = total[c]


def collect(pieces, chan_count):
    chans, stations, refs, terms = pieces[0].shape
    vmem = pl.BlockSpec(memory_space=pltpu.VMEM)
    return pl.pallas_call(
        collect_kernel,
        in_specs=[vmem] * len(pieces),
        out_specs=vmem,
        out_shape=jax.ShapeDtypeStruct((stations, chans * chan_count, refs, terms), jnp.float32),
        name="sum_time_blocks",
    )(*pieces)


def on_device(voltages, ref_index, positions, aperture_weight):
    chans, parts, stations, times = voltages.shape
    refs = ref_index.shape[0]
    stat_count = lax.axis_size("stat")
    tm_count = lax.axis_size("tm")
    chan_count = lax.axis_size("chan")
    picked = pick(ref_index, voltages)
    ref_parts = [picked]
    for shift in range(1, stat_count):
        ref_parts.append(
            lax.ppermute(picked, "stat", [(i, (i + shift) % stat_count) for i in range(stat_count)])
        )
    scale = (tm_count * times / CELLS) ** (-0.5)
    table = tables(aperture_weight, positions, scale)
    sums = correlate(voltages, ref_parts, table)
    owners = tm_count * chan_count
    sums = sums.reshape(chans, owners, stations // owners, refs, 2 * ZERN)
    chan = lax.axis_index("chan")
    tm = lax.axis_index("tm")
    pieces = []
    for dt in range(tm_count):
        for dc in range(chan_count):
            owner = (tm ^ dt) * chan_count + (chan ^ dc)
            block = lax.dynamic_index_in_dim(sums, owner, 1, keepdims=False)
            if dt or dc:
                pairs = [
                    (c * tm_count + t, (c ^ dc) * tm_count + (t ^ dt))
                    for c in range(chan_count)
                    for t in range(tm_count)
                ]
                block = lax.ppermute(block, ("chan", "tm"), pairs)
            pieces.append(block)
    return collect(pieces, chan_count)


def solution(mesh):
    in_specs = (P("chan", None, "stat", "tm"), P(), P("tm"), P())
    out_specs = P(("stat", "tm", "chan"), None, None, None)
    return jax.shard_map(
        on_device, mesh=mesh, in_specs=in_specs, out_specs=out_specs, check_vma=False
    )
```

profile of v0, /device:TPU:0, one launch (start us, length us, event | category | flops | bytes accessed | tf_op | source)
XLA Modules:
  0.0 44.5 jit_solution(7414374241460341430)
XLA Ops:
  0.0 3.7 %pick_references.1.rest_0_ = bf16[2,2,8,2048]{3,2,1,0:T(8,128)(2,1)} custom-call(s32[8]{0:T(128)} %index_ref.1, bf16[2,2,128,2048]{3,2,1,0:T(8,128)(2,1)} %volt_ref.3), custom_call_target="tpu_custom_call" | custom-call | tf_op jit(solution)/shard_map/pick_references/pallas_call | solution.py:83
  3.7 3.0 %collective-permute-start = (bf16[2,2,8,2048]{3,2,1,0:T(8,128)(2,1)}, bf16[2,2,8,2048]{3,2,1,0:T(8,128)(2,1)S(1)}, u32[]{:S(2)}, u32[]{:S(2)}) collective-permute-start(bf16[2,2,8,2048]{3,2,1,0:T(8,128)(2,1)} %pick_references.1.rest_0_), channel_id=1, source_target_pairs={{0,1},{1,2},{2,3},{3,0},{4,5},{5,6},{6,7},{7,4},{8,9},{9,10},{10,1... | collective-permute-start | bytes 393224 | tf_op jit(solution)/shard_map/ppermute | solution.py:264
  6.8 2.6 %collective-permute-start.1 = (bf16[2,2,8,2048]{3,2,1,0:T(8,128)(2,1)}, bf16[2,2,8,2048]{3,2,1,0:T(8,128)(2,1)S(1)}, u32[]{:S(2)}, u32[]{:S(2)}) collective-permute-start(bf16[2,2,8,2048]{3,2,1,0:T(8,128)(2,1)} %pick_references.1.rest_0_), channel_id=1, source_target_pairs={{0,2},{1,3},{2,0},{3,1},{4,6},{5,7},{6,4},{7,5},{8,10},{9,11},{10,... | collective-permute-start | bytes 393224 | tf_op jit(solution)/shard_map/ppermute | solution.py:264
  9.3 1.3 %collective-permute-start.2 = (bf16[2,2,8,2048]{3,2,1,0:T(8,128)(2,1)}, bf16[2,2,8,2048]{3,2,1,0:T(8,128)(2,1)S(1)}, u32[]{:S(2)}, u32[]{:S(2)}) collective-permute-start(bf16[2,2,8,2048]{3,2,1,0:T(8,128)(2,1)} %pick_references.1.rest_0_), channel_id=1, source_target_pairs={{0,3},{1,0},{2,1},{3,2},{4,7},{5,4},{6,5},{7,6},{8,11},{9,8},{10,9... | collective-permute-start | bytes 393224 | tf_op jit(solution)/shard_map/ppermute | solution.py:264
  10.7 0.0 copy-start
  10.7 0.0 copy-start.1
  10.7 8.8 %fit_tables.1.rest_4_ = f32[128,2048]{1,0:T(8,128)} custom-call(f32[1,256]{1,0:T(1,128)} %bitcast.37, f32[64,256]{1,0:T(8,128)} %constant.42.clone.zern_ref, f32[256,512]{1,0:T(8,128)} %constant.43.clone.dft_ref, s32[1,2048]{1,0:T(1,128)} %bitcast.36), custom_call_target="tpu_custom_call" | custom-call | flops 4000000000 | bytes 2000000 | tf_op jit(solution)/shard_map/fit_tables/pallas_call | solution.py:138
  19.5 0.0 collective-permute-done.rest_1_
  19.5 0.0 collective-permute-done.1.rest_2_
  19.5 0.0 collective-permute-done.2.rest_3_
  19.5 0.0 copy-done
  19.6 0.0 copy-done.1
  19.6 0.0 copy-start.2
  19.6 1.2 %copy-done.2 = f32[128,2048]{1,0:T(8,128)S(1)} copy-done((f32[128,2048]{1,0:T(8,128)S(1)}, f32[128,2048]{1,0:T(8,128)}, u32[]{:S(2)}) %copy-start.2) | copy-done | bytes 1048600
  20.8 5.1 %correlate.1 = f32[2,1024,128]{2,1,0:T(8,128)S(1)} custom-call(bf16[2,2,128,2048]{3,2,1,0:T(8,128)(2,1)S(1)} %copy-done, bf16[2,2,8,2048]{3,2,1,0:T(8,128)(2,1)S(1)} %copy-done.1, bf16[2,2,8,2048]{3,2,1,0:T(8,128)(2,1)S(1)} %collective-permute-done.rest_1_, bf16[2,2,8,2048]{3,2,1,0:T(8,128)(2,1)S(1)} %collective-permute-done.1.rest_2_, ...), custom_call_target="tpu_custom_call" | custom-call | flops 8600000512 | bytes 5000000 | tf_op jit(solution)/shard_map/correlate/pallas_call | solution.py:211
  25.9 0.8 %dynamic-slice_bitcast_fusion = (f32[2,16,8,128]{3,2,1,0:T(8,128)S(1)}, f32[2,16,8,128]{3,2,1,0:T(8,128)S(1)}, f32[2,16,8,128]{3,2,1,0:T(8,128)S(1)}, f32[2,16,8...) fusion(f32[2,8,16,8,128]{4,3,2,1,0:T(8,128)S(1)} %bitcast.35, ...), kind=kLoop, calls=%fused_computation | loop fusion | bytes 2097184 | tf_op jit(solution)/shard_map/jit(dynamic_index_in_dim)/squeeze | solution.py:277
  26.6 0.0 collective-permute-start.3
  26.6 1.5 %collective-permute-start.4 = (f32[2,16,8,128]{3,2,1,0:T(8,128)S(1)}, f32[2,16,8,128]{3,2,1,0:T(8,128)S(1)}, u32[]{:S(2)}, u32[]{:S(2)}) collective-permute-start(f32[2,16,8,128]{3,2,1,0:T(8,128)S(1)} %get-tuple-element.10), channel_id=1, source_target_pairs={{0,16},{4,20},{8,24},{12,28},{16,0},{20,4},{24,8},{28,12},{1,17},{... | collective-permute-start | bytes 393224 | tf_op jit(solution)/shard_map/ppermute | solution.py:284
  28.1 0.4 collective-permute-start.5
  28.5 1.5 %collective-permute-start.6 = (f32[2,16,8,128]{3,2,1,0:T(8,128)S(1)}, f32[2,16,8,128]{3,2,1,0:T(8,128)S(1)}, u32[]{:S(2)}, u32[]{:S(2)}) collective-permute-start(f32[2,16,8,128]{3,2,1,0:T(8,128)S(1)} %get-tuple-element.8), channel_id=1, source_target_pairs={{0,4},{4,0},{8,12},{12,8},{16,20},{20,16},{24,28},{28,24},{1,5},{5... | collective-permute-start | bytes 393224 | tf_op jit(solution)/shard_map/ppermute | solution.py:284
  30.0 0.1 collective-permute-start.7
  30.1 0.0 collective-permute-done.3.refs_1_
  30.1 0.0 copy-start.3
  30.1 2.4 %collective-permute-start.8 = (f32[2,16,8,128]{3,2,1,0:T(8,128)S(1)}, f32[2,16,8,128]{3,2,1,0:T(8,128)S(1)}, u32[]{:S(2)}, u32[]{:S(2)}) collective-permute-start(f32[2,16,8,128]{3,2,1,0:T(8,128)S(1)} %get-tuple-element.6), channel_id=1, source_target_pairs={{0,20},{4,16},{8,28},{12,24},{16,4},{20,0},{24,12},{28,8},{1,21},{... | collective-permute-start | bytes 393224 | tf_op jit(solution)/shard_map/ppermute | solution.py:284
  32.6 0.3 collective-permute-done.4.refs_2_
  32.9 0.0 copy-start.4
  32.9 1.4 %collective-permute-start.9 = (f32[2,16,8,128]{3,2,1,0:T(8,128)S(1)}, f32[2,16,8,128]{3,2,1,0:T(8,128)S(1)}, u32[]{:S(2)}, u32[]{:S(2)}) collective-permute-start(f32[2,16,8,128]{3,2,1,0:T(8,128)S(1)} %get-tuple-element.5), channel_id=1, source_target_pairs={{0,28},{4,24},{8,20},{12,16},{16,12},{20,8},{24,4},{28,0},{1,29},{... | collective-permute-start | bytes 393224 | tf_op jit(solution)/shard_map/ppermute | solution.py:284
  34.3 0.6 %collective-permute-done.5.refs_3_ = f32[2,16,8,128]{3,2,1,0:T(8,128)S(1)} collective-permute-done((f32[2,16,8,128]{3,2,1,0:T(8,128)S(1)}, f32[2,16,8,128]{3,2,1,0:T(8,128)S(1)}, u32[]{:S(2)}, u32[]{:S(2)}) %collective-permute-start.5) | collective-permute-done | bytes 131104 | tf_op jit(solution)/shard_map/ppermute | solution.py:284
  35.0 0.0 copy-start.5
  35.0 0.0 collective-permute-done.6.refs_4_
  35.0 0.0 copy-start.6
  35.0 6.7 %collective-permute-done.7.refs_5_ = f32[2,16,8,128]{3,2,1,0:T(8,128)S(1)} collective-permute-done((f32[2,16,8,128]{3,2,1,0:T(8,128)S(1)}, f32[2,16,8,128]{3,2,1,0:T(8,128)S(1)}, u32[]{:S(2)}, u32[]{:S(2)}) %collective-permute-start.7) | collective-permute-done | bytes 131104 | tf_op jit(solution)/shard_map/ppermute | solution.py:284
  41.6 0.0 copy-start.7
  41.6 0.0 collective-permute-done.8.refs_6_
  41.7 0.0 copy-start.8
  41.7 0.0 collective-permute-done.9.refs_7_
  41.7 0.0 copy-start.9
  41.7 0.0 copy-done.3
  41.7 0.0 copy-done.4
  41.7 0.0 copy-done.5
  41.7 0.0 copy-done.6
  41.7 0.6 %copy-done.7 = f32[2,16,8,128]{3,2,1,0:T(8,128)} copy-done((f32[2,16,8,128]{3,2,1,0:T(8,128)}, f32[2,16,8,128]{3,2,1,0:T(8,128)S(1)}, u32[]{:S(2)}) %copy-start.7) | copy-done | bytes 131096
  42.3 0.1 copy-done.8
  42.4 0.0 copy-done.9
  42.4 2.1 %sum_time_blocks.1 = f32[16,8,8,128]{3,2,1,0:T(8,128)} custom-call(f32[2,16,8,128]{3,2,1,0:T(8,128)} %get-tuple-element.12.refs_0_, f32[2,16,8,128]{3,2,1,0:T(8,128)} %copy-done.3, f32[2,16,8,128]{3,2,1,0:T(8,128)} %copy-done.4, f32[2,16,8,128]{3,2,1,0:T(8,128)} %copy-done.5, f32[2,16,8,128]{3,2,1,0:T(8,128)} %copy-done.6, f32[2,16,8,128]{3,2,1,0:T(8,128)} %copy-done.7, ...), custom_call_target="tpu_custom_call" | custom-call | tf_op jit(solution)/shard_map/sum_time_blocks/pallas_call | solution.py:245
Async XLA Ops:
  3.7 15.8 %collective-permute-start = (bf16[2,2,8,2048]{3,2,1,0:T(8,128)(2,1)}, bf16[2,2,8,2048]{3,2,1,0:T(8,128)(2,1)S(1)}, u32[]{:S(2)}, u32[]{:S(2)}) collective-permute-start(bf16[2,2,8,2048]{3,2,1,0:T(8,128)(2,1)} %pick_references.1.rest_0_), channel_id=1, source_target_pairs={{0,1},{1,2},{2,3},{3,0},{4,5},{5,6},{6,7},{7,4},{8,9},{9,10},{10,1... | collective-permute-start | bytes 393224 | tf_op jit(solution)/shard_map/ppermute | solution.py:264
  6.8 12.8 %collective-permute-start.1 = (bf16[2,2,8,2048]{3,2,1,0:T(8,128)(2,1)}, bf16[2,2,8,2048]{3,2,1,0:T(8,128)(2,1)S(1)}, u32[]{:S(2)}, u32[]{:S(2)}) collective-permute-start(bf16[2,2,8,2048]{3,2,1,0:T(8,128)(2,1)} %pick_references.1.rest_0_), channel_id=1, source_target_pairs={{0,2},{1,3},{2,0},{3,1},{4,6},{5,7},{6,4},{7,5},{8,10},{9,11},{10,... | collective-permute-start | bytes 393224 | tf_op jit(solution)/shard_map/ppermute | solution.py:264
  9.3 10.2 %collective-permute-start.2 = (bf16[2,2,8,2048]{3,2,1,0:T(8,128)(2,1)}, bf16[2,2,8,2048]{3,2,1,0:T(8,128)(2,1)S(1)}, u32[]{:S(2)}, u32[]{:S(2)}) collective-permute-start(bf16[2,2,8,2048]{3,2,1,0:T(8,128)(2,1)} %pick_references.1.rest_0_), channel_id=1, source_target_pairs={{0,3},{1,0},{2,1},{3,2},{4,7},{5,4},{6,5},{7,6},{8,11},{9,8},{10,9... | collective-permute-start | bytes 393224 | tf_op jit(solution)/shard_map/ppermute | solution.py:264
  10.7 8.9 %copy-start = (bf16[2,2,128,2048]{3,2,1,0:T(8,128)(2,1)S(1)}, bf16[2,2,128,2048]{3,2,1,0:T(8,128)(2,1)}, u32[]{:S(2)}) copy-start(bf16[2,2,128,2048]{3,2,1,0:T(8,128)(2,1)} %volt_ref.3) | copy-start | bytes 6291460
  10.7 8.9 %copy-start.1 = (bf16[2,2,8,2048]{3,2,1,0:T(8,128)(2,1)S(1)}, bf16[2,2,8,2048]{3,2,1,0:T(8,128)(2,1)}, u32[]{:S(2)}) copy-start(bf16[2,2,8,2048]{3,2,1,0:T(8,128)(2,1)} %pick_references.1.rest_0_) | copy-start | bytes 393220
  19.6 1.2 %copy-start.2 = (f32[128,2048]{1,0:T(8,128)S(1)}, f32[128,2048]{1,0:T(8,128)}, u32[]{:S(2)}) copy-start(f32[128,2048]{1,0:T(8,128)} %fit_tables.1.rest_4_) | copy-start | bytes 3145732
  26.6 3.5 %collective-permute-start.3 = (f32[2,16,8,128]{3,2,1,0:T(8,128)S(1)}, f32[2,16,8,128]{3,2,1,0:T(8,128)S(1)}, u32[]{:S(2)}, u32[]{:S(2)}) collective-permute-start(f32[2,16,8,128]{3,2,1,0:T(8,128)S(1)} %get-tuple-element.11), channel_id=1, source_target_pairs={{0,8},{4,12},{8,0},{12,4},{16,24},{20,28},{24,16},{28,20},{1,9},{5... | collective-permute-start | bytes 393224 | tf_op jit(solution)/shard_map/ppermute | solution.py:284
  26.6 6.3 %collective-permute-start.4 = (f32[2,16,8,128]{3,2,1,0:T(8,128)S(1)}, f32[2,16,8,128]{3,2,1,0:T(8,128)S(1)}, u32[]{:S(2)}, u32[]{:S(2)}) collective-permute-start(f32[2,16,8,128]{3,2,1,0:T(8,128)S(1)} %get-tuple-element.10), channel_id=1, source_target_pairs={{0,16},{4,20},{8,24},{12,28},{16,0},{20,4},{24,8},{28,12},{1,17},{... | collective-permute-start | bytes 393224 | tf_op jit(solution)/shard_map/ppermute | solution.py:284
  28.1 6.8 %collective-permute-start.5 = (f32[2,16,8,128]{3,2,1,0:T(8,128)S(1)}, f32[2,16,8,128]{3,2,1,0:T(8,128)S(1)}, u32[]{:S(2)}, u32[]{:S(2)}) collective-permute-start(f32[2,16,8,128]{3,2,1,0:T(8,128)S(1)} %get-tuple-element.9), channel_id=1, source_target_pairs={{0,24},{4,28},{8,16},{12,20},{16,8},{20,12},{24,0},{28,4},{1,25},{... | collective-permute-start | bytes 393224 | tf_op jit(solution)/shard_map/ppermute | solution.py:284
  28.5 6.5 %collective-permute-start.6 = (f32[2,16,8,128]{3,2,1,0:T(8,128)S(1)}, f32[2,16,8,128]{3,2,1,0:T(8,128)S(1)}, u32[]{:S(2)}, u32[]{:S(2)}) collective-permute-start(f32[2,16,8,128]{3,2,1,0:T(8,128)S(1)} %get-tuple-element.8), channel_id=1, source_target_pairs={{0,4},{4,0},{8,12},{12,8},{16,20},{20,16},{24,28},{28,24},{1,5},{5... | collective-permute-start | bytes 393224 | tf_op jit(solution)/shard_map/ppermute | solution.py:284
  30.0 11.6 %collective-permute-start.7 = (f32[2,16,8,128]{3,2,1,0:T(8,128)S(1)}, f32[2,16,8,128]{3,2,1,0:T(8,128)S(1)}, u32[]{:S(2)}, u32[]{:S(2)}) collective-permute-start(f32[2,16,8,128]{3,2,1,0:T(8,128)S(1)} %get-tuple-element.7), channel_id=1, source_target_pairs={{0,12},{4,8},{8,4},{12,0},{16,28},{20,24},{24,20},{28,16},{1,13},{... | collective-permute-start | bytes 393224 | tf_op jit(solution)/shard_map/ppermute | solution.py:284
  30.1 11.5 %copy-start.3 = (f32[2,16,8,128]{3,2,1,0:T(8,128)}, f32[2,16,8,128]{3,2,1,0:T(8,128)S(1)}, u32[]{:S(2)}) copy-start(f32[2,16,8,128]{3,2,1,0:T(8,128)S(1)} %collective-permute-done.3.refs_1_) | copy-start | bytes 393220
  30.1 11.5 %collective-permute-start.8 = (f32[2,16,8,128]{3,2,1,0:T(8,128)S(1)}, f32[2,16,8,128]{3,2,1,0:T(8,128)S(1)}, u32[]{:S(2)}, u32[]{:S(2)}) collective-permute-start(f32[2,16,8,128]{3,2,1,0:T(8,128)S(1)} %get-tuple-element.6), channel_id=1, source_target_pairs={{0,20},{4,16},{8,28},{12,24},{16,4},{20,0},{24,12},{28,8},{1,21},{... | collective-permute-start | bytes 393224 | tf_op jit(solution)/shard_map/ppermute | solution.py:284
  32.9 8.8 %copy-start.4 = (f32[2,16,8,128]{3,2,1,0:T(8,128)}, f32[2,16,8,128]{3,2,1,0:T(8,128)S(1)}, u32[]{:S(2)}) copy-start(f32[2,16,8,128]{3,2,1,0:T(8,128)S(1)} %collective-permute-done.4.refs_2_) | copy-start | bytes 393220
  32.9 8.7 %collective-permute-start.9 = (f32[2,16,8,128]{3,2,1,0:T(8,128)S(1)}, f32[2,16,8,128]{3,2,1,0:T(8,128)S(1)}, u32[]{:S(2)}, u32[]{:S(2)}) collective-permute-start(f32[2,16,8,128]{3,2,1,0:T(8,128)S(1)} %get-tuple-element.5), channel_id=1, source_target_pairs={{0,28},{4,24},{8,20},{12,16},{16,12},{20,8},{24,4},{28,0},{1,29},{... | collective-permute-start | bytes 393224 | tf_op jit(solution)/shard_map/ppermute | solution.py:284
  35.0 6.7 %copy-start.5 = (f32[2,16,8,128]{3,2,1,0:T(8,128)}, f32[2,16,8,128]{3,2,1,0:T(8,128)S(1)}, u32[]{:S(2)}) copy-start(f32[2,16,8,128]{3,2,1,0:T(8,128)S(1)} %collective-permute-done.5.refs_3_) | copy-start | bytes 393220
  35.0 6.7 %copy-start.6 = (f32[2,16,8,128]{3,2,1,0:T(8,128)}, f32[2,16,8,128]{3,2,1,0:T(8,128)S(1)}, u32[]{:S(2)}) copy-start(f32[2,16,8,128]{3,2,1,0:T(8,128)S(1)} %collective-permute-done.6.refs_4_) | copy-start | bytes 393220
  41.6 0.7 %copy-start.7 = (f32[2,16,8,128]{3,2,1,0:T(8,128)}, f32[2,16,8,128]{3,2,1,0:T(8,128)S(1)}, u32[]{:S(2)}) copy-start(f32[2,16,8,128]{3,2,1,0:T(8,128)S(1)} %collective-permute-done.7.refs_5_) | copy-start | bytes 393220
  41.7 0.7 %copy-start.8 = (f32[2,16,8,128]{3,2,1,0:T(8,128)}, f32[2,16,8,128]{3,2,1,0:T(8,128)S(1)}, u32[]{:S(2)}) copy-start(f32[2,16,8,128]{3,2,1,0:T(8,128)S(1)} %collective-permute-done.8.refs_6_) | copy-start | bytes 393220
  41.7 0.7 %copy-start.9 = (f32[2,16,8,128]{3,2,1,0:T(8,128)}, f32[2,16,8,128]{3,2,1,0:T(8,128)S(1)}, u32[]{:S(2)}) copy-start(f32[2,16,8,128]{3,2,1,0:T(8,128)S(1)} %collective-permute-done.9.refs_7_) | copy-start | bytes 393220
where the time goes:
time: 45.1 us; the launch traced here: 44.5 us
  Pallas kernels  19.8 us (44%)
  starting transfers between devices  14.3 us (32%)
  waiting for transfers between devices  7.68 us (17%)
  local copies, waits for them, and re-layouts  2.69 us (6%)
    pallas_call x1, Pallas kernels, tables(): pl.pallas_call(functools.partial(tables_kernel, scale), out_shape=jax.Sha...  8.83 us
    ppermute x7, waiting for transfers between devices, on_device(): block = lax.ppermute(block, ('chan', 'tm'), pairs)  7.67 us
    ppermute x7, starting transfers between devices, on_device(): block = lax.ppermute(block, ('chan', 'tm'), pairs)  7.33 us
    ppermute x3, starting transfers between devices, on_device(): lax.ppermute(picked, 'stat', [(i, (i + shift) % stat_count) for i in rang...  6.96 us
    pallas_call x1, Pallas kernels, correlate(): pl.pallas_call(correlate_kernel, in_specs=[vmem] * (2 + len(ref_parts)),...  5.08 us
    pallas_call x1, Pallas kernels, pick(): pl.pallas_call(pick_kernel, grid=(chans, parts), in_specs=[pl.BlockSpec(m...  3.73 us
    pallas_call x1, Pallas kernels, collect(): pl.pallas_call(collect_kernel, in_specs=[vmem] * len(pieces), out_specs=v...  2.14 us
    unnamed x20, local copies, waits for them, and re-layouts  1.93 us
  transfers between devices with their start and end apart: 10, of which 3 were waited for; matrix products, arithmetic and copies ran while one was open for 0% of the time, Pallas kernels for 20%

commit v1 on v0

--- a/solution.py
+++ b/solution.py
@@ -14,6 +14,8 @@
 CELLS = RASTER * RASTER
 HIGHEST = lax.Precision.HIGHEST
 ROWS = (((1,), (1,)), ((), ()))
+GROUP = 16
+STEP = 512
 
 
 def zernike_rows():
@@ -62,33 +64,38 @@
     return np.concatenate([np.cos(angles), -np.sin(angles)], axis=1).astype(np.float32)
 
 
-def pick_kernel(index_ref, volt_ref, out_ref):
-    stations = volt_ref.shape[2]
+def pick_kernel(index_ref, volt_ref, out_ref, rows_ref):
+    chans, parts, stations, _ = volt_ref.shape
     refs = out_ref.shape[2]
     first = lax.axis_index("stat") * stations
-    row = lax.broadcasted_iota(jnp.int32, (refs, stations), 0)
-    lane = lax.broadcasted_iota(jnp.int32, (refs, stations), 1)
-    wanted = jnp.zeros((refs, stations), jnp.int32)
+    rows_ref[...] = jnp.zeros_like(rows_ref)
     for r in range(refs):
-        wanted = jnp.where(row == r, index_ref[r] - first, wanted)
-    select = jnp.where(lane == wanted, 1.0, 0.0).astype(jnp.bfloat16)
-    out_ref[0, 0] = jnp.dot(
-        select, volt_ref[0, 0], preferred_element_type=jnp.float32
-    ).astype(jnp.bfloat16)
+        local = index_ref[r] - first
+
+        @pl.when(jnp.logical_and(local >= 0, local < stations))
+        def _():
+            begin = pl.multiple_of(local // GROUP * GROUP, GROUP)
+            for c in range(chans):
+                for k in range(parts):
+                    group = volt_ref[c, k, pl.ds(begin, GROUP), :].astype(jnp.float32)
+                    row = lax.broadcasted_iota(jnp.int32, group.shape, 0)
+                    group = jnp.where(row == local - begin, group, 0.0)
+                    rows_ref[c, k, r : r + 1, :] = jnp.sum(group, axis=0, keepdims=True)
+
+    out_ref[...] = rows_ref[...].astype(jnp.bfloat16)
 
 
 def pick(ref_index, voltages):
-    chans, parts, stations, times = voltages.shape
+    chans, parts, _, times = voltages.shape
     refs = ref_index.shape[0]
+    vmem = pl.BlockSpec(memory_space=pltpu.VMEM)
     return pl.pallas_call(
         pick_kernel,
-        grid=(chans, parts),
-        in_specs=[
-            pl.BlockSpec(memory_space=pltpu.SMEM),
-            pl.BlockSpec((1, 1, stations, times), lambda c, k: (c, k, 0, 0)),
-        ],
-        out_specs=pl.BlockSpec((1, 1, refs, times), lambda c, k: (c, k, 0, 0)),
+        in_specs=[pl.BlockSpec(memory_space=pltpu.SMEM), vmem],
+        out_specs=vmem,
         out_shape=jax.ShapeDtypeStruct((chans, parts, refs, times), jnp.bfloat16),
+        scratch_shapes=[pltpu.VMEM((chans, parts, refs, times), jnp.float32)],
+        compiler_params=pltpu.CompilerParams(vmem_limit_bytes=8 * 2**20),
         name="pick_references",
     )(ref_index, voltages)
 
@@ -115,22 +122,18 @@
 
 
 def tables_kernel(scale, weight_ref, zern_ref, dft_ref, pos_ref, out_ref):
-    zern = zern_ref[...]
-    weighted = zern * weight_ref[...]
-    gram = lax.dot_general(weighted, zern, ROWS, precision=HIGHEST, preferred_element_type=jnp.float32)
+    weighted = zern_ref[...] * (weight_ref[...] * scale)
     field = jnp.dot(weighted, dft_ref[...], precision=HIGHEST, preferred_element_type=jnp.float32)
-    fit = jnp.dot(invert(gram), field, precision=HIGHEST, preferred_element_type=jnp.float32) * scale
-    fit = jnp.concatenate([fit[:, :CELLS], fit[:, CELLS:]], axis=0)
-    pieces = split(fit, 3)
+    field = jnp.concatenate([field[:, :CELLS], field[:, CELLS:]], axis=0)
+    pieces = split(field, 3)
     times = pos_ref.shape[1]
-    step = 512
-    cell = lax.broadcasted_iota(jnp.int32, (CELLS, step), 0)
-    for begin in range(0, times, step):
-        onehot = jnp.where(cell == pos_ref[:, begin : begin + step], 1.0, 0.0).astype(jnp.bfloat16)
+    cell = lax.broadcasted_iota(jnp.int32, (CELLS, STEP), 0)
+    for begin in range(0, times, STEP):
+        onehot = jnp.where(cell == pos_ref[:, begin : begin + STEP], 1.0, 0.0).astype(jnp.bfloat16)
         total = jnp.dot(pieces[0], onehot, preferred_element_type=jnp.float32)
         for piece in pieces[1:]:
             total = total + jnp.dot(piece, onehot, preferred_element_type=jnp.float32)
-        out_ref[:, begin : begin + step] = total
+        out_ref[:, begin : begin + STEP] = total
 
 
 def tables(weight, positions, scale):
@@ -138,17 +141,37 @@
     return pl.pallas_call(
         functools.partial(tables_kernel, scale),
         out_shape=jax.ShapeDtypeStruct((2 * ZERN, times), jnp.float32),
-        name="fit_tables",
+        name="projection_per_sample",
+        compiler_params=pltpu.CompilerParams(vmem_limit_bytes=12 * 2**20),
         cost_estimate=pl.CostEstimate(flops=4_000_000_000, bytes_accessed=2_000_000, transcendentals=0),
     )(weight.reshape(1, CELLS), jnp.asarray(zernike_rows()), jnp.asarray(dft_rows()), positions.reshape(1, times))
 
 
-STEP = 512
-
-
-def correlate_kernel(volt_ref, *rest):
-    ref_parts = rest[:-6]
-    table_ref, out_ref, refs_ref, left_a, left_b, total_ref = rest[-6:]
+def inverse_kernel(weight_ref, zern_ref, out_ref):
+    zern = zern_ref[...]
+    gram = lax.dot_general(
+        zern * weight_ref[...], zern, ROWS, precision=HIGHEST, preferred_element_type=jnp.float32
+    )
+    inverse = invert(gram)
+    zeros = jnp.zeros_like(inverse)
+    out_ref[...] = jnp.concatenate(
+        [jnp.concatenate([inverse, zeros], axis=1), jnp.concatenate([zeros, inverse], axis=1)], axis=0
+    )
+
+
+def gram_inverse(weight):
+    return pl.pallas_call(
+        inverse_kernel,
+        out_shape=jax.ShapeDtypeStruct((2 * ZERN, 2 * ZERN), jnp.float32),
+        name="gram_inverse",
+        compiler_params=pltpu.CompilerParams(vmem_limit_bytes=4 * 2**20),
+        cost_estimate=pl.CostEstimate(flops=5_000_000_000, bytes_accessed=200_000, transcendentals=0),
+    )(weight.reshape(1, CELLS), jnp.asarray(zernike_rows()))
+
+
+def correlate_kernel(owners, volt_ref, *rest):
+    table_ref, *out_refs, refs_ref, left_a, left_b, total_ref = rest[-(5 + (len(owners) if owners else 1)) :]
+    ref_parts = rest[: len(rest) - (5 + len(out_refs))]
     chans, parts, stations, times = volt_ref.shape
     refs = refs_ref.shape[2]
     steps = times // STEP
@@ -156,6 +179,16 @@
     for other in ref_parts[1:]:
         picked = picked + other[...]
     refs_ref[...] = picked.astype(jnp.float32)
+    own = stations // len(out_refs)
+    begins = [0]
+    if owners:
+        tm, chan_at, chan_count = lax.axis_index("tm"), lax.axis_index("chan"), lax.axis_size("chan")
+        begins = [
+            pl.multiple_of(
+                (jnp.bitwise_xor(tm, dt) * chan_count + jnp.bitwise_xor(chan_at, dc)) * own, own
+            )
+            for dt, dc in owners
+        ]
 
     def produce(chan, step, left_ref):
         span = pl.ds(step * STEP, STEP)
@@ -176,7 +209,9 @@
 
     def consume(chan, step, left_ref):
         span = pl.ds(step * STEP, STEP)
-        right = volt_ref[chan, :, :, span].reshape(parts * stations, STEP)
+        right = jnp.concatenate(
+            [volt_ref[chan, k, pl.ds(begin, own), span] for k in range(parts) for begin in begins], axis=0
+        )
         right = jnp.concatenate([right, right], axis=1)
         product = lax.dot_general(left_ref[...], right, ROWS, preferred_element_type=jnp.float32)
         if step == 0:
@@ -191,7 +226,8 @@
             real = top[:, :stations] - low[:, stations:]
             imag = top[:, stations:] + low[:, :stations]
             both = jnp.concatenate([real, imag], axis=0).T
-            out_ref[chan, pl.ds(r, stations, stride=refs), :] = both
+            for i, out_ref in enumerate(out_refs):
+                out_ref[chan, pl.ds(r, own, stride=refs), :] = both[i * own : (i + 1) * own]
 
     order = [(chan, step) for chan in range(chans) for step in range(steps)]
     buffers = (left_a, left_b)
@@ -204,51 +240,60 @@
             finish(chan)
 
 
-def correlate(voltages, ref_parts, table):
+def correlate(voltages, ref_parts, table, owners):
     chans, parts, stations, times = voltages.shape
     refs = ref_parts[0].shape[2]
     vmem = pl.BlockSpec(memory_space=pltpu.VMEM)
-    return pl.pallas_call(
-        correlate_kernel,
+    blocks = len(owners) if owners else 1
+    return pl.pallas_call(
+        functools.partial(correlate_kernel, owners),
         in_specs=[vmem] * (2 + len(ref_parts)),
-        out_specs=vmem,
-        out_shape=jax.ShapeDtypeStruct((chans, stations * refs, 2 * ZERN), jnp.float32),
+        out_specs=[vmem] * blocks,
+        out_shape=[jax.ShapeDtypeStruct((chans, stations // blocks * refs, 2 * ZERN), jnp.float32)] * blocks,
         scratch_shapes=[
             pltpu.VMEM((chans, parts, refs, times), jnp.float32),
             pltpu.VMEM((refs * 2 * ZERN, 2 * STEP), jnp.bfloat16),
             pltpu.VMEM((refs * 2 * ZERN, 2 * STEP), jnp.bfloat16),
             pltpu.VMEM((refs * 2 * ZERN, parts * stations), jnp.float32),
         ],
-        compiler_params=pltpu.CompilerParams(vmem_limit_bytes=40 * 2**20),
+        compiler_params=pltpu.CompilerParams(vmem_limit_bytes=24 * 2**20),
         cost_estimate=pl.CostEstimate(flops=8_600_000_000, bytes_accessed=5_000_000, transcendentals=0),
         name="correlate",
     )(voltages, *ref_parts, table)
 
 
 def collect_kernel(*refs):
-    *ins, out_ref = refs
+    *ins, inverse_ref, out_ref = refs
     chan = lax.axis_index("chan")
     chan_count = lax.axis_size("chan")
     tm_count = len(ins) // chan_count
+    chans, stations, rows, terms = ins[0].shape
     for dc in range(chan_count):
         total = ins[dc][...]
         for dt in range(1, tm_count):
             total = total + ins[dt * chan_count + dc][...]
+        solved = jnp.dot(
+            total.reshape(chans * stations * rows, terms),
+            inverse_ref[...],
+            precision=HIGHEST,
+            preferred_element_type=jnp.float32,
+        ).reshape(total.shape)
         source = jnp.bitwise_xor(chan, dc)
-        for c in range(total.shape[0]):
-            out_ref[:, source * total.shape[0] + c] = total[c]
-
-
-def collect(pieces, chan_count):
+        for c in range(chans):
+            out_ref[:, source * chans + c] = solved[c]
+
+
+def collect(pieces, inverse, chan_count):
     chans, stations, refs, terms = pieces[0].shape
     vmem = pl.BlockSpec(memory_space=pltpu.VMEM)
     return pl.pallas_call(
         collect_kernel,
-        in_specs=[vmem] * len(pieces),
+        in_specs=[vmem] * (len(pieces) + 1),
         out_specs=vmem,
         out_shape=jax.ShapeDtypeStruct((stations, chans * chan_count, refs, terms), jnp.float32),
-        name="sum_time_blocks",
-    )(*pieces)
+        compiler_params=pltpu.CompilerParams(vmem_limit_bytes=8 * 2**20),
+        name="sum_and_solve",
+    )(*pieces, inverse)
 
 
 def on_device(voltages, ref_index, positions, aperture_weight):
@@ -265,25 +310,30 @@
         )
     scale = (tm_count * times / CELLS) ** (-0.5)
     table = tables(aperture_weight, positions, scale)
-    sums = correlate(voltages, ref_parts, table)
-    owners = tm_count * chan_count
-    sums = sums.reshape(chans, owners, stations // owners, refs, 2 * ZERN)
-    chan = lax.axis_index("chan")
-    tm = lax.axis_index("tm")
+    inverse = gram_inverse(aperture_weight)
+    owners = [(dt, dc) for dt in range(tm_count) for dc in range(chan_count)]
+    own = stations // len(owners)
+    block = (chans, own, refs, 2 * ZERN)
+    if own % GROUP == 0:
+        sums = [x.reshape(block) for x in correlate(voltages, ref_parts, table, owners)]
+    else:
+        whole = correlate(voltages, ref_parts, table, None)[0].reshape((chans, len(owners)) + block[1:])
+        tm, chan = lax.axis_index("tm"), lax.axis_index("chan")
+        sums = [
+            lax.dynamic_index_in_dim(whole, (tm ^ dt) * chan_count + (chan ^ dc), 1, keepdims=False)
+            for dt, dc in owners
+        ]
     pieces = []
-    for dt in range(tm_count):
-        for dc in range(chan_count):
-            owner = (tm ^ dt) * chan_count + (chan ^ dc)
-            block = lax.dynamic_index_in_dim(sums, owner, 1, keepdims=False)
-            if dt or dc:
-                pairs = [
-                    (c * tm_count + t, (c ^ dc) * tm_count + (t ^ dt))
-                    for c in range(chan_count)
-                    for t in range(tm_count)
-                ]
-                block = lax.ppermute(block, ("chan", "tm"), pairs)
-            pieces.append(block)
-    return collect(pieces, chan_count)
+    for (dt, dc), x in zip(owners, sums):
+        if dt or dc:
+            pairs = [
+                (c * tm_count + t, (c ^ dc) * tm_count + (t ^ dt))
+                for c in range(chan_count)
+                for t in range(tm_count)
+            ]
+            x = lax.ppermute(x, ("chan", "tm"), pairs)
+        pieces.append(x)
+    return collect(pieces, inverse, chan_count)
 
 
 def solution(mesh):

time: 45.1 us -> 40.6 us (0.900)
  the two profiles are of different devices: /device:TPU:0 before, /device:TPU:15 now
where the time goes in v1:
time: 40.6 us; the launch traced here: 40.3 us
  waiting for transfers between devices  14.6 us (36%)
  Pallas kernels  14 us (34%)
  starting transfers between devices  9.36 us (23%)
  local copies, waits for them, and re-layouts  2.27 us (6%)
    ppermute x3, waiting for transfers between devices, on_device(): lax.ppermute(picked, 'stat', [(i, (i + shift) % stat_count) for i in rang...  9.93 us
    pallas_call x1, Pallas kernels, gram_inverse(): pl.pallas_call(inverse_kernel, out_shape=jax.ShapeDtypeStruct((2 * ZERN,...  5.68 us
    ppermute x7, starting transfers between devices, on_device(): x = lax.ppermute(x, ('chan', 'tm'), pairs)  5.54 us
    pallas_call x1, Pallas kernels, correlate(): pl.pallas_call(functools.partial(correlate_kernel, owners), in_specs=[vme...  5.09 us
    ppermute x7, waiting for transfers between devices, on_device(): x = lax.ppermute(x, ('chan', 'tm'), pairs)  4.68 us
    ppermute x3, starting transfers between devices, on_device(): lax.ppermute(picked, 'stat', [(i, (i + shift) % stat_count) for i in rang...  3.83 us
    unnamed x14, local copies, waits for them, and re-layouts  2.27 us
    pallas_call x1, Pallas kernels, collect(): pl.pallas_call(collect_kernel, in_specs=[vmem] * (len(pieces) + 1), out_s...  1.39 us
  transfers between devices with their start and end apart: 10, of which 4 were waited for; matrix products, arithmetic and copies ran while one was open for 0% of the time, Pallas kernels for 17%

profile of v1, /device:TPU:15, one launch (start us, length us, event | category | flops | bytes accessed | tf_op | source)
XLA Modules:
  0.0 40.3 jit_solution(11953588761025178595)
XLA Ops:
  0.0 0.0 copy-start
  0.0 1.6 %copy-done = bf16[2,2,128,2048]{3,2,1,0:T(8,128)(2,1)S(1)} copy-done((bf16[2,2,128,2048]{3,2,1,0:T(8,128)(2,1)S(1)}, bf16[2,2,128,2048]{3,2,1,0:T(8,128)(2,1)}, u32[]{:S(2)}) %copy-start) | copy-done | bytes 2097176
  1.6 0.0 copy-start.2
  1.6 0.7 %copy-done.2 = s32[8]{0:T(128)S(1)} copy-done((s32[8]{0:T(128)S(1)}, s32[8]{0:T(128)}, u32[]{:S(2)}) %copy-start.2) | copy-done | bytes 56
  2.2 0.0 copy-start.3
  2.2 0.0 copy-start.4
  2.3 0.0 copy-start.5
  2.3 0.0 copy-start.6
  2.3 0.9 %pick_references.1.rest_0_ = bf16[2,2,8,2048]{3,2,1,0:T(8,128)(2,1)S(1)} custom-call(s32[8]{0:T(128)S(1)} %copy-done.2, bf16[2,2,128,2048]{3,2,1,0:T(8,128)(2,1)S(1)} %copy-done), custom_call_target="tpu_custom_call" | custom-call | tf_op jit(solution)/shard_map/pick_references/pallas_call | solution.py:92
  3.1 1.2 %collective-permute-start = (bf16[2,2,8,2048]{3,2,1,0:T(8,128)(2,1)S(1)}, bf16[2,2,8,2048]{3,2,1,0:T(8,128)(2,1)S(1)}, u32[]{:S(2)}, u32[]{:S(2)}) collective-permute-start(bf16[2,2,8,2048]{3,2,1,0:T(8,128)(2,1)S(1)} %pick_references.1.rest_0_), channel_id=1, source_target_pairs={{0,1},{1,2},{2,3},{3,0},{4,5},{5,6},{6,7},{7,4},{8,9},{9,10},{10,1... | collective-permute-start | bytes 393224 | tf_op jit(solution)/shard_map/ppermute | solution.py:309
  4.4 1.2 %collective-permute-start.1 = (bf16[2,2,8,2048]{3,2,1,0:T(8,128)(2,1)S(1)}, bf16[2,2,8,2048]{3,2,1,0:T(8,128)(2,1)S(1)}, u32[]{:S(2)}, u32[]{:S(2)}) collective-permute-start(bf16[2,2,8,2048]{3,2,1,0:T(8,128)(2,1)S(1)} %pick_references.1.rest_0_), channel_id=1, source_target_pairs={{0,2},{1,3},{2,0},{3,1},{4,6},{5,7},{6,4},{7,5},{8,10},{9,11},{10,... | collective-permute-start | bytes 393224 | tf_op jit(solution)/shard_map/ppermute | solution.py:309
  5.6 1.4 %collective-permute-start.2 = (bf16[2,2,8,2048]{3,2,1,0:T(8,128)(2,1)S(1)}, bf16[2,2,8,2048]{3,2,1,0:T(8,128)(2,1)S(1)}, u32[]{:S(2)}, u32[]{:S(2)}) collective-permute-start(bf16[2,2,8,2048]{3,2,1,0:T(8,128)(2,1)S(1)} %pick_references.1.rest_0_), channel_id=1, source_target_pairs={{0,3},{1,0},{2,1},{3,2},{4,7},{5,4},{6,5},{7,6},{8,11},{9,8},{10,9... | collective-permute-start | bytes 393224 | tf_op jit(solution)/shard_map/ppermute | solution.py:309
  7.0 0.0 copy-done.3
  7.0 0.0 copy-done.4
  7.0 0.0 copy-done.5
  7.0 0.0 copy-done.6
  7.0 0.0 copy-start.1
  7.0 1.0 %projection_per_sample.1.rest_4_ = f32[128,2048]{1,0:T(8,128)S(1)} custom-call(f32[1,256]{1,0:T(1,128)S(1)} %bitcast.19, f32[64,256]{1,0:T(8,128)S(1)} %copy-done.6, f32[256,512]{1,0:T(8,128)S(1)} %copy-done.5, s32[1,2048]{1,0:T(1,128)S(1)} %bitcast.18), custom_call_target="tpu_custom_call" | custom-call | flops 4000000000 | bytes 2000000 | tf_op jit(solution)/shard_map/projection_per_sample/pallas_call | solution.py:141
  8.0 0.0 collective-permute-done.rest_1_
  8.0 7.0 %collective-permute-done.1.rest_2_ = bf16[2,2,8,2048]{3,2,1,0:T(8,128)(2,1)S(1)} collective-permute-done((bf16[2,2,8,2048]{3,2,1,0:T(8,128)(2,1)S(1)}, bf16[2,2,8,2048]{3,2,1,0:T(8,128)(2,1)S(1)}, u32[]{:S(2)}, u32[]{:S(2)}) %collective-permute-start.1) | collective-permute-done | bytes 131104 | tf_op jit(solution)/shard_map/ppermute | solution.py:309
  15.0 3.0 %collective-permute-done.2.rest_3_ = bf16[2,2,8,2048]{3,2,1,0:T(8,128)(2,1)S(1)} collective-permute-done((bf16[2,2,8,2048]{3,2,1,0:T(8,128)(2,1)S(1)}, bf16[2,2,8,2048]{3,2,1,0:T(8,128)(2,1)S(1)}, u32[]{:S(2)}, u32[]{:S(2)}) %collective-permute-start.2) | collective-permute-done | bytes 131104 | tf_op jit(solution)/shard_map/ppermute | solution.py:309
  17.9 0.0 copy-done.1
  17.9 5.1 %correlate.1 = (f32[2,128,128]{2,1,0:T(8,128)S(1)}, f32[2,128,128]{2,1,0:T(8,128)S(1)}, f32[2,128,128]{2,1,0:T(8,128)S(1)}, f32[2,128,128]{2,1,0:T(8,128)S(1)}, ...) custom-call(bf16[2,2,128,2048]{3,2,1,0:T(8,128)(2,1)S(1)} %copy-done, ...), custom_call_target="tpu_custom_call" | custom-call | flops 8600000512 | bytes 5000000 | tf_op jit(solution)/shard_map/correlate/pallas_call | solution.py:248
  23.0 0.6 %collective-permute-start.3 = (f32[2,16,8,128]{3,2,1,0:T(8,128)S(1)}, f32[2,16,8,128]{3,2,1,0:T(8,128)S(1)}, u32[]{:S(2)}, u32[]{:S(2)}) collective-permute-start(f32[2,16,8,128]{3,2,1,0:T(8,128)S(1)} %bitcast.17), channel_id=1, source_target_pairs={{0,8},{4,12},{8,0},{12,4},{16,24},{20,28},{24,16},{28,20},{1,9},{5... | collective-permute-start | bytes 393224 | tf_op jit(solution)/shard_map/ppermute | solution.py:334
  23.6 0.3 collective-permute-start.4
  23.9 1.4 %collective-permute-start.5 = (f32[2,16,8,128]{3,2,1,0:T(8,128)S(1)}, f32[2,16,8,128]{3,2,1,0:T(8,128)S(1)}, u32[]{:S(2)}, u32[]{:S(2)}) collective-permute-start(f32[2,16,8,128]{3,2,1,0:T(8,128)S(1)} %bitcast.15), channel_id=1, source_target_pairs={{0,24},{4,28},{8,16},{12,20},{16,8},{20,12},{24,0},{28,4},{1,25},{... | collective-permute-start | bytes 393224 | tf_op jit(solution)/shard_map/ppermute | solution.py:334
  25.3 0.2 collective-permute-start.6
  25.5 1.6 %collective-permute-start.7 = (f32[2,16,8,128]{3,2,1,0:T(8,128)S(1)}, f32[2,16,8,128]{3,2,1,0:T(8,128)S(1)}, u32[]{:S(2)}, u32[]{:S(2)}) collective-permute-start(f32[2,16,8,128]{3,2,1,0:T(8,128)S(1)} %bitcast.13), channel_id=1, source_target_pairs={{0,12},{4,8},{8,4},{12,0},{16,28},{20,24},{24,20},{28,16},{1,13},{... | collective-permute-start | bytes 393224 | tf_op jit(solution)/shard_map/ppermute | solution.py:334
  27.1 0.0 collective-permute-done.3.refs_1_
  27.1 0.1 collective-permute-start.8
  27.2 1.4 %collective-permute-done.4.refs_2_ = f32[2,16,8,128]{3,2,1,0:T(8,128)S(1)} collective-permute-done((f32[2,16,8,128]{3,2,1,0:T(8,128)S(1)}, f32[2,16,8,128]{3,2,1,0:T(8,128)S(1)}, u32[]{:S(2)}, u32[]{:S(2)}) %collective-permute-start.4) | collective-permute-done | bytes 131104 | tf_op jit(solution)/shard_map/ppermute | solution.py:334
  28.7 1.3 %collective-permute-start.9 = (f32[2,16,8,128]{3,2,1,0:T(8,128)S(1)}, f32[2,16,8,128]{3,2,1,0:T(8,128)S(1)}, u32[]{:S(2)}, u32[]{:S(2)}) collective-permute-start(f32[2,16,8,128]{3,2,1,0:T(8,128)S(1)} %bitcast.11), channel_id=1, source_target_pairs={{0,28},{4,24},{8,20},{12,16},{16,12},{20,8},{24,4},{28,0},{1,29},{... | collective-permute-start | bytes 393224 | tf_op jit(solution)/shard_map/ppermute | solution.py:334
  30.0 5.7 %gram_inverse.1.refs_8_ = f32[128,128]{1,0:T(8,128)S(1)} custom-call(f32[1,256]{1,0:T(1,128)S(1)} %bitcast.20, f32[64,256]{1,0:T(8,128)S(1)} %copy-done.6), custom_call_target="tpu_custom_call" | custom-call | flops 5000000000 | bytes 200000 | tf_op jit(solution)/shard_map/gram_inverse/pallas_call | solution.py:163
  35.7 0.0 collective-permute-done.5.refs_3_
  35.7 0.0 collective-permute-done.6.refs_4_
  35.7 3.2 %collective-permute-done.7.refs_5_ = f32[2,16,8,128]{3,2,1,0:T(8,128)S(1)} collective-permute-done((f32[2,16,8,128]{3,2,1,0:T(8,128)S(1)}, f32[2,16,8,128]{3,2,1,0:T(8,128)S(1)}, u32[]{:S(2)}, u32[]{:S(2)}) %collective-permute-start.7) | collective-permute-done | bytes 131104 | tf_op jit(solution)/shard_map/ppermute | solution.py:334
  38.9 0.0 collective-permute-done.8.refs_6_
  39.0 0.0 collective-permute-done.9.refs_7_
  39.0 1.4 %sum_and_solve.1 = f32[16,8,8,128]{3,2,1,0:T(8,128)} custom-call(f32[2,16,8,128]{3,2,1,0:T(8,128)S(1)} %bitcast.10, f32[2,16,8,128]{3,2,1,0:T(8,128)S(1)} %collective-permute-done.3.refs_1_, f32[2,16,8,128]{3,2,1,0:T(8,128)S(1)} %collective-permute-done.4.refs_2_, f32[2,16,8,128]{3,2,1,0:T(8,128)S(1)} %collective-permute-done.5.refs_3_, ...), custom_call_target="tpu_custom_call" | custom-call | tf_op jit(solution)/shard_map/sum_and_solve/pallas_call | solution.py:289
Async XLA Ops:
  0.0 1.6 %copy-start = (bf16[2,2,128,2048]{3,2,1,0:T(8,128)(2,1)S(1)}, bf16[2,2,128,2048]{3,2,1,0:T(8,128)(2,1)}, u32[]{:S(2)}) copy-start(bf16[2,2,128,2048]{3,2,1,0:T(8,128)(2,1)} %volt_ref.3) | copy-start | bytes 6291460
  1.6 0.7 %copy-start.2 = (s32[8]{0:T(128)S(1)}, s32[8]{0:T(128)}, u32[]{:S(2)}) copy-start(s32[8]{0:T(128)} %index_ref.1) | copy-start | bytes 100
  2.2 4.7 %copy-start.3 = (s32[2048]{0:T(1024)S(1)}, s32[2048]{0:T(1024)}, u32[]{:S(2)}) copy-start(s32[2048]{0:T(1024)} %param.9) | copy-start | bytes 24580
  2.2 4.7 %copy-start.4 = (f32[256]{0:T(256)S(1)}, f32[256]{0:T(256)}, u32[]{:S(2)}) copy-start(f32[256]{0:T(256)} %param.10) | copy-start | bytes 3076
  2.3 4.7 %copy-start.5 = (f32[256,512]{1,0:T(8,128)S(1)}, f32[256,512]{1,0:T(8,128)}, u32[]{:S(2)}) copy-start(f32[256,512]{1,0:T(8,128)} %constant.5.clone.dft_ref) | copy-start | bytes 1572868
  2.3 4.7 %copy-start.6 = (f32[64,256]{1,0:T(8,128)S(1)}, f32[64,256]{1,0:T(8,128)}, u32[]{:S(2)}) copy-start(f32[64,256]{1,0:T(8,128)} %constant.4.clone.zern_ref) | copy-start | bytes 196612
  3.1 4.9 %collective-permute-start = (bf16[2,2,8,2048]{3,2,1,0:T(8,128)(2,1)S(1)}, bf16[2,2,8,2048]{3,2,1,0:T(8,128)(2,1)S(1)}, u32[]{:S(2)}, u32[]{:S(2)}) collective-permute-start(bf16[2,2,8,2048]{3,2,1,0:T(8,128)(2,1)S(1)} %pick_references.1.rest_0_), channel_id=1, source_target_pairs={{0,1},{1,2},{2,3},{3,0},{4,5},{5,6},{6,7},{7,4},{8,9},{9,10},{10,1... | collective-permute-start | bytes 393224 | tf_op jit(solution)/shard_map/ppermute | solution.py:309
  4.4 10.6 %collective-permute-start.1 = (bf16[2,2,8,2048]{3,2,1,0:T(8,128)(2,1)S(1)}, bf16[2,2,8,2048]{3,2,1,0:T(8,128)(2,1)S(1)}, u32[]{:S(2)}, u32[]{:S(2)}) collective-permute-start(bf16[2,2,8,2048]{3,2,1,0:T(8,128)(2,1)S(1)} %pick_references.1.rest_0_), channel_id=1, source_target_pairs={{0,2},{1,3},{2,0},{3,1},{4,6},{5,7},{6,4},{7,5},{8,10},{9,11},{10,... | collective-permute-start | bytes 393224 | tf_op jit(solution)/shard_map/ppermute | solution.py:309
  5.6 12.4 %collective-permute-start.2 = (bf16[2,2,8,2048]{3,2,1,0:T(8,128)(2,1)S(1)}, bf16[2,2,8,2048]{3,2,1,0:T(8,128)(2,1)S(1)}, u32[]{:S(2)}, u32[]{:S(2)}) collective-permute-start(bf16[2,2,8,2048]{3,2,1,0:T(8,128)(2,1)S(1)} %pick_references.1.rest_0_), channel_id=1, source_target_pairs={{0,3},{1,0},{2,1},{3,2},{4,7},{5,4},{6,5},{7,6},{8,11},{9,8},{10,9... | collective-permute-start | bytes 393224 | tf_op jit(solution)/shard_map/ppermute | solution.py:309
  7.0 11.0 %copy-start.1 = (bf16[2,2,128,2048]{3,2,1,0:T(8,128)(2,1)S(1)}, bf16[2,2,128,2048]{3,2,1,0:T(8,128)(2,1)}, u32[]{:S(2)}) copy-start(bf16[2,2,128,2048]{3,2,1,0:T(8,128)(2,1)} %volt_ref.3) | copy-start | bytes 6291460
  23.0 4.1 %collective-permute-start.3 = (f32[2,16,8,128]{3,2,1,0:T(8,128)S(1)}, f32[2,16,8,128]{3,2,1,0:T(8,128)S(1)}, u32[]{:S(2)}, u32[]{:S(2)}) collective-permute-start(f32[2,16,8,128]{3,2,1,0:T(8,128)S(1)} %bitcast.17), channel_id=1, source_target_pairs={{0,8},{4,12},{8,0},{12,4},{16,24},{20,28},{24,16},{28,20},{1,9},{5... | collective-permute-start | bytes 393224 | tf_op jit(solution)/shard_map/ppermute | solution.py:334
  23.6 5.1 %collective-permute-start.4 = (f32[2,16,8,128]{3,2,1,0:T(8,128)S(1)}, f32[2,16,8,128]{3,2,1,0:T(8,128)S(1)}, u32[]{:S(2)}, u32[]{:S(2)}) collective-permute-start(f32[2,16,8,128]{3,2,1,0:T(8,128)S(1)} %bitcast.16), channel_id=1, source_target_pairs={{0,16},{4,20},{8,24},{12,28},{16,0},{20,4},{24,8},{28,12},{1,17},{... | collective-permute-start | bytes 393224 | tf_op jit(solution)/shard_map/ppermute | solution.py:334
  23.9 11.8 %collective-permute-start.5 = (f32[2,16,8,128]{3,2,1,0:T(8,128)S(1)}, f32[2,16,8,128]{3,2,1,0:T(8,128)S(1)}, u32[]{:S(2)}, u32[]{:S(2)}) collective-permute-start(f32[2,16,8,128]{3,2,1,0:T(8,128)S(1)} %bitcast.15), channel_id=1, source_target_pairs={{0,24},{4,28},{8,16},{12,20},{16,8},{20,12},{24,0},{28,4},{1,25},{... | collective-permute-start | bytes 393224 | tf_op jit(solution)/shard_map/ppermute | solution.py:334
  25.3 10.4 %collective-permute-start.6 = (f32[2,16,8,128]{3,2,1,0:T(8,128)S(1)}, f32[2,16,8,128]{3,2,1,0:T(8,128)S(1)}, u32[]{:S(2)}, u32[]{:S(2)}) collective-permute-start(f32[2,16,8,128]{3,2,1,0:T(8,128)S(1)} %bitcast.14), channel_id=1, source_target_pairs={{0,4},{4,0},{8,12},{12,8},{16,20},{20,16},{24,28},{28,24},{1,5},{5... | collective-permute-start | bytes 393224 | tf_op jit(solution)/shard_map/ppermute | solution.py:334
  25.5 13.4 %collective-permute-start.7 = (f32[2,16,8,128]{3,2,1,0:T(8,128)S(1)}, f32[2,16,8,128]{3,2,1,0:T(8,128)S(1)}, u32[]{:S(2)}, u32[]{:S(2)}) collective-permute-start(f32[2,16,8,128]{3,2,1,0:T(8,128)S(1)} %bitcast.13), channel_id=1, source_target_pairs={{0,12},{4,8},{8,4},{12,0},{16,28},{20,24},{24,20},{28,16},{1,13},{... | collective-permute-start | bytes 393224 | tf_op jit(solution)/shard_map/ppermute | solution.py:334
  27.1 11.9 %collective-permute-start.8 = (f32[2,16,8,128]{3,2,1,0:T(8,128)S(1)}, f32[2,16,8,128]{3,2,1,0:T(8,128)S(1)}, u32[]{:S(2)}, u32[]{:S(2)}) collective-permute-start(f32[2,16,8,128]{3,2,1,0:T(8,128)S(1)} %bitcast.12), channel_id=1, source_target_pairs={{0,20},{4,16},{8,28},{12,24},{16,4},{20,0},{24,12},{28,8},{1,21},{... | collective-permute-start | bytes 393224 | tf_op jit(solution)/shard_map/ppermute | solution.py:334
  28.7 10.3 %collective-permute-start.9 = (f32[2,16,8,128]{3,2,1,0:T(8,128)S(1)}, f32[2,16,8,128]{3,2,1,0:T(8,128)S(1)}, u32[]{:S(2)}, u32[]{:S(2)}) collective-permute-start(f32[2,16,8,128]{3,2,1,0:T(8,128)S(1)} %bitcast.11), channel_id=1, source_target_pairs={{0,28},{4,24},{8,20},{12,16},{16,12},{20,8},{24,4},{28,0},{1,29},{... | collective-permute-start | bytes 393224 | tf_op jit(solution)/shard_map/ppermute | solution.py:334

commit v2 on v1

--- a/solution.py
+++ b/solution.py
@@ -16,6 +16,8 @@
 ROWS = (((1,), (1,)), ((), ()))
 GROUP = 16
 STEP = 512
+LEVELS = 64.0
+MOST = 32500.0
 
 
 def zernike_rows():
@@ -64,25 +66,35 @@
     return np.concatenate([np.cos(angles), -np.sin(angles)], axis=1).astype(np.float32)
 
 
-def pick_kernel(index_ref, volt_ref, out_ref, rows_ref):
+def pick_kernel(index_ref, volt_ref, *rest):
+    *out_refs, group_ref, rows_ref, sems = rest
     chans, parts, stations, _ = volt_ref.shape
-    refs = out_ref.shape[2]
+    refs = rows_ref.shape[2]
     first = lax.axis_index("stat") * stations
+
+    def each_owned(work):
+        for r in range(refs):
+            local = index_ref[r] - first
+            pl.when(jnp.logical_and(local >= 0, local < stations))(functools.partial(work, r, local))
+
+    def copy(r, local):
+        begin = pl.multiple_of(local // GROUP * GROUP, GROUP)
+        return pltpu.make_async_copy(volt_ref.at[:, :, pl.ds(begin, GROUP), :], group_ref.at[r], sems.at[r])
+
+    def fill(r, local):
+        copy(r, local).wait()
+        for c in range(chans):
+            for k in range(parts):
+                group = group_ref[r, c, k].astype(jnp.float32)
+                row = lax.broadcasted_iota(jnp.int32, group.shape, 0)
+                group = jnp.where(row == lax.rem(local, GROUP), group, 0.0)
+                rows_ref[c, k, r : r + 1, :] = jnp.sum(group, axis=0, keepdims=True)
+
+    each_owned(lambda r, local: copy(r, local).start())
     rows_ref[...] = jnp.zeros_like(rows_ref)
-    for r in range(refs):
-        local = index_ref[r] - first
-
-        @pl.when(jnp.logical_and(local >= 0, local < stations))
-        def _():
-            begin = pl.multiple_of(local // GROUP * GROUP, GROUP)
-            for c in range(chans):
-                for k in range(parts):
-                    group = volt_ref[c, k, pl.ds(begin, GROUP), :].astype(jnp.float32)
-                    row = lax.broadcasted_iota(jnp.int32, group.shape, 0)
-                    group = jnp.where(row == local - begin, group, 0.0)
-                    rows_ref[c, k, r : r + 1, :] = jnp.sum(group, axis=0, keepdims=True)
-
-    out_ref[...] = rows_ref[...].astype(jnp.bfloat16)
+    each_owned(fill)
+    for c, out_ref in enumerate(out_refs):
+        out_ref[...] = rows_ref[c].astype(jnp.bfloat16)
 
 
 def pick(ref_index, voltages):
@@ -91,10 +103,14 @@
     vmem = pl.BlockSpec(memory_space=pltpu.VMEM)
     return pl.pallas_call(
         pick_kernel,
-        in_specs=[pl.BlockSpec(memory_space=pltpu.SMEM), vmem],
-        out_specs=vmem,
-        out_shape=jax.ShapeDtypeStruct((chans, parts, refs, times), jnp.bfloat16),
-        scratch_shapes=[pltpu.VMEM((chans, parts, refs, times), jnp.float32)],
+        in_specs=[pl.BlockSpec(memory_space=pltpu.SMEM), pl.BlockSpec(memory_space=pl.ANY)],
+        out_specs=[vmem] * chans,
+        out_shape=[jax.ShapeDtypeStruct((parts, refs, times), jnp.bfloat16)] * chans,
+        scratch_shapes=[
+            pltpu.VMEM((refs, chans, parts, GROUP, times), jnp.bfloat16),
+            pltpu.VMEM((chans, parts, refs, times), jnp.float32),
+            pltpu.SemaphoreType.DMA((refs,)),
+        ],
         compiler_params=pltpu.CompilerParams(vmem_limit_bytes=8 * 2**20),
         name="pick_references",
     )(ref_index, voltages)
@@ -169,17 +185,15 @@
     )(weight.reshape(1, CELLS), jnp.asarray(zernike_rows()))
 
 
-def correlate_kernel(owners, volt_ref, *rest):
-    table_ref, *out_refs, refs_ref, left_a, left_b, total_ref = rest[-(5 + (len(owners) if owners else 1)) :]
-    ref_parts = rest[: len(rest) - (5 + len(out_refs))]
-    chans, parts, stations, times = volt_ref.shape
-    refs = refs_ref.shape[2]
+def correlate_kernel(chan, owners, last, *args):
+    (volt_ref, first_ref, second_ref, table_ref), args = args[:4], args[4:]
+    before_refs, args = args[: 3 * last], args[3 * last :]
+    out_refs, (refs_ref, left_a, left_b, total_ref, stage_ref) = args[:-5], args[-5:]
+    _, parts, stations, times = volt_ref.shape
+    refs = refs_ref.shape[1]
     steps = times // STEP
-    picked = ref_parts[0][...]
-    for other in ref_parts[1:]:
-        picked = picked + other[...]
-    refs_ref[...] = picked.astype(jnp.float32)
-    own = stations // len(out_refs)
+    refs_ref[...] = (first_ref[...] + second_ref[...]).astype(jnp.float32)
+    own = stations // (len(owners) if owners else 1)
     begins = [0]
     if owners:
         tm, chan_at, chan_count = lax.axis_index("tm"), lax.axis_index("chan"), lax.axis_size("chan")
@@ -190,11 +204,11 @@
             for dt, dc in owners
         ]
 
-    def produce(chan, step, left_ref):
+    def produce(step, left_ref):
         span = pl.ds(step * STEP, STEP)
         for r in range(refs):
-            real = refs_ref[chan, 0, r : r + 1, span]
-            imag = refs_ref[chan, 1, r : r + 1, span]
+            real = refs_ref[0, r : r + 1, span]
+            imag = refs_ref[1, r : r + 1, span]
             for half in range(0, ZERN, 16):
                 table_r = table_ref[half : half + 16, span]
                 table_i = table_ref[ZERN + half : ZERN + half + 16, span]
@@ -207,7 +221,7 @@
                     left_ref[rows, 0:STEP] = high
                     left_ref[rows, STEP : 2 * STEP] = low
 
-    def consume(chan, step, left_ref):
+    def consume(step, left_ref):
         span = pl.ds(step * STEP, STEP)
         right = jnp.concatenate(
             [volt_ref[chan, k, pl.ds(begin, own), span] for k in range(parts) for begin in begins], axis=0
@@ -219,75 +233,120 @@
         else:
             total_ref[...] += product
 
-    def finish(chan):
-        for r in range(refs):
-            top = total_ref[r * 2 * ZERN : r * 2 * ZERN + ZERN, :]
-            low = total_ref[r * 2 * ZERN + ZERN : (r + 1) * 2 * ZERN, :]
-            real = top[:, :stations] - low[:, stations:]
-            imag = top[:, stations:] + low[:, :stations]
-            both = jnp.concatenate([real, imag], axis=0).T
-            for i, out_ref in enumerate(out_refs):
-                out_ref[chan, pl.ds(r, own, stride=refs), :] = both[i * own : (i + 1) * own]
-
-    order = [(chan, step) for chan in range(chans) for step in range(steps)]
     buffers = (left_a, left_b)
-    produce(*order[0], buffers[0])
-    for i, (chan, step) in enumerate(order):
-        if i + 1 < len(order):
-            produce(*order[i + 1], buffers[(i + 1) % 2])
-        consume(chan, step, buffers[i % 2])
-        if step == steps - 1:
-            finish(chan)
+    produce(0, buffers[0])
+    for step in range(steps):
+        if step + 1 < steps:
+            produce(step + 1, buffers[(step + 1) % 2])
+        consume(step, buffers[step % 2])
+    kept = lax.broadcasted_iota(jnp.int32, (1, stations), 1) < own
+    levels = []
+    for r in range(refs):
+        top = total_ref[r * 2 * ZERN : r * 2 * ZERN + ZERN, :]
+        low = total_ref[r * 2 * ZERN + ZERN : (r + 1) * 2 * ZERN, :]
+        real = top[:, :stations] - low[:, stations:]
+        imag = top[:, stations:] + low[:, :stations]
+        both = jnp.concatenate([real, imag], axis=0)
+        if owners:
+            most = jnp.maximum(jnp.max(jnp.abs(both), axis=0, keepdims=True), 1e-30)
+            level = jnp.floor(jnp.log2(most) * LEVELS) + 1.0
+            levels.append(level)
+            rounded = jnp.floor(both * (jnp.exp2(level * (-1.0 / LEVELS)) * MOST) + 0.5)
+            both = jnp.where(kept, both, rounded)
+        stage_ref[pl.ds(r, stations, stride=refs), :] = both.T
+    if not owners:
+        out_refs[0][...] = stage_ref[...]
+        return
+    rows = own * refs
+    level = jnp.concatenate(levels, axis=0)
+    sent = stage_ref[rows:, :].astype(jnp.int32).astype(jnp.int16)
+    if not last:
+        out_refs[0][...] = stage_ref[:rows, :]
+        out_refs[1][...] = sent
+        out_refs[2][...] = level
+        return
+    out_refs[0][0] = before_refs[0][...]
+    out_refs[0][1] = stage_ref[:rows, :]
+    levels = jnp.concatenate([before_refs[2][...], level], axis=0).astype(jnp.int32).astype(jnp.int16)
+    for i, out_ref in enumerate(out_refs[1:]):
+        out_ref[:rows, :] = before_refs[1][i * rows : (i + 1) * rows, :]
+        out_ref[rows : 2 * rows, :] = sent[i * rows : (i + 1) * rows]
+        out_ref[2 * rows :, :] = levels
 
 
 def correlate(voltages, ref_parts, table, owners):
     chans, parts, stations, times = voltages.shape
-    refs = ref_parts[0].shape[2]
+    refs = ref_parts[0][0].shape[1]
     vmem = pl.BlockSpec(memory_space=pltpu.VMEM)
-    blocks = len(owners) if owners else 1
-    return pl.pallas_call(
-        functools.partial(correlate_kernel, owners),
-        in_specs=[vmem] * (2 + len(ref_parts)),
-        out_specs=[vmem] * blocks,
-        out_shape=[jax.ShapeDtypeStruct((chans, stations // blocks * refs, 2 * ZERN), jnp.float32)] * blocks,
-        scratch_shapes=[
-            pltpu.VMEM((chans, parts, refs, times), jnp.float32),
-            pltpu.VMEM((refs * 2 * ZERN, 2 * STEP), jnp.bfloat16),
-            pltpu.VMEM((refs * 2 * ZERN, 2 * STEP), jnp.bfloat16),
-            pltpu.VMEM((refs * 2 * ZERN, parts * stations), jnp.float32),
-        ],
-        compiler_params=pltpu.CompilerParams(vmem_limit_bytes=24 * 2**20),
-        cost_estimate=pl.CostEstimate(flops=8_600_000_000, bytes_accessed=5_000_000, transcendentals=0),
-        name="correlate",
-    )(voltages, *ref_parts, table)
-
-
-def collect_kernel(*refs):
+    rows = stations // (len(owners) if owners else 1) * refs
+    plain = jax.ShapeDtypeStruct((stations * refs, 2 * ZERN), jnp.float32)
+    sums = []
+    for chan in range(chans):
+        last = owners is not None and chan == chans - 1
+        if last:
+            shapes = [jax.ShapeDtypeStruct((chans, rows, 2 * ZERN), jnp.float32)]
+            shapes += [jax.ShapeDtypeStruct((chans * rows + chans * refs, 2 * ZERN), jnp.int16)] * (len(owners) - 1)
+        elif owners:
+            shapes = [
+                jax.ShapeDtypeStruct((rows, 2 * ZERN), jnp.float32),
+                jax.ShapeDtypeStruct((stations * refs - rows, 2 * ZERN), jnp.int16),
+                jax.ShapeDtypeStruct((refs, stations), jnp.float32),
+            ]
+        else:
+            shapes = [plain]
+        before = sums if last else []
+        call = pl.pallas_call(
+            functools.partial(correlate_kernel, chan, owners, last),
+            in_specs=[vmem] * (4 + len(before)),
+            out_specs=[vmem] * len(shapes),
+            out_shape=shapes,
+            scratch_shapes=[
+                pltpu.VMEM((parts, refs, times), jnp.float32),
+                pltpu.VMEM((refs * 2 * ZERN, 2 * STEP), jnp.bfloat16),
+                pltpu.VMEM((refs * 2 * ZERN, 2 * STEP), jnp.bfloat16),
+                pltpu.VMEM((refs * 2 * ZERN, parts * stations), jnp.float32),
+                pltpu.VMEM(plain.shape, jnp.float32),
+            ],
+            compiler_params=pltpu.CompilerParams(vmem_limit_bytes=24 * 2**20),
+            cost_estimate=pl.CostEstimate(flops=4_300_000_000, bytes_accessed=3_000_000, transcendentals=0),
+            name="correlate",
+        )
+        out = list(call(voltages, *ref_parts[chan], table, *before))
+        sums = out if owners else sums + out
+    return sums
+
+
+def collect_kernel(shape, *refs):
     *ins, inverse_ref, out_ref = refs
     chan = lax.axis_index("chan")
     chan_count = lax.axis_size("chan")
     tm_count = len(ins) // chan_count
-    chans, stations, rows, terms = ins[0].shape
+    chans, own, rows, terms = shape
     for dc in range(chan_count):
-        total = ins[dc][...]
-        for dt in range(1, tm_count):
-            total = total + ins[dt * chan_count + dc][...]
-        solved = jnp.dot(
-            total.reshape(chans * stations * rows, terms),
-            inverse_ref[...],
-            precision=HIGHEST,
-            preferred_element_type=jnp.float32,
-        ).reshape(total.shape)
         source = jnp.bitwise_xor(chan, dc)
         for c in range(chans):
-            out_ref[:, source * chans + c] = solved[c]
-
-
-def collect(pieces, inverse, chan_count):
-    chans, stations, refs, terms = pieces[0].shape
+            total = None
+            for at in range(dc, len(ins), chan_count):
+                if ins[at].dtype == jnp.int16:
+                    begin = c * own * rows
+                    level = ins[at][chans * own * rows :, :].astype(jnp.int32).astype(jnp.float32)
+                    step = jnp.exp2(level[c * rows : (c + 1) * rows] * (1.0 / LEVELS)) * (1.0 / MOST)
+                    part = ins[at][begin : begin + own * rows, :].astype(jnp.int32).astype(jnp.float32)
+                    steps = [step[:, at * own + s : at * own + s + 1] for s in range(own)]
+                    steps = [jnp.broadcast_to(x, (rows, terms)) for x in steps]
+                    part = part * jnp.concatenate(steps, axis=0)
+                else:
+                    part = ins[at][c].reshape(own * rows, terms)
+                total = part if total is None else total + part
+            solved = jnp.dot(total, inverse_ref[...], precision=HIGHEST, preferred_element_type=jnp.float32)
+            out_ref[:, source * chans + c] = solved.reshape(own, rows, terms)
+
+
+def collect(pieces, inverse, chan_count, shape):
+    chans, stations, refs, terms = shape
     vmem = pl.BlockSpec(memory_space=pltpu.VMEM)
     return pl.pallas_call(
-        collect_kernel,
+        functools.partial(collect_kernel, shape),
         in_specs=[vmem] * (len(pieces) + 1),
         out_specs=vmem,
         out_shape=jax.ShapeDtypeStruct((stations, chans * chan_count, refs, terms), jnp.float32),
@@ -302,22 +361,25 @@
     stat_count = lax.axis_size("stat")
     tm_count = lax.axis_size("tm")
     chan_count = lax.axis_size("chan")
-    picked = pick(ref_index, voltages)
-    ref_parts = [picked]
-    for shift in range(1, stat_count):
-        ref_parts.append(
-            lax.ppermute(picked, "stat", [(i, (i + shift) % stat_count) for i in range(stat_count)])
-        )
+    ref_parts = []
+    for picked in pick(ref_index, voltages):
+        step = 1
+        other = jnp.zeros_like(picked)
+        while step < stat_count:
+            picked = picked + other if step > 1 else picked
+            other = lax.ppermute(picked, "stat", [(i, i ^ step) for i in range(stat_count)])
+            step *= 2
+        ref_parts.append((picked, other))
     scale = (tm_count * times / CELLS) ** (-0.5)
     table = tables(aperture_weight, positions, scale)
     inverse = gram_inverse(aperture_weight)
     owners = [(dt, dc) for dt in range(tm_count) for dc in range(chan_count)]
     own = stations // len(owners)
     block = (chans, own, refs, 2 * ZERN)
-    if own % GROUP == 0:
-        sums = [x.reshape(block) for x in correlate(voltages, ref_parts, table, owners)]
+    if own % GROUP == 0 and chans == 2:
+        sums = correlate(voltages, ref_parts, table, owners)
     else:
-        whole = correlate(voltages, ref_parts, table, None)[0].reshape((chans, len(owners)) + block[1:])
+        whole = jnp.stack(correlate(voltages, ref_parts, table, None)).reshape((chans, len(owners)) + block[1:])
         tm, chan = lax.axis_index("tm"), lax.axis_index("chan")
         sums = [
             lax.dynamic_index_in_dim(whole, (tm ^ dt) * chan_count + (chan ^ dc), 1, keepdims=False)
@@ -333,7 +395,7 @@
             ]
             x = lax.ppermute(x, ("chan", "tm"), pairs)
         pieces.append(x)
-    return collect(pieces, inverse, chan_count)
+    return collect(pieces, inverse, chan_count, block)
 
 
 def solution(mesh):

time: 40.6 us -> 36.1 us (0.89)
  the two profiles are of different devices: /device:TPU:15 before, /device:TPU:0 now
where the time goes in v2:
time: 36.1 us; the launch traced here: 35.8 us
  Pallas kernels  15.2 us (42%)
  starting transfers between devices  13.6 us (38%)
  waiting for transfers between devices  4.54 us (13%)
  local copies, waits for them, and re-layouts  2.27 us (6%)
    ppermute x4, starting transfers between devices, on_device(): lax.ppermute(picked, 'stat', [(i, i ^ step) for i in range(stat_count)])  7.3 us
    ppermute x7, starting transfers between devices, on_device(): x = lax.ppermute(x, ('chan', 'tm'), pairs)  6.29 us
    pallas_call x2, Pallas kernels, correlate(): out = list(call(voltages, *ref_parts[chan], table, *before))  6.07 us
    pallas_call x1, Pallas kernels, gram_inverse(): pl.pallas_call(inverse_kernel, out_shape=jax.ShapeDtypeStruct((2 * ZERN,...  5.68 us
    ppermute x4, waiting for transfers between devices, on_device(): lax.ppermute(picked, 'stat', [(i, i ^ step) for i in range(stat_count)])  3.67 us
    unnamed x14, local copies, waits for them, and re-layouts  2.27 us
    pallas_call x1, Pallas kernels, collect(): pl.pallas_call(functools.partial(collect_kernel, shape), in_specs=[vmem]...  1.54 us
    pallas_call x1, Pallas kernels, tables(): pl.pallas_call(functools.partial(tables_kernel, scale), out_shape=jax.Sha...  1 us
  transfers between devices with their start and end apart: 11, of which 4 were waited for; matrix products, arithmetic and copies ran while one was open for 0% of the time, Pallas kernels for 27%

profile of v2, /device:TPU:0, one launch (start us, length us, event | category | flops | bytes accessed | tf_op | source)
XLA Modules:
  0.0 35.8 jit_solution(2687158537163983374)
XLA Ops:
  0.0 0.0 copy-start
  0.0 1.6 %copy-done = bf16[2,2,128,2048]{3,2,1,0:T(8,128)(2,1)S(1)} copy-done((bf16[2,2,128,2048]{3,2,1,0:T(8,128)(2,1)S(1)}, bf16[2,2,128,2048]{3,2,1,0:T(8,128)(2,1)}, u32[]{:S(2)}) %copy-start) | copy-done | bytes 2097176
  1.6 0.0 copy-start.2
  1.6 0.7 %copy-done.2 = s32[8]{0:T(128)S(1)} copy-done((s32[8]{0:T(128)S(1)}, s32[8]{0:T(128)}, u32[]{:S(2)}) %copy-start.2) | copy-done | bytes 56
  2.2 0.0 copy-start.3
  2.2 0.0 copy-start.4
  2.3 0.0 copy-start.5
  2.3 0.0 copy-start.6
  2.3 0.9 %pick_references.1 = (bf16[2,8,2048]{2,1,0:T(8,128)(2,1)S(1)}, bf16[2,8,2048]{2,1,0:T(8,128)(2,1)S(1)}) custom-call(s32[8]{0:T(128)S(1)} %copy-done.2, bf16[2,2,128,2048]{3,2,1,0:T(8,128)(2,1)S(1)} %copy-done), custom_call_target="tpu_custom_call" | custom-call | tf_op jit(solution)/shard_map/pick_references/pallas_call | solution.py:104
  3.2 3.4 %collective-permute-start.2 = (bf16[2,8,2048]{2,1,0:T(8,128)(2,1)S(1)}, bf16[2,8,2048]{2,1,0:T(8,128)(2,1)S(1)}, u32[]{:S(2)}, u32[]{:S(2)}) collective-permute-start(bf16[2,8,2048]{2,1,0:T(8,128)(2,1)S(1)} %get-tuple-element.19), channel_id=1, source_target_pairs={{0,1},{1,0},{2,3},{3,2},{4,5},{5,4},{6,7},{7,6},{8,9},{9,8},{10,11... | collective-permute-start | bytes 196616 | tf_op jit(solution)/shard_map/ppermute | solution.py:370
  6.6 0.1 collective-permute-start
  6.6 2.3 %collective-permute-done.2 = bf16[2,8,2048]{2,1,0:T(8,128)(2,1)S(1)} collective-permute-done((bf16[2,8,2048]{2,1,0:T(8,128)(2,1)S(1)}, bf16[2,8,2048]{2,1,0:T(8,128)(2,1)S(1)}, u32[]{:S(2)}, u32[]{:S(2)}) %collective-permute-start.2) | collective-permute-done | bytes 65568 | tf_op jit(solution)/shard_map/ppermute | solution.py:370
  9.0 3.0 %collective-permute-start.3 = (bf16[2,8,2048]{2,1,0:T(8,128)(2,1)S(1)}, bf16[2,8,2048]{2,1,0:T(8,128)(2,1)S(1)}, u32[]{:S(2)}, u32[]{:S(2)}) collective-permute-start(bf16[2,8,2048]{2,1,0:T(8,128)(2,1)S(1)} %add.7.args_1_), channel_id=1, source_target_pairs={{0,2},{1,3},{2,0},{3,1},{4,6},{5,7},{6,4},{7,5},{8,10},{9,11},{10,... | collective-permute-start | bytes 196616 | tf_op jit(solution)/shard_map/ppermute | solution.py:370
  12.0 0.0 copy-done.3
  12.0 0.0 copy-done.4
  12.0 0.0 copy-done.5
  12.0 0.0 copy-done.6
  12.0 0.0 copy-start.1
  12.0 1.0 %projection_per_sample.1.args_3_ = f32[128,2048]{1,0:T(8,128)S(1)} custom-call(f32[1,256]{1,0:T(1,128)S(1)} %bitcast.3, f32[64,256]{1,0:T(8,128)S(1)} %copy-done.6, f32[256,512]{1,0:T(8,128)S(1)} %copy-done.5, s32[1,2048]{1,0:T(1,128)S(1)} %bitcast.2), custom_call_target="tpu_custom_call" | custom-call | flops 4000000000 | bytes 2000000 | tf_op jit(solution)/shard_map/projection_per_sample/pallas_call | solution.py:157
  13.0 0.0 collective-permute-done
  13.1 0.8 %collective-permute-start.1 = (bf16[2,8,2048]{2,1,0:T(8,128)(2,1)S(1)}, bf16[2,8,2048]{2,1,0:T(8,128)(2,1)S(1)}, u32[]{:S(2)}, u32[]{:S(2)}) collective-permute-start(bf16[2,8,2048]{2,1,0:T(8,128)(2,1)S(1)} %add.6.args_1_), channel_id=1, source_target_pairs={{0,2},{1,3},{2,0},{3,1},{4,6},{5,7},{6,4},{7,5},{8,10},{9,11},{10,... | collective-permute-start | bytes 196616 | tf_op jit(solution)/shard_map/ppermute | solution.py:370
  13.9 0.3 collective-permute-done.3.args_2_
  14.2 0.0 copy-done.1
  14.3 3.0 %correlate.2 = (f32[128,128]{1,0:T(8,128)S(1)}, s16[896,128]{1,0:T(8,128)(2,1)S(1)}, f32[8,128]{1,0:T(8,128)S(1)}) custom-call(bf16[2,2,128,2048]{3,2,1,0:T(8,128)(2,1)S(1)} %copy-done.1, bf16[2,8,2048]{2,1,0:T(8,128)(2,1)S(1)} %add.7.args_1_, bf16[2,8,2048]{2,1,0:T(8,128)(2,1)S(1)} %collective-permute-done.3.args_2_, ...), custom_call_target="tpu_custom_call" | custom-call | flops 4300000256 | bytes 3000000 | tf_op jit(solution)/shard_map/correlate/pallas_call | solution.py:314
  17.3 1.0 %collective-permute-done.1.args_2_ = bf16[2,8,2048]{2,1,0:T(8,128)(2,1)S(1)} collective-permute-done((bf16[2,8,2048]{2,1,0:T(8,128)(2,1)S(1)}, bf16[2,8,2048]{2,1,0:T(8,128)(2,1)S(1)}, u32[]{:S(2)}, u32[]{:S(2)}) %collective-permute-start.1) | collective-permute-done | bytes 65568 | tf_op jit(solution)/shard_map/ppermute | solution.py:370
  18.3 3.0 %correlate.3 = (f32[2,128,128]{2,1,0:T(8,128)S(1)}, s16[272,128]{1,0:T(8,128)(2,1)S(1)}, s16[272,128]{1,0:T(8,128)(2,1)S(1)}, s16[272,128]{1,0:T(8,128)(2,1)S(1)...) custom-call(bf16[2,2,128,2048]{3,2,1,0:T(8,128)(2,1)S(1)} %copy-done, ...), custom_call_target="tpu_custom_call" | custom-call | flops 4300000256 | bytes 3000000 | tf_op jit(solution)/shard_map/correlate/pallas_call | solution.py:314
  21.3 0.5 %collective-permute-start.10 = (s16[272,128]{1,0:T(8,128)(2,1)S(1)}, s16[272,128]{1,0:T(8,128)(2,1)S(1)}, u32[]{:S(2)}, u32[]{:S(2)}) collective-permute-start(s16[272,128]{1,0:T(8,128)(2,1)S(1)} %get-tuple-element.30), channel_id=1, source_target_pairs={{0,28},{4,24},{8,20},{12,16},{16,12},{20,8},{24,4},{28,0},{1,29},{... | collective-permute-start | bytes 208904 | tf_op jit(solution)/shard_map/ppermute | solution.py:396
  21.9 2.1 %collective-permute-start.4 = (s16[272,128]{1,0:T(8,128)(2,1)S(1)}, s16[272,128]{1,0:T(8,128)(2,1)S(1)}, u32[]{:S(2)}, u32[]{:S(2)}) collective-permute-start(s16[272,128]{1,0:T(8,128)(2,1)S(1)} %get-tuple-element.24), channel_id=1, source_target_pairs={{0,8},{4,12},{8,0},{12,4},{16,24},{20,28},{24,16},{28,20},{1,9},{5... | collective-permute-start | bytes 208904 | tf_op jit(solution)/shard_map/ppermute | solution.py:396
  24.0 0.5 %collective-permute-start.5 = (s16[272,128]{1,0:T(8,128)(2,1)S(1)}, s16[272,128]{1,0:T(8,128)(2,1)S(1)}, u32[]{:S(2)}, u32[]{:S(2)}) collective-permute-start(s16[272,128]{1,0:T(8,128)(2,1)S(1)} %get-tuple-element.25), channel_id=1, source_target_pairs={{0,16},{4,20},{8,24},{12,28},{16,0},{20,4},{24,8},{28,12},{1,17},{... | collective-permute-start | bytes 208904 | tf_op jit(solution)/shard_map/ppermute | solution.py:396
  24.5 0.8 %collective-permute-start.6 = (s16[272,128]{1,0:T(8,128)(2,1)S(1)}, s16[272,128]{1,0:T(8,128)(2,1)S(1)}, u32[]{:S(2)}, u32[]{:S(2)}) collective-permute-start(s16[272,128]{1,0:T(8,128)(2,1)S(1)} %get-tuple-element.26), channel_id=1, source_target_pairs={{0,24},{4,28},{8,16},{12,20},{16,8},{20,12},{24,0},{28,4},{1,25},{... | collective-permute-start | bytes 208904 | tf_op jit(solution)/shard_map/ppermute | solution.py:396
  25.3 0.5 %collective-permute-start.7 = (s16[272,128]{1,0:T(8,128)(2,1)S(1)}, s16[272,128]{1,0:T(8,128)(2,1)S(1)}, u32[]{:S(2)}, u32[]{:S(2)}) collective-permute-start(s16[272,128]{1,0:T(8,128)(2,1)S(1)} %get-tuple-element.27), channel_id=1, source_target_pairs={{0,4},{4,0},{8,12},{12,8},{16,20},{20,16},{24,28},{28,24},{1,5},{5... | collective-permute-start | bytes 208904 | tf_op jit(solution)/shard_map/ppermute | solution.py:396
  25.8 0.9 %collective-permute-done.10.refs_7_ = s16[272,128]{1,0:T(8,128)(2,1)S(1)} collective-permute-done((s16[272,128]{1,0:T(8,128)(2,1)S(1)}, s16[272,128]{1,0:T(8,128)(2,1)S(1)}, u32[]{:S(2)}, u32[]{:S(2)}) %collective-permute-start.10) | collective-permute-done | bytes 69664 | tf_op jit(solution)/shard_map/ppermute | solution.py:396
  26.7 0.8 %collective-permute-start.8 = (s16[272,128]{1,0:T(8,128)(2,1)S(1)}, s16[272,128]{1,0:T(8,128)(2,1)S(1)}, u32[]{:S(2)}, u32[]{:S(2)}) collective-permute-start(s16[272,128]{1,0:T(8,128)(2,1)S(1)} %get-tuple-element.28), channel_id=1, source_target_pairs={{0,12},{4,8},{8,4},{12,0},{16,28},{20,24},{24,20},{28,16},{1,13},{... | collective-permute-start | bytes 208904 | tf_op jit(solution)/shard_map/ppermute | solution.py:396
  27.5 0.0 collective-permute-done.4.refs_1_
  27.5 1.0 %collective-permute-start.9 = (s16[272,128]{1,0:T(8,128)(2,1)S(1)}, s16[272,128]{1,0:T(8,128)(2,1)S(1)}, u32[]{:S(2)}, u32[]{:S(2)}) collective-permute-start(s16[272,128]{1,0:T(8,128)(2,1)S(1)} %get-tuple-element.29), channel_id=1, source_target_pairs={{0,20},{4,16},{8,28},{12,24},{16,4},{20,0},{24,12},{28,8},{1,21},{... | collective-permute-start | bytes 208904 | tf_op jit(solution)/shard_map/ppermute | solution.py:396
  28.5 5.7 %gram_inverse.1.refs_8_ = f32[128,128]{1,0:T(8,128)S(1)} custom-call(f32[1,256]{1,0:T(1,128)S(1)} %bitcast.4, f32[64,256]{1,0:T(8,128)S(1)} %copy-done.6), custom_call_target="tpu_custom_call" | custom-call | flops 5000000000 | bytes 200000 | tf_op jit(solution)/shard_map/gram_inverse/pallas_call | solution.py:179
  34.2 0.0 collective-permute-done.5.refs_2_
  34.2 0.0 collective-permute-done.6.refs_3_
  34.2 0.0 collective-permute-done.7.refs_4_
  34.2 0.0 collective-permute-done.8.refs_5_
  34.2 0.0 collective-permute-done.9.refs_6_
  34.2 1.5 %sum_and_solve.1 = f32[16,8,8,128]{3,2,1,0:T(8,128)} custom-call(f32[2,128,128]{2,1,0:T(8,128)S(1)} %get-tuple-element.23.refs_0_, s16[272,128]{1,0:T(8,128)(2,1)S(1)} %collective-permute-done.4.refs_1_, s16[272,128]{1,0:T(8,128)(2,1)S(1)} %collective-permute-done.5.refs_2_, s16[272,128]{1,0:T(8,128)(2,1)S(1)} %collective-permute-done.6.refs_3_, ...), custom_call_target="tpu_custom_call" | custom-call | tf_op jit(solution)/shard_map/sum_and_solve/pallas_call | solution.py:348
  (2 shorter events, 0.0 us)
Async XLA Ops:
  0.0 1.6 %copy-start = (bf16[2,2,128,2048]{3,2,1,0:T(8,128)(2,1)S(1)}, bf16[2,2,128,2048]{3,2,1,0:T(8,128)(2,1)}, u32[]{:S(2)}) copy-start(bf16[2,2,128,2048]{3,2,1,0:T(8,128)(2,1)} %args_0_.6) | copy-start | bytes 6291460
  1.6 0.7 %copy-start.2 = (s32[8]{0:T(128)S(1)}, s32[8]{0:T(128)}, u32[]{:S(2)}) copy-start(s32[8]{0:T(128)} %index_ref.1) | copy-start | bytes 100
  2.2 9.8 %copy-start.3 = (s32[2048]{0:T(1024)S(1)}, s32[2048]{0:T(1024)}, u32[]{:S(2)}) copy-start(s32[2048]{0:T(1024)} %param.9) | copy-start | bytes 24580
  2.2 9.8 %copy-start.4 = (f32[256]{0:T(256)S(1)}, f32[256]{0:T(256)}, u32[]{:S(2)}) copy-start(f32[256]{0:T(256)} %param.10) | copy-start | bytes 3076
  2.3 9.8 %copy-start.5 = (f32[256,512]{1,0:T(8,128)S(1)}, f32[256,512]{1,0:T(8,128)}, u32[]{:S(2)}) copy-start(f32[256,512]{1,0:T(8,128)} %constant.5.clone.dft_ref) | copy-start | bytes 1572868
  2.3 9.8 %copy-start.6 = (f32[64,256]{1,0:T(8,128)S(1)}, f32[64,256]{1,0:T(8,128)}, u32[]{:S(2)}) copy-start(f32[64,256]{1,0:T(8,128)} %constant.4.clone.zern_ref) | copy-start | bytes 196612
  3.2 5.8 %collective-permute-start.2 = (bf16[2,8,2048]{2,1,0:T(8,128)(2,1)S(1)}, bf16[2,8,2048]{2,1,0:T(8,128)(2,1)S(1)}, u32[]{:S(2)}, u32[]{:S(2)}) collective-permute-start(bf16[2,8,2048]{2,1,0:T(8,128)(2,1)S(1)} %get-tuple-element.19), channel_id=1, source_target_pairs={{0,1},{1,0},{2,3},{3,2},{4,5},{5,4},{6,7},{7,6},{8,9},{9,8},{10,11... | collective-permute-start | bytes 196616 | tf_op jit(solution)/shard_map/ppermute | solution.py:370
  6.6 6.5 %collective-permute-start = (bf16[2,8,2048]{2,1,0:T(8,128)(2,1)S(1)}, bf16[2,8,2048]{2,1,0:T(8,128)(2,1)S(1)}, u32[]{:S(2)}, u32[]{:S(2)}) collective-permute-start(bf16[2,8,2048]{2,1,0:T(8,128)(2,1)S(1)} %get-tuple-element.18), channel_id=1, source_target_pairs={{0,1},{1,0},{2,3},{3,2},{4,5},{5,4},{6,7},{7,6},{8,9},{9,8},{10,11... | collective-permute-start | bytes 196616 | tf_op jit(solution)/shard_map/ppermute | solution.py:370
  9.0 5.3 %collective-permute-start.3 = (bf16[2,8,2048]{2,1,0:T(8,128)(2,1)S(1)}, bf16[2,8,2048]{2,1,0:T(8,128)(2,1)S(1)}, u32[]{:S(2)}, u32[]{:S(2)}) collective-permute-start(bf16[2,8,2048]{2,1,0:T(8,128)(2,1)S(1)} %add.7.args_1_), channel_id=1, source_target_pairs={{0,2},{1,3},{2,0},{3,1},{4,6},{5,7},{6,4},{7,5},{8,10},{9,11},{10,... | collective-permute-start | bytes 196616 | tf_op jit(solution)/shard_map/ppermute | solution.py:370
  12.0 2.2 %copy-start.1 = (bf16[2,2,128,2048]{3,2,1,0:T(8,128)(2,1)S(1)}, bf16[2,2,128,2048]{3,2,1,0:T(8,128)(2,1)}, u32[]{:S(2)}) copy-start(bf16[2,2,128,2048]{3,2,1,0:T(8,128)(2,1)} %args_0_.6) | copy-start | bytes 6291460
  13.1 5.2 %collective-permute-start.1 = (bf16[2,8,2048]{2,1,0:T(8,128)(2,1)S(1)}, bf16[2,8,2048]{2,1,0:T(8,128)(2,1)S(1)}, u32[]{:S(2)}, u32[]{:S(2)}) collective-permute-start(bf16[2,8,2048]{2,1,0:T(8,128)(2,1)S(1)} %add.6.args_1_), channel_id=1, source_target_pairs={{0,2},{1,3},{2,0},{3,1},{4,6},{5,7},{6,4},{7,5},{8,10},{9,11},{10,... | collective-permute-start | bytes 196616 | tf_op jit(solution)/shard_map/ppermute | solution.py:370
  21.3 5.3 %collective-permute-start.10 = (s16[272,128]{1,0:T(8,128)(2,1)S(1)}, s16[272,128]{1,0:T(8,128)(2,1)S(1)}, u32[]{:S(2)}, u32[]{:S(2)}) collective-permute-start(s16[272,128]{1,0:T(8,128)(2,1)S(1)} %get-tuple-element.30), channel_id=1, source_target_pairs={{0,28},{4,24},{8,20},{12,16},{16,12},{20,8},{24,4},{28,0},{1,29},{... | collective-permute-start | bytes 208904 | tf_op jit(solution)/shard_map/ppermute | solution.py:396
  21.9 5.6 %collective-permute-start.4 = (s16[272,128]{1,0:T(8,128)(2,1)S(1)}, s16[272,128]{1,0:T(8,128)(2,1)S(1)}, u32[]{:S(2)}, u32[]{:S(2)}) collective-permute-start(s16[272,128]{1,0:T(8,128)(2,1)S(1)} %get-tuple-element.24), channel_id=1, source_target_pairs={{0,8},{4,12},{8,0},{12,4},{16,24},{20,28},{24,16},{28,20},{1,9},{5... | collective-permute-start | bytes 208904 | tf_op jit(solution)/shard_map/ppermute | solution.py:396
  24.0 10.2 %collective-permute-start.5 = (s16[272,128]{1,0:T(8,128)(2,1)S(1)}, s16[272,128]{1,0:T(8,128)(2,1)S(1)}, u32[]{:S(2)}, u32[]{:S(2)}) collective-permute-start(s16[272,128]{1,0:T(8,128)(2,1)S(1)} %get-tuple-element.25), channel_id=1, source_target_pairs={{0,16},{4,20},{8,24},{12,28},{16,0},{20,4},{24,8},{28,12},{1,17},{... | collective-permute-start | bytes 208904 | tf_op jit(solution)/shard_map/ppermute | solution.py:396
  24.5 9.7 %collective-permute-start.6 = (s16[272,128]{1,0:T(8,128)(2,1)S(1)}, s16[272,128]{1,0:T(8,128)(2,1)S(1)}, u32[]{:S(2)}, u32[]{:S(2)}) collective-permute-start(s16[272,128]{1,0:T(8,128)(2,1)S(1)} %get-tuple-element.26), channel_id=1, source_target_pairs={{0,24},{4,28},{8,16},{12,20},{16,8},{20,12},{24,0},{28,4},{1,25},{... | collective-permute-start | bytes 208904 | tf_op jit(solution)/shard_map/ppermute | solution.py:396
  25.3 8.9 %collective-permute-start.7 = (s16[272,128]{1,0:T(8,128)(2,1)S(1)}, s16[272,128]{1,0:T(8,128)(2,1)S(1)}, u32[]{:S(2)}, u32[]{:S(2)}) collective-permute-start(s16[272,128]{1,0:T(8,128)(2,1)S(1)} %get-tuple-element.27), channel_id=1, source_target_pairs={{0,4},{4,0},{8,12},{12,8},{16,20},{20,16},{24,28},{28,24},{1,5},{5... | collective-permute-start | bytes 208904 | tf_op jit(solution)/shard_map/ppermute | solution.py:396
  26.7 7.5 %collective-permute-start.8 = (s16[272,128]{1,0:T(8,128)(2,1)S(1)}, s16[272,128]{1,0:T(8,128)(2,1)S(1)}, u32[]{:S(2)}, u32[]{:S(2)}) collective-permute-start(s16[272,128]{1,0:T(8,128)(2,1)S(1)} %get-tuple-element.28), channel_id=1, source_target_pairs={{0,12},{4,8},{8,4},{12,0},{16,28},{20,24},{24,20},{28,16},{1,13},{... | collective-permute-start | bytes 208904 | tf_op jit(solution)/shard_map/ppermute | solution.py:396
  27.5 6.8 %collective-permute-start.9 = (s16[272,128]{1,0:T(8,128)(2,1)S(1)}, s16[272,128]{1,0:T(8,128)(2,1)S(1)}, u32[]{:S(2)}, u32[]{:S(2)}) collective-permute-start(s16[272,128]{1,0:T(8,128)(2,1)S(1)} %get-tuple-element.29), channel_id=1, source_target_pairs={{0,20},{4,16},{8,28},{12,24},{16,4},{20,0},{24,12},{28,8},{1,21},{... | collective-permute-start | bytes 208904 | tf_op jit(solution)/shard_map/ppermute | solution.py:396

commit v3 on v2

--- a/solution.py
+++ b/solution.py
@@ -66,33 +66,31 @@
     return np.concatenate([np.cos(angles), -np.sin(angles)], axis=1).astype(np.float32)
 
 
-def pick_kernel(index_ref, volt_ref, *rest):
-    *out_refs, group_ref, rows_ref, sems = rest
+def pick_kernel(index_hbm, volt_hbm, *rest):
+    *out_refs, index_ref, volt_ref, rows_ref, index_sem, volt_sem = rest
     chans, parts, stations, _ = volt_ref.shape
     refs = rows_ref.shape[2]
+    index_copy = pltpu.make_async_copy(index_hbm, index_ref, index_sem)
+    volt_copy = pltpu.make_async_copy(volt_hbm, volt_ref, volt_sem)
+    index_copy.start()
+    volt_copy.start()
+    rows_ref[...] = jnp.zeros_like(rows_ref)
     first = lax.axis_index("stat") * stations
-
-    def each_owned(work):
-        for r in range(refs):
-            local = index_ref[r] - first
-            pl.when(jnp.logical_and(local >= 0, local < stations))(functools.partial(work, r, local))
-
-    def copy(r, local):
-        begin = pl.multiple_of(local // GROUP * GROUP, GROUP)
-        return pltpu.make_async_copy(volt_ref.at[:, :, pl.ds(begin, GROUP), :], group_ref.at[r], sems.at[r])
-
-    def fill(r, local):
-        copy(r, local).wait()
-        for c in range(chans):
-            for k in range(parts):
-                group = group_ref[r, c, k].astype(jnp.float32)
-                row = lax.broadcasted_iota(jnp.int32, group.shape, 0)
-                group = jnp.where(row == lax.rem(local, GROUP), group, 0.0)
-                rows_ref[c, k, r : r + 1, :] = jnp.sum(group, axis=0, keepdims=True)
-
-    each_owned(lambda r, local: copy(r, local).start())
-    rows_ref[...] = jnp.zeros_like(rows_ref)
-    each_owned(fill)
+    index_copy.wait()
+    volt_copy.wait()
+    for r in range(refs):
+        local = index_ref[r] - first
+
+        @pl.when(jnp.logical_and(local >= 0, local < stations))
+        def _():
+            begin = pl.multiple_of(local // GROUP * GROUP, GROUP)
+            for c in range(chans):
+                for k in range(parts):
+                    group = volt_ref[c, k, pl.ds(begin, GROUP), :].astype(jnp.float32)
+                    row = lax.broadcasted_iota(jnp.int32, group.shape, 0)
+                    group = jnp.where(row == local - begin, group, 0.0)
+                    rows_ref[c, k, r : r + 1, :] = jnp.sum(group, axis=0, keepdims=True)
+
     for c, out_ref in enumerate(out_refs):
         out_ref[...] = rows_ref[c].astype(jnp.bfloat16)
 
@@ -103,17 +101,22 @@
     vmem = pl.BlockSpec(memory_space=pltpu.VMEM)
     return pl.pallas_call(
         pick_kernel,
-        in_specs=[pl.BlockSpec(memory_space=pltpu.SMEM), pl.BlockSpec(memory_space=pl.ANY)],
+        in_specs=[pl.BlockSpec(memory_space=pltpu.HBM)] * 2,
         out_specs=[vmem] * chans,
         out_shape=[jax.ShapeDtypeStruct((parts, refs, times), jnp.bfloat16)] * chans,
         scratch_shapes=[
-            pltpu.VMEM((refs, chans, parts, GROUP, times), jnp.bfloat16),
+            pltpu.SMEM((refs,), jnp.int32),
+            pltpu.VMEM(voltages.shape, jnp.bfloat16),
             pltpu.VMEM((chans, parts, refs, times), jnp.float32),
-            pltpu.SemaphoreType.DMA((refs,)),
+            pltpu.SemaphoreType.DMA,
+            pltpu.SemaphoreType.DMA,
         ],
         compiler_params=pltpu.CompilerParams(vmem_limit_bytes=8 * 2**20),
         name="pick_references",
-    )(ref_index, voltages)
+    )(
+        pltpu.with_memory_space_constraint(ref_index, pltpu.HBM),
+        pltpu.with_memory_space_constraint(voltages, pltpu.HBM),
+    )
 
 
 def invert(gram):
@@ -121,11 +124,35 @@
     row = lax.broadcasted_iota(jnp.int32, (size, size), 0)
     lane = lax.broadcasted_iota(jnp.int32, (size, size), 1)
     work = jnp.concatenate([gram, jnp.where(row == lane, 1.0, 0.0)], axis=1)
-    row = lax.broadcasted_iota(jnp.int32, work.shape, 0)
-    for k in range(size):
-        pivot = work[k : k + 1, :] / work[k : k + 1, k : k + 1]
-        work = jnp.where(row == k, pivot, work - work[:, k : k + 1] * pivot)
-    return work[:, size:]
+    shape = (8, 2 * size)
+    tiles = [work[t : t + 8] for t in range(0, size, 8)]
+    row = lax.broadcasted_iota(jnp.int32, shape, 0)
+    for k in range(0, size, 4):
+        home, begin = divmod(k, 8)
+        r = [jnp.broadcast_to(tiles[home][begin + i : begin + i + 1], shape) for i in range(4)]
+        p = {
+            (i, j): jnp.broadcast_to(r[i][:, k + j : k + j + 1], shape) for i in range(4) for j in range(i, 4)
+        }
+        columns = [[jnp.broadcast_to(x[:, k + j : k + j + 1], shape) for j in range(4)] for x in tiles]
+        scale = 1.0 / (p[0, 0] * p[1, 1] - p[0, 1] * p[0, 1])
+        a00, a01, a11 = p[1, 1] * scale, -p[0, 1] * scale, p[0, 0] * scale
+        f00, f01 = a00 * p[0, 2] + a01 * p[1, 2], a00 * p[0, 3] + a01 * p[1, 3]
+        f10, f11 = a01 * p[0, 2] + a11 * p[1, 2], a01 * p[0, 3] + a11 * p[1, 3]
+        s00 = p[2, 2] - p[0, 2] * f00 - p[1, 2] * f10
+        s01 = p[2, 3] - p[0, 2] * f01 - p[1, 2] * f11
+        s11 = p[3, 3] - p[0, 3] * f01 - p[1, 3] * f11
+        scale = 1.0 / (s00 * s11 - s01 * s01)
+        x0, x1 = a00 * r[0] + a01 * r[1], a01 * r[0] + a11 * r[1]
+        y0, y1 = r[2] - p[0, 2] * x0 - p[1, 2] * x1, r[3] - p[0, 3] * x0 - p[1, 3] * x1
+        n2, n3 = (s11 * y0 - s01 * y1) * scale, (s00 * y1 - s01 * y0) * scale
+        new = [x0 - f00 * n2 - f01 * n3, x1 - f10 * n2 - f11 * n3, n2, n3]
+        for t, c in enumerate(columns):
+            tile = tiles[t] - (c[0] * new[0] + c[1] * new[1]) - (c[2] * new[2] + c[3] * new[3])
+            if t == home:
+                for i in range(4):
+                    tile = jnp.where(row == begin + i, new[i], tile)
+            tiles[t] = tile
+    return jnp.concatenate(tiles, axis=0)[:, size:]
 
 
 def split(value, parts):

time: 36.1 us -> 35.1 us (0.972); the launches traced: 35.8 us -> 35.1 us
  local copies, waits for them, and re-layouts: 2.27 us -> 0.02 us
  starting transfers between devices: 13.6 us -> 15.3 us
  Pallas kernels: 15.2 us -> 13.9 us
  waiting for transfers between devices: 4.54 us -> 5.76 us
    pallas_call x1, Pallas kernels: 5.68 us -> 3.08 us  [gram_inverse(): pl.pallas_call(inverse_kernel, out_shape=jax.ShapeDtypeStruct((2 * ZERN,...]
    ppermute x7, starting transfers between devices: 6.29 us -> 8.84 us  [on_device(): x = lax.ppermute(x, ('chan', 'tm'), pairs)]
    unnamed x14 -> x10, local copies, waits for them, and re-layouts: 2.27 us -> 0.02 us
    pallas_call x1, Pallas kernels: 0.93 us -> 2.21 us  [pick(): pl.pallas_call(pick_kernel, in_specs=[pl.BlockSpec(memory_space=pltpu.HBM...]
    ppermute x4, starting transfers between devices: 7.3 us -> 6.47 us  [on_device(): lax.ppermute(picked, 'stat', [(i, i ^ step) for i in range(stat_count)])]
    ppermute x4, waiting for transfers between devices: 3.67 us -> 4.36 us  [on_device(): lax.ppermute(picked, 'stat', [(i, i ^ step) for i in range(stat_count)])]
    ppermute x7, waiting for transfers between devices: 0.87 us -> 1.4 us  [on_device(): x = lax.ppermute(x, ('chan', 'tm'), pairs)]
  transfers between devices with their start and end apart: 11 -> 11, of which waited for: 4 -> 4; matrix products, arithmetic and copies ran while one was open for 0% -> 0% of each run, Pallas kernels for 27% -> 20%
where the time goes in v3:
time: 35.1 us
  starting transfers between devices  15.3 us (44%)
  Pallas kernels  13.9 us (40%)
  waiting for transfers between devices  5.76 us (16%)
    ppermute x7, starting transfers between devices, on_device(): x = lax.ppermute(x, ('chan', 'tm'), pairs)  8.84 us
    ppermute x4, starting transfers between devices, on_device(): lax.ppermute(picked, 'stat', [(i, i ^ step) for i in range(stat_count)])  6.47 us
    pallas_call x2, Pallas kernels, correlate(): out = list(call(voltages, *ref_parts[chan], table, *before))  6.07 us
    ppermute x4, waiting for transfers between devices, on_device(): lax.ppermute(picked, 'stat', [(i, i ^ step) for i in range(stat_count)])  4.36 us
    pallas_call x1, Pallas kernels, gram_inverse(): pl.pallas_call(inverse_kernel, out_shape=jax.ShapeDtypeStruct((2 * ZERN,...  3.08 us
    pallas_call x1, Pallas kernels, pick(): pl.pallas_call(pick_kernel, in_specs=[pl.BlockSpec(memory_space=pltpu.HBM...  2.21 us
    pallas_call x1, Pallas kernels, collect(): pl.pallas_call(functools.partial(collect_kernel, shape), in_specs=[vmem]...  1.54 us
    ppermute x7, waiting for transfers between devices, on_device(): x = lax.ppermute(x, ('chan', 'tm'), pairs)  1.4 us
  transfers between devices with their start and end apart: 11, of which 4 were waited for; matrix products, arithmetic and copies ran while one was open for 0% of the time, Pallas kernels for 20%

profile of v3, /device:TPU:0, one launch (start us, length us, event | category | flops | bytes accessed | tf_op | source)
XLA Modules:
  0.0 35.1 jit_solution(46280953059954820)
XLA Ops:
  0.0 0.0 copy-start.4
  0.0 0.0 copy-start.3
  0.0 0.0 copy-start.2
  0.0 0.0 copy-start.1
  0.0 2.2 %pick_references.1 = (bf16[2,8,2048]{2,1,0:T(8,128)(2,1)S(1)}, bf16[2,8,2048]{2,1,0:T(8,128)(2,1)S(1)}) custom-call(s32[8]{0:T(128)} %index_hbm.1, bf16[2,2,128,2048]{3,2,1,0:T(8,128)(2,1)} %args_0_.6), custom_call_target="tpu_custom_call" | custom-call | tf_op jit(solution)/shard_map/pick_references/pallas_call | solution.py:102
  2.2 2.9 %collective-permute-start.2 = (bf16[2,8,2048]{2,1,0:T(8,128)(2,1)S(1)}, bf16[2,8,2048]{2,1,0:T(8,128)(2,1)S(1)}, u32[]{:S(2)}, u32[]{:S(2)}) collective-permute-start(bf16[2,8,2048]{2,1,0:T(8,128)(2,1)S(1)} %get-tuple-element.19), channel_id=1, source_target_pairs={{0,1},{1,0},{2,3},{3,2},{4,5},{5,4},{6,7},{7,6},{8,9},{9,8},{10,11... | collective-permute-start | bytes 196616 | tf_op jit(solution)/shard_map/ppermute | solution.py:397
  5.1 0.1 collective-permute-start
  5.2 2.3 %collective-permute-done.2 = bf16[2,8,2048]{2,1,0:T(8,128)(2,1)S(1)} collective-permute-done((bf16[2,8,2048]{2,1,0:T(8,128)(2,1)S(1)}, bf16[2,8,2048]{2,1,0:T(8,128)(2,1)S(1)}, u32[]{:S(2)}, u32[]{:S(2)}) %collective-permute-start.2) | collective-permute-done | bytes 65568 | tf_op jit(solution)/shard_map/ppermute | solution.py:397
  7.5 3.4 %collective-permute-start.3 = (bf16[2,8,2048]{2,1,0:T(8,128)(2,1)S(1)}, bf16[2,8,2048]{2,1,0:T(8,128)(2,1)S(1)}, u32[]{:S(2)}, u32[]{:S(2)}) collective-permute-start(bf16[2,8,2048]{2,1,0:T(8,128)(2,1)S(1)} %add.7.args_1_), channel_id=1, source_target_pairs={{0,2},{1,3},{2,0},{3,1},{4,6},{5,7},{6,4},{7,5},{8,10},{9,11},{10,... | collective-permute-start | bytes 196616 | tf_op jit(solution)/shard_map/ppermute | solution.py:397
  10.9 0.0 copy-done.4
  10.9 0.0 copy-done.3
  10.9 0.0 copy-done.2
  10.9 0.0 copy-done.1
  10.9 0.0 copy-start
  10.9 1.0 %projection_per_sample.1.args_3_ = f32[128,2048]{1,0:T(8,128)S(1)} custom-call(f32[1,256]{1,0:T(1,128)S(1)} %bitcast.3, f32[64,256]{1,0:T(8,128)S(1)} %copy-done.4, f32[256,512]{1,0:T(8,128)S(1)} %copy-done.3, s32[1,2048]{1,0:T(1,128)S(1)} %bitcast.2), custom_call_target="tpu_custom_call" | custom-call | flops 4000000000 | bytes 2000000 | tf_op jit(solution)/shard_map/projection_per_sample/pallas_call | solution.py:184
  11.9 0.0 collective-permute-done
  12.0 0.1 collective-permute-start.1
  12.1 1.0 %collective-permute-done.3.args_2_ = bf16[2,8,2048]{2,1,0:T(8,128)(2,1)S(1)} collective-permute-done((bf16[2,8,2048]{2,1,0:T(8,128)(2,1)S(1)}, bf16[2,8,2048]{2,1,0:T(8,128)(2,1)S(1)}, u32[]{:S(2)}, u32[]{:S(2)}) %collective-permute-start.3) | collective-permute-done | bytes 65568 | tf_op jit(solution)/shard_map/ppermute | solution.py:397
  13.1 0.0 copy-done
  13.1 3.0 %correlate.2 = (f32[128,128]{1,0:T(8,128)S(1)}, s16[896,128]{1,0:T(8,128)(2,1)S(1)}, f32[8,128]{1,0:T(8,128)S(1)}) custom-call(bf16[2,2,128,2048]{3,2,1,0:T(8,128)(2,1)S(1)} %copy-done, bf16[2,8,2048]{2,1,0:T(8,128)(2,1)S(1)} %add.7.args_1_, bf16[2,8,2048]{2,1,0:T(8,128)(2,1)S(1)} %collective-permute-done.3.args_2_, f32[128,2048]{1,0:T(8,128)S(1)} %projection_per_sample.1.args_3_), custom_call_target="tpu_custom_call" | custom-call | flops 4300000256 | bytes 3000000 | tf_op jit(solution)/shard_map/correlate/pallas_call | solution.py:341
  16.2 1.0 %collective-permute-done.1.args_2_ = bf16[2,8,2048]{2,1,0:T(8,128)(2,1)S(1)} collective-permute-done((bf16[2,8,2048]{2,1,0:T(8,128)(2,1)S(1)}, bf16[2,8,2048]{2,1,0:T(8,128)(2,1)S(1)}, u32[]{:S(2)}, u32[]{:S(2)}) %collective-permute-start.1) | collective-permute-done | bytes 65568 | tf_op jit(solution)/shard_map/ppermute | solution.py:397
  17.2 3.0 %correlate.3 = (f32[2,128,128]{2,1,0:T(8,128)S(1)}, s16[272,128]{1,0:T(8,128)(2,1)S(1)}, s16[272,128]{1,0:T(8,128)(2,1)S(1)}, s16[272,128]{1,0:T(8,128)(2,1)S(1)...) custom-call(bf16[2,2,128,2048]{3,2,1,0:T(8,128)(2,1)S(1)} %copy-done, ...), custom_call_target="tpu_custom_call" | custom-call | flops 4300000256 | bytes 3000000 | tf_op jit(solution)/shard_map/correlate/pallas_call | solution.py:341
  20.2 0.9 %collective-permute-start.10 = (s16[272,128]{1,0:T(8,128)(2,1)S(1)}, s16[272,128]{1,0:T(8,128)(2,1)S(1)}, u32[]{:S(2)}, u32[]{:S(2)}) collective-permute-start(s16[272,128]{1,0:T(8,128)(2,1)S(1)} %get-tuple-element.30), channel_id=1, source_target_pairs={{0,28},{4,24},{8,20},{12,16},{16,12},{20,8},{24,4},{28,0},{1,29},{... | collective-permute-start | bytes 208904 | tf_op jit(solution)/shard_map/ppermute | solution.py:423
  21.1 3.5 %collective-permute-start.4 = (s16[272,128]{1,0:T(8,128)(2,1)S(1)}, s16[272,128]{1,0:T(8,128)(2,1)S(1)}, u32[]{:S(2)}, u32[]{:S(2)}) collective-permute-start(s16[272,128]{1,0:T(8,128)(2,1)S(1)} %get-tuple-element.24), channel_id=1, source_target_pairs={{0,8},{4,12},{8,0},{12,4},{16,24},{20,28},{24,16},{28,20},{1,9},{5... | collective-permute-start | bytes 208904 | tf_op jit(solution)/shard_map/ppermute | solution.py:423
  24.6 0.5 %collective-permute-start.5 = (s16[272,128]{1,0:T(8,128)(2,1)S(1)}, s16[272,128]{1,0:T(8,128)(2,1)S(1)}, u32[]{:S(2)}, u32[]{:S(2)}) collective-permute-start(s16[272,128]{1,0:T(8,128)(2,1)S(1)} %get-tuple-element.25), channel_id=1, source_target_pairs={{0,16},{4,20},{8,24},{12,28},{16,0},{20,4},{24,8},{28,12},{1,17},{... | collective-permute-start | bytes 208904 | tf_op jit(solution)/shard_map/ppermute | solution.py:423
  25.1 0.8 %collective-permute-start.6 = (s16[272,128]{1,0:T(8,128)(2,1)S(1)}, s16[272,128]{1,0:T(8,128)(2,1)S(1)}, u32[]{:S(2)}, u32[]{:S(2)}) collective-permute-start(s16[272,128]{1,0:T(8,128)(2,1)S(1)} %get-tuple-element.26), channel_id=1, source_target_pairs={{0,24},{4,28},{8,16},{12,20},{16,8},{20,12},{24,0},{28,4},{1,25},{... | collective-permute-start | bytes 208904 | tf_op jit(solution)/shard_map/ppermute | solution.py:423
  25.9 0.5 %collective-permute-start.7 = (s16[272,128]{1,0:T(8,128)(2,1)S(1)}, s16[272,128]{1,0:T(8,128)(2,1)S(1)}, u32[]{:S(2)}, u32[]{:S(2)}) collective-permute-start(s16[272,128]{1,0:T(8,128)(2,1)S(1)} %get-tuple-element.27), channel_id=1, source_target_pairs={{0,4},{4,0},{8,12},{12,8},{16,20},{20,16},{24,28},{28,24},{1,5},{5... | collective-permute-start | bytes 208904 | tf_op jit(solution)/shard_map/ppermute | solution.py:423
  26.4 0.0 collective-permute-done.10.refs_7_
  26.4 1.6 %collective-permute-start.8 = (s16[272,128]{1,0:T(8,128)(2,1)S(1)}, s16[272,128]{1,0:T(8,128)(2,1)S(1)}, u32[]{:S(2)}, u32[]{:S(2)}) collective-permute-start(s16[272,128]{1,0:T(8,128)(2,1)S(1)} %get-tuple-element.28), channel_id=1, source_target_pairs={{0,12},{4,8},{8,4},{12,0},{16,28},{20,24},{24,20},{28,16},{1,13},{... | collective-permute-start | bytes 208904 | tf_op jit(solution)/shard_map/ppermute | solution.py:423
  28.1 0.0 collective-permute-done.4.refs_1_
  28.1 1.0 %collective-permute-start.9 = (s16[272,128]{1,0:T(8,128)(2,1)S(1)}, s16[272,128]{1,0:T(8,128)(2,1)S(1)}, u32[]{:S(2)}, u32[]{:S(2)}) collective-permute-start(s16[272,128]{1,0:T(8,128)(2,1)S(1)} %get-tuple-element.29), channel_id=1, source_target_pairs={{0,20},{4,16},{8,28},{12,24},{16,4},{20,0},{24,12},{28,8},{1,21},{... | collective-permute-start | bytes 208904 | tf_op jit(solution)/shard_map/ppermute | solution.py:423
  29.1 3.1 %gram_inverse.1.refs_8_ = f32[128,128]{1,0:T(8,128)S(1)} custom-call(f32[1,256]{1,0:T(1,128)S(1)} %bitcast.4, f32[64,256]{1,0:T(8,128)S(1)} %copy-done.4), custom_call_target="tpu_custom_call" | custom-call | flops 5000000000 | bytes 200000 | tf_op jit(solution)/shard_map/gram_inverse/pallas_call | solution.py:206
  32.2 0.0 collective-permute-done.5.refs_2_
  32.2 0.0 collective-permute-done.6.refs_3_
  32.2 0.0 collective-permute-done.7.refs_4_
  32.2 1.4 %collective-permute-done.8.refs_5_ = s16[272,128]{1,0:T(8,128)(2,1)S(1)} collective-permute-done((s16[272,128]{1,0:T(8,128)(2,1)S(1)}, s16[272,128]{1,0:T(8,128)(2,1)S(1)}, u32[]{:S(2)}, u32[]{:S(2)}) %collective-permute-start.8) | collective-permute-done | bytes 69664 | tf_op jit(solution)/shard_map/ppermute | solution.py:423
  33.6 0.0 collective-permute-done.9.refs_6_
  33.6 1.5 %sum_and_solve.1 = f32[16,8,8,128]{3,2,1,0:T(8,128)} custom-call(f32[2,128,128]{2,1,0:T(8,128)S(1)} %get-tuple-element.23.refs_0_, s16[272,128]{1,0:T(8,128)(2,1)S(1)} %collective-permute-done.4.refs_1_, s16[272,128]{1,0:T(8,128)(2,1)S(1)} %collective-permute-done.5.refs_2_, s16[272,128]{1,0:T(8,128)(2,1)S(1)} %collective-permute-done.6.refs_3_, ...), custom_call_target="tpu_custom_call" | custom-call | tf_op jit(solution)/shard_map/sum_and_solve/pallas_call | solution.py:375
  (2 shorter events, 0.0 us)
Async XLA Ops:
  0.0 10.9 %copy-start.4 = (f32[64,256]{1,0:T(8,128)S(1)}, f32[64,256]{1,0:T(8,128)}, u32[]{:S(2)}) copy-start(f32[64,256]{1,0:T(8,128)} %constant.4.clone.zern_ref) | copy-start | bytes 196612
  0.0 10.9 %copy-start.3 = (f32[256,512]{1,0:T(8,128)S(1)}, f32[256,512]{1,0:T(8,128)}, u32[]{:S(2)}) copy-start(f32[256,512]{1,0:T(8,128)} %constant.5.clone.dft_ref) | copy-start | bytes 1572868
  0.0 10.9 %copy-start.2 = (f32[256]{0:T(256)S(1)}, f32[256]{0:T(256)}, u32[]{:S(2)}) copy-start(f32[256]{0:T(256)} %param.10) | copy-start | bytes 3076
  0.0 10.9 %copy-start.1 = (s32[2048]{0:T(1024)S(1)}, s32[2048]{0:T(1024)}, u32[]{:S(2)}) copy-start(s32[2048]{0:T(1024)} %param.9) | copy-start | bytes 24580
  2.2 5.3 %collective-permute-start.2 = (bf16[2,8,2048]{2,1,0:T(8,128)(2,1)S(1)}, bf16[2,8,2048]{2,1,0:T(8,128)(2,1)S(1)}, u32[]{:S(2)}, u32[]{:S(2)}) collective-permute-start(bf16[2,8,2048]{2,1,0:T(8,128)(2,1)S(1)} %get-tuple-element.19), channel_id=1, source_target_pairs={{0,1},{1,0},{2,3},{3,2},{4,5},{5,4},{6,7},{7,6},{8,9},{9,8},{10,11... | collective-permute-start | bytes 196616 | tf_op jit(solution)/shard_map/ppermute | solution.py:397
  5.1 6.8 %collective-permute-start = (bf16[2,8,2048]{2,1,0:T(8,128)(2,1)S(1)}, bf16[2,8,2048]{2,1,0:T(8,128)(2,1)S(1)}, u32[]{:S(2)}, u32[]{:S(2)}) collective-permute-start(bf16[2,8,2048]{2,1,0:T(8,128)(2,1)S(1)} %get-tuple-element.18), channel_id=1, source_target_pairs={{0,1},{1,0},{2,3},{3,2},{4,5},{5,4},{6,7},{7,6},{8,9},{9,8},{10,11... | collective-permute-start | bytes 196616 | tf_op jit(solution)/shard_map/ppermute | solution.py:397
  7.5 5.6 %collective-permute-start.3 = (bf16[2,8,2048]{2,1,0:T(8,128)(2,1)S(1)}, bf16[2,8,2048]{2,1,0:T(8,128)(2,1)S(1)}, u32[]{:S(2)}, u32[]{:S(2)}) collective-permute-start(bf16[2,8,2048]{2,1,0:T(8,128)(2,1)S(1)} %add.7.args_1_), channel_id=1, source_target_pairs={{0,2},{1,3},{2,0},{3,1},{4,6},{5,7},{6,4},{7,5},{8,10},{9,11},{10,... | collective-permute-start | bytes 196616 | tf_op jit(solution)/shard_map/ppermute | solution.py:397
  10.9 2.2 %copy-start = (bf16[2,2,128,2048]{3,2,1,0:T(8,128)(2,1)S(1)}, bf16[2,2,128,2048]{3,2,1,0:T(8,128)(2,1)}, u32[]{:S(2)}) copy-start(bf16[2,2,128,2048]{3,2,1,0:T(8,128)(2,1)} %args_0_.6) | copy-start | bytes 6291460
  12.0 5.2 %collective-permute-start.1 = (bf16[2,8,2048]{2,1,0:T(8,128)(2,1)S(1)}, bf16[2,8,2048]{2,1,0:T(8,128)(2,1)S(1)}, u32[]{:S(2)}, u32[]{:S(2)}) collective-permute-start(bf16[2,8,2048]{2,1,0:T(8,128)(2,1)S(1)} %add.6.args_1_), channel_id=1, source_target_pairs={{0,2},{1,3},{2,0},{3,1},{4,6},{5,7},{6,4},{7,5},{8,10},{9,11},{10,... | collective-permute-start | bytes 196616 | tf_op jit(solution)/shard_map/ppermute | solution.py:397
  20.2 6.2 %collective-permute-start.10 = (s16[272,128]{1,0:T(8,128)(2,1)S(1)}, s16[272,128]{1,0:T(8,128)(2,1)S(1)}, u32[]{:S(2)}, u32[]{:S(2)}) collective-permute-start(s16[272,128]{1,0:T(8,128)(2,1)S(1)} %get-tuple-element.30), channel_id=1, source_target_pairs={{0,28},{4,24},{8,20},{12,16},{16,12},{20,8},{24,4},{28,0},{1,29},{... | collective-permute-start | bytes 208904 | tf_op jit(solution)/shard_map/ppermute | solution.py:423
  21.1 7.0 %collective-permute-start.4 = (s16[272,128]{1,0:T(8,128)(2,1)S(1)}, s16[272,128]{1,0:T(8,128)(2,1)S(1)}, u32[]{:S(2)}, u32[]{:S(2)}) collective-permute-start(s16[272,128]{1,0:T(8,128)(2,1)S(1)} %get-tuple-element.24), channel_id=1, source_target_pairs={{0,8},{4,12},{8,0},{12,4},{16,24},{20,28},{24,16},{28,20},{1,9},{5... | collective-permute-start | bytes 208904 | tf_op jit(solution)/shard_map/ppermute | solution.py:423
  24.6 7.6 %collective-permute-start.5 = (s16[272,128]{1,0:T(8,128)(2,1)S(1)}, s16[272,128]{1,0:T(8,128)(2,1)S(1)}, u32[]{:S(2)}, u32[]{:S(2)}) collective-permute-start(s16[272,128]{1,0:T(8,128)(2,1)S(1)} %get-tuple-element.25), channel_id=1, source_target_pairs={{0,16},{4,20},{8,24},{12,28},{16,0},{20,4},{24,8},{28,12},{1,17},{... | collective-permute-start | bytes 208904 | tf_op jit(solution)/shard_map/ppermute | solution.py:423
  25.1 7.1 %collective-permute-start.6 = (s16[272,128]{1,0:T(8,128)(2,1)S(1)}, s16[272,128]{1,0:T(8,128)(2,1)S(1)}, u32[]{:S(2)}, u32[]{:S(2)}) collective-permute-start(s16[272,128]{1,0:T(8,128)(2,1)S(1)} %get-tuple-element.26), channel_id=1, source_target_pairs={{0,24},{4,28},{8,16},{12,20},{16,8},{20,12},{24,0},{28,4},{1,25},{... | collective-permute-start | bytes 208904 | tf_op jit(solution)/shard_map/ppermute | solution.py:423
  25.9 6.3 %collective-permute-start.7 = (s16[272,128]{1,0:T(8,128)(2,1)S(1)}, s16[272,128]{1,0:T(8,128)(2,1)S(1)}, u32[]{:S(2)}, u32[]{:S(2)}) collective-permute-start(s16[272,128]{1,0:T(8,128)(2,1)S(1)} %get-tuple-element.27), channel_id=1, source_target_pairs={{0,4},{4,0},{8,12},{12,8},{16,20},{20,16},{24,28},{28,24},{1,5},{5... | collective-permute-start | bytes 208904 | tf_op jit(solution)/shard_map/ppermute | solution.py:423
  26.4 7.2 %collective-permute-start.8 = (s16[272,128]{1,0:T(8,128)(2,1)S(1)}, s16[272,128]{1,0:T(8,128)(2,1)S(1)}, u32[]{:S(2)}, u32[]{:S(2)}) collective-permute-start(s16[272,128]{1,0:T(8,128)(2,1)S(1)} %get-tuple-element.28), channel_id=1, source_target_pairs={{0,12},{4,8},{8,4},{12,0},{16,28},{20,24},{24,20},{28,16},{1,13},{... | collective-permute-start | bytes 208904 | tf_op jit(solution)/shard_map/ppermute | solution.py:423
  28.1 5.5 %collective-permute-start.9 = (s16[272,128]{1,0:T(8,128)(2,1)S(1)}, s16[272,128]{1,0:T(8,128)(2,1)S(1)}, u32[]{:S(2)}, u32[]{:S(2)}) collective-permute-start(s16[272,128]{1,0:T(8,128)(2,1)S(1)} %get-tuple-element.29), channel_id=1, source_target_pairs={{0,20},{4,16},{8,28},{12,24},{16,4},{20,0},{24,12},{28,8},{1,21},{... | collective-permute-start | bytes 208904 | tf_op jit(solution)/shard_map/ppermute | solution.py:423

commit v4 on v1

--- a/solution.py
+++ b/solution.py
@@ -16,6 +16,8 @@
 ROWS = (((1,), (1,)), ((), ()))
 GROUP = 16
 STEP = 512
+LEVELS = 64.0
+MOST = 32500.0
 
 
 def zernike_rows():
@@ -64,40 +66,71 @@
     return np.concatenate([np.cos(angles), -np.sin(angles)], axis=1).astype(np.float32)
 
 
-def pick_kernel(index_ref, volt_ref, out_ref, rows_ref):
+def owner_and_slot(index_ref, stations):
+    owners = [index_ref[r] // stations for r in range(index_ref.shape[0])]
+    slots = []
+    for r, owner in enumerate(owners):
+        slot = jnp.int32(0)
+        for other in owners[:r]:
+            slot = slot + jnp.where(other == owner, 1, 0)
+        slots.append(slot)
+    return owners, slots
+
+
+def pick_kernel(index_hbm, volt_hbm, *rest):
+    *out_refs, index_ref, volt_ref, rows_ref, index_sem, volt_sem = rest
     chans, parts, stations, _ = volt_ref.shape
-    refs = out_ref.shape[2]
-    first = lax.axis_index("stat") * stations
+    count = rows_ref.shape[2] // parts
+    index_copy = pltpu.make_async_copy(index_hbm, index_ref, index_sem)
+    volt_copy = pltpu.make_async_copy(volt_hbm, volt_ref, volt_sem)
+    index_copy.start()
+    volt_copy.start()
     rows_ref[...] = jnp.zeros_like(rows_ref)
-    for r in range(refs):
-        local = index_ref[r] - first
-
-        @pl.when(jnp.logical_and(local >= 0, local < stations))
+    me = lax.axis_index("stat")
+    index_copy.wait()
+    owners, slots = owner_and_slot(index_ref, stations)
+    volt_copy.wait()
+    for r, (owner, slot) in enumerate(zip(owners, slots)):
+
+        @pl.when(owner == me)
         def _():
+            local = index_ref[r] - me * stations
             begin = pl.multiple_of(local // GROUP * GROUP, GROUP)
             for c in range(chans):
                 for k in range(parts):
                     group = volt_ref[c, k, pl.ds(begin, GROUP), :].astype(jnp.float32)
                     row = lax.broadcasted_iota(jnp.int32, group.shape, 0)
                     group = jnp.where(row == local - begin, group, 0.0)
-                    rows_ref[c, k, r : r + 1, :] = jnp.sum(group, axis=0, keepdims=True)
-
-    out_ref[...] = rows_ref[...].astype(jnp.bfloat16)
+                    to = pl.ds(k * count + lax.rem(slot, count), 1)
+                    rows_ref[slot // count, c, to, :] = jnp.sum(group, axis=0, keepdims=True)
+
+    for i, out_ref in enumerate(out_refs):
+        out_ref[...] = rows_ref[i].astype(jnp.bfloat16)
 
 
 def pick(ref_index, voltages):
     chans, parts, _, times = voltages.shape
     refs = ref_index.shape[0]
+    half = (chans, parts * refs // 2, times)
     vmem = pl.BlockSpec(memory_space=pltpu.VMEM)
     return pl.pallas_call(
         pick_kernel,
-        in_specs=[pl.BlockSpec(memory_space=pltpu.SMEM), vmem],
-        out_specs=vmem,
-        out_shape=jax.ShapeDtypeStruct((chans, parts, refs, times), jnp.bfloat16),
-        scratch_shapes=[pltpu.VMEM((chans, parts, refs, times), jnp.float32)],
+        in_specs=[pl.BlockSpec(memory_space=pltpu.HBM)] * 2,
+        out_specs=[vmem] * 2,
+        out_shape=[jax.ShapeDtypeStruct(half, jnp.bfloat16)] * 2,
+        scratch_shapes=[
+            pltpu.SMEM((refs,), jnp.int32),
+            pltpu.VMEM(voltages.shape, jnp.bfloat16),
+            pltpu.VMEM((2,) + half, jnp.float32),
+            pltpu.SemaphoreType.DMA,
+            pltpu.SemaphoreType.DMA,
+        ],
         compiler_params=pltpu.CompilerParams(vmem_limit_bytes=8 * 2**20),
         name="pick_references",
-    )(ref_index, voltages)
+    )(
+        pltpu.with_memory_space_constraint(ref_index, pltpu.HBM),
+        pltpu.with_memory_space_constraint(voltages, pltpu.HBM),
+    )
 
 
 def invert(gram):
@@ -105,11 +138,35 @@
     row = lax.broadcasted_iota(jnp.int32, (size, size), 0)
     lane = lax.broadcasted_iota(jnp.int32, (size, size), 1)
     work = jnp.concatenate([gram, jnp.where(row == lane, 1.0, 0.0)], axis=1)
-    row = lax.broadcasted_iota(jnp.int32, work.shape, 0)
-    for k in range(size):
-        pivot = work[k : k + 1, :] / work[k : k + 1, k : k + 1]
-        work = jnp.where(row == k, pivot, work - work[:, k : k + 1] * pivot)
-    return work[:, size:]
+    shape = (8, 2 * size)
+    tiles = [work[t : t + 8] for t in range(0, size, 8)]
+    row = lax.broadcasted_iota(jnp.int32, shape, 0)
+    for k in range(0, size, 4):
+        home, begin = divmod(k, 8)
+        r = [jnp.broadcast_to(tiles[home][begin + i : begin + i + 1], shape) for i in range(4)]
+        p = {
+            (i, j): jnp.broadcast_to(r[i][:, k + j : k + j + 1], shape) for i in range(4) for j in range(i, 4)
+        }
+        columns = [[jnp.broadcast_to(x[:, k + j : k + j + 1], shape) for j in range(4)] for x in tiles]
+        scale = 1.0 / (p[0, 0] * p[1, 1] - p[0, 1] * p[0, 1])
+        a00, a01, a11 = p[1, 1] * scale, -p[0, 1] * scale, p[0, 0] * scale
+        f00, f01 = a00 * p[0, 2] + a01 * p[1, 2], a00 * p[0, 3] + a01 * p[1, 3]
+        f10, f11 = a01 * p[0, 2] + a11 * p[1, 2], a01 * p[0, 3] + a11 * p[1, 3]
+        s00 = p[2, 2] - p[0, 2] * f00 - p[1, 2] * f10
+        s01 = p[2, 3] - p[0, 2] * f01 - p[1, 2] * f11
+        s11 = p[3, 3] - p[0, 3] * f01 - p[1, 3] * f11
+        scale = 1.0 / (s00 * s11 - s01 * s01)
+        x0, x1 = a00 * r[0] + a01 * r[1], a01 * r[0] + a11 * r[1]
+        y0, y1 = r[2] - p[0, 2] * x0 - p[1, 2] * x1, r[3] - p[0, 3] * x0 - p[1, 3] * x1
+        n2, n3 = (s11 * y0 - s01 * y1) * scale, (s00 * y1 - s01 * y0) * scale
+        new = [x0 - f00 * n2 - f01 * n3, x1 - f10 * n2 - f11 * n3, n2, n3]
+        for t, c in enumerate(columns):
+            tile = tiles[t] - (c[0] * new[0] + c[1] * new[1]) - (c[2] * new[2] + c[3] * new[3])
+            if t == home:
+                for i in range(4):
+                    tile = jnp.where(row == begin + i, new[i], tile)
+            tiles[t] = tile
+    return jnp.concatenate(tiles, axis=0)[:, size:]
 
 
 def split(value, parts):
@@ -169,17 +226,31 @@
     )(weight.reshape(1, CELLS), jnp.asarray(zernike_rows()))
 
 
-def correlate_kernel(owners, volt_ref, *rest):
-    table_ref, *out_refs, refs_ref, left_a, left_b, total_ref = rest[-(5 + (len(owners) if owners else 1)) :]
-    ref_parts = rest[: len(rest) - (5 + len(out_refs))]
+def correlate_kernel(owners, stat_count, index_ref, volt_ref, *args):
+    part_refs, args = args[:stat_count], args[stat_count:]
+    extra_ref, table_ref, *out_refs = args[:-7]
+    refs_ref, left_a, left_b, total_ref, stage_ref, more_ref, more_sem = args[-7:]
     chans, parts, stations, times = volt_ref.shape
-    refs = refs_ref.shape[2]
+    refs = index_ref.shape[0]
+    count = refs // 2
     steps = times // STEP
-    picked = ref_parts[0][...]
-    for other in ref_parts[1:]:
-        picked = picked + other[...]
-    refs_ref[...] = picked.astype(jnp.float32)
-    own = stations // len(out_refs)
+    me = lax.axis_index("stat")
+    places, more = [], jnp.int32(0)
+    for owner, slot in zip(*owner_and_slot(index_ref, stations)):
+        places.append(((slot // count) * stat_count + lax.rem(me - owner + stat_count, stat_count), lax.rem(slot, count)))
+        more = more + slot // count
+    for i, part_ref in enumerate(part_refs):
+        refs_ref[i] = part_ref[...].astype(jnp.float32)
+
+    @pl.when(more > 0)
+    def _():
+        copy = pltpu.make_async_copy(extra_ref, more_ref, more_sem)
+        copy.start()
+        copy.wait()
+        for i in range(stat_count):
+            refs_ref[stat_count + i] = more_ref[i].astype(jnp.float32)
+
+    own = stations // (len(owners) if owners else 1)
     begins = [0]
     if owners:
         tm, chan_at, chan_count = lax.axis_index("tm"), lax.axis_index("chan"), lax.axis_size("chan")
@@ -192,9 +263,9 @@
 
     def produce(chan, step, left_ref):
         span = pl.ds(step * STEP, STEP)
-        for r in range(refs):
-            real = refs_ref[chan, 0, r : r + 1, span]
-            imag = refs_ref[chan, 1, r : r + 1, span]
+        for r, (place, row) in enumerate(places):
+            real = refs_ref[place, chan, pl.ds(row, 1), span]
+            imag = refs_ref[place, chan, pl.ds(count + row, 1), span]
             for half in range(0, ZERN, 16):
                 table_r = table_ref[half : half + 16, span]
                 table_i = table_ref[ZERN + half : ZERN + half + 16, span]
@@ -220,14 +291,31 @@
             total_ref[...] += product
 
     def finish(chan):
+        kept = lax.broadcasted_iota(jnp.int32, (1, stations), 1) < own
+        levels = []
         for r in range(refs):
             top = total_ref[r * 2 * ZERN : r * 2 * ZERN + ZERN, :]
             low = total_ref[r * 2 * ZERN + ZERN : (r + 1) * 2 * ZERN, :]
             real = top[:, :stations] - low[:, stations:]
             imag = top[:, stations:] + low[:, :stations]
-            both = jnp.concatenate([real, imag], axis=0).T
-            for i, out_ref in enumerate(out_refs):
-                out_ref[chan, pl.ds(r, own, stride=refs), :] = both[i * own : (i + 1) * own]
+            both = jnp.concatenate([real, imag], axis=0)
+            if owners:
+                most = jnp.maximum(jnp.max(jnp.abs(both), axis=0, keepdims=True), 1e-30)
+                level = jnp.floor(jnp.log2(most) * LEVELS) + 1.0
+                levels.append(level)
+                rounded = jnp.floor(both * (jnp.exp2(level * (-1.0 / LEVELS)) * MOST) + 0.5)
+                both = jnp.where(kept, both, rounded)
+            stage_ref[pl.ds(r, stations, stride=refs), :] = both.T
+        if not owners:
+            out_refs[0][chan] = stage_ref[...]
+            return
+        rows = own * refs
+        out_refs[0][chan] = stage_ref[:rows, :]
+        level = jnp.concatenate(levels, axis=0).astype(jnp.int32).astype(jnp.int16)
+        for i, out_ref in enumerate(out_refs[1:]):
+            block = stage_ref[(i + 1) * rows : (i + 2) * rows, :]
+            out_ref[chan * rows : (chan + 1) * rows, :] = block.astype(jnp.int32).astype(jnp.int16)
+            out_ref[chans * rows + chan * refs : chans * rows + (chan + 1) * refs, :] = level
 
     order = [(chan, step) for chan in range(chans) for step in range(steps)]
     buffers = (left_a, left_b)
@@ -240,54 +328,77 @@
             finish(chan)
 
 
-def correlate(voltages, ref_parts, table, owners):
+def correlate(ref_index, voltages, ref_parts, extra, table, owners):
     chans, parts, stations, times = voltages.shape
-    refs = ref_parts[0].shape[2]
+    refs = ref_index.shape[0]
     vmem = pl.BlockSpec(memory_space=pltpu.VMEM)
-    blocks = len(owners) if owners else 1
-    return pl.pallas_call(
-        functools.partial(correlate_kernel, owners),
-        in_specs=[vmem] * (2 + len(ref_parts)),
-        out_specs=[vmem] * blocks,
-        out_shape=[jax.ShapeDtypeStruct((chans, stations // blocks * refs, 2 * ZERN), jnp.float32)] * blocks,
+    rows = stations // (len(owners) if owners else 1) * refs
+    shapes = [jax.ShapeDtypeStruct((chans, rows, 2 * ZERN), jnp.float32)]
+    if owners:
+        shapes += [jax.ShapeDtypeStruct((chans * (rows + refs), 2 * ZERN), jnp.int16)] * (len(owners) - 1)
+    return pl.pallas_call(
+        functools.partial(correlate_kernel, owners, len(ref_parts)),
+        in_specs=[pl.BlockSpec(memory_space=pltpu.SMEM)]
+        + [vmem] * (1 + len(ref_parts))
+        + [pl.BlockSpec(memory_space=pltpu.HBM), vmem],
+        out_specs=[vmem] * len(shapes),
+        out_shape=shapes,
         scratch_shapes=[
-            pltpu.VMEM((chans, parts, refs, times), jnp.float32),
+            pltpu.VMEM((2 * len(ref_parts),) + ref_parts[0].shape, jnp.float32),
             pltpu.VMEM((refs * 2 * ZERN, 2 * STEP), jnp.bfloat16),
             pltpu.VMEM((refs * 2 * ZERN, 2 * STEP), jnp.bfloat16),
             pltpu.VMEM((refs * 2 * ZERN, parts * stations), jnp.float32),
+            pltpu.VMEM((stations * refs, 2 * ZERN), jnp.float32),
+            pltpu.VMEM(extra.shape, extra.dtype),
+            pltpu.SemaphoreType.DMA,
         ],
         compiler_params=pltpu.CompilerParams(vmem_limit_bytes=24 * 2**20),
         cost_estimate=pl.CostEstimate(flops=8_600_000_000, bytes_accessed=5_000_000, transcendentals=0),
         name="correlate",
-    )(voltages, *ref_parts, table)
-
-
-def collect_kernel(*refs):
+    )(ref_index, voltages, *ref_parts, pltpu.with_memory_space_constraint(extra, pltpu.HBM), table)
+
+
+def unwritten(shape, dtype):
+    return pl.pallas_call(
+        lambda out_ref: None,
+        out_specs=pl.BlockSpec(memory_space=pltpu.HBM),
+        out_shape=jax.ShapeDtypeStruct(shape, dtype),
+        name="no_second_round",
+    )()
+
+
+def collect_kernel(order, shape, *refs):
     *ins, inverse_ref, out_ref = refs
+    ins = [ins[list(order).index(at)] for at in range(len(ins))]
     chan = lax.axis_index("chan")
     chan_count = lax.axis_size("chan")
     tm_count = len(ins) // chan_count
-    chans, stations, rows, terms = ins[0].shape
+    chans, own, rows, terms = shape
     for dc in range(chan_count):
-        total = ins[dc][...]
-        for dt in range(1, tm_count):
-            total = total + ins[dt * chan_count + dc][...]
-        solved = jnp.dot(
-            total.reshape(chans * stations * rows, terms),
-            inverse_ref[...],
-            precision=HIGHEST,
-            preferred_element_type=jnp.float32,
-        ).reshape(total.shape)
         source = jnp.bitwise_xor(chan, dc)
         for c in range(chans):
-            out_ref[:, source * chans + c] = solved[c]
-
-
-def collect(pieces, inverse, chan_count):
-    chans, stations, refs, terms = pieces[0].shape
+            total = None
+            for at in range(dc, len(ins), chan_count):
+                if ins[at].dtype == jnp.int16:
+                    begin = c * own * rows
+                    level = ins[at][chans * own * rows :, :].astype(jnp.int32).astype(jnp.float32)
+                    step = jnp.exp2(level[c * rows : (c + 1) * rows] * (1.0 / LEVELS)) * (1.0 / MOST)
+                    part = ins[at][begin : begin + own * rows, :].astype(jnp.int32).astype(jnp.float32)
+                    steps = [step[:, at * own + s : at * own + s + 1] for s in range(own)]
+                    steps = [jnp.broadcast_to(x, (rows, terms)) for x in steps]
+                    part = part * jnp.concatenate(steps, axis=0)
+                else:
+                    part = ins[at][c].reshape(own * rows, terms)
+                total = part if total is None else total + part
+            solved = jnp.dot(total, inverse_ref[...], precision=HIGHEST, preferred_element_type=jnp.float32)
+            out_ref[:, source * chans + c] = solved.reshape(own, rows, terms)
+
+
+def collect(pieces, order, inverse, chan_count, shape):
+    chans, stations, refs, terms = shape
     vmem = pl.BlockSpec(memory_space=pltpu.VMEM)
     return pl.pallas_call(
-        collect_kernel,
+        functools.partial(collect_kernel, order, shape),
         in_specs=[vmem] * (len(pieces) + 1),
         out_specs=vmem,
         out_shape=jax.ShapeDtypeStruct((stations, chans * chan_count, refs, terms), jnp.float32),
@@ -302,30 +413,44 @@
     stat_count = lax.axis_size("stat")
     tm_count = lax.axis_size("tm")
     chan_count = lax.axis_size("chan")
-    picked = pick(ref_index, voltages)
-    ref_parts = [picked]
-    for shift in range(1, stat_count):
-        ref_parts.append(
-            lax.ppermute(picked, "stat", [(i, (i + shift) % stat_count) for i in range(stat_count)])
-        )
+    first, second = pick(ref_index, voltages)
+
+    def to_all(own):
+        shifts = [[(i, (i + k) % stat_count) for i in range(stat_count)] for k in range(1, stat_count)]
+        return [own] + [lax.ppermute(own, "stat", pairs) for pairs in shifts]
+
+    ref_parts = to_all(first)
+    holders = ref_index // stations
+    most = jnp.max(jnp.sum(holders[:, None] == jnp.arange(stat_count)[None, :], axis=0))
+    second, *ref_parts = lax.optimization_barrier((second, *ref_parts))
+    extra = lax.cond(
+        most > refs // 2,
+        lambda own: jnp.stack(to_all(own)),
+        lambda own: unwritten((stat_count,) + own.shape, own.dtype),
+        second,
+    )
     scale = (tm_count * times / CELLS) ** (-0.5)
     table = tables(aperture_weight, positions, scale)
     inverse = gram_inverse(aperture_weight)
     owners = [(dt, dc) for dt in range(tm_count) for dc in range(chan_count)]
+    order = [0, 4, 5, 2, 3, 1, 6, 7] if len(owners) == 8 else range(len(owners))
     own = stations // len(owners)
     block = (chans, own, refs, 2 * ZERN)
     if own % GROUP == 0:
-        sums = [x.reshape(block) for x in correlate(voltages, ref_parts, table, owners)]
+        sums = correlate(ref_index, voltages, ref_parts, extra, table, owners)
     else:
-        whole = correlate(voltages, ref_parts, table, None)[0].reshape((chans, len(owners)) + block[1:])
+        whole = correlate(ref_index, voltages, ref_parts, extra, table, None)[0]
+        whole = whole.reshape((chans, len(owners)) + block[1:])
         tm, chan = lax.axis_index("tm"), lax.axis_index("chan")
         sums = [
             lax.dynamic_index_in_dim(whole, (tm ^ dt) * chan_count + (chan ^ dc), 1, keepdims=False)
             for dt, dc in owners
         ]
     pieces = []
-    for (dt, dc), x in zip(owners, sums):
-        if dt or dc:
+    for at in order:
+        x = sums[at]
+        if at:
+            dt, dc = owners[at]
             pairs = [
                 (c * tm_count + t, (c ^ dc) * tm_count + (t ^ dt))
                 for c in range(chan_count)
@@ -333,7 +458,7 @@
             ]
             x = lax.ppermute(x, ("chan", "tm"), pairs)
         pieces.append(x)
-    return collect(pieces, inverse, chan_count)
+    return collect(pieces, order, inverse, chan_count, block)
 
 
 def solution(mesh):

time: 40.6 us -> 30.1 us (0.74)
  the two profiles are of different devices: /device:TPU:15 before, /device:TPU:0 now
where the time goes in v4:
time: 30.1 us; the launch traced here: 30 us
  Pallas kernels  13.5 us (45%)
  starting transfers between devices  13.2 us (44%)
  waiting for transfers between devices  1.87 us (6%)
  between operations  0.77 us (3%)
  other arithmetic  0.76 us (3%)
    ppermute x3, starting transfers between devices, to_all(): return [own] + [lax.ppermute(own, 'stat', pairs) for pairs in shifts]  6.77 us
    ppermute x7, starting transfers between devices, on_device(): x = lax.ppermute(x, ('chan', 'tm'), pairs)  6.39 us
    pallas_call x1, Pallas kernels, correlate(): pl.pallas_call(functools.partial(correlate_kernel, owners, len(ref_parts)...  5.76 us
    pallas_call x1, Pallas kernels, gram_inverse(): pl.pallas_call(inverse_kernel, out_shape=jax.ShapeDtypeStruct((2 * ZERN,...  3.08 us
    pallas_call x1, Pallas kernels, pick(): pl.pallas_call(pick_kernel, in_specs=[pl.BlockSpec(memory_space=pltpu.HBM...  2.07 us
    pallas_call x1, Pallas kernels, collect(): pl.pallas_call(functools.partial(collect_kernel, order, shape), in_specs=...  1.53 us
    ppermute x3, waiting for transfers between devices, to_all(): return [own] + [lax.ppermute(own, 'stat', pairs) for pairs in shifts]  1.12 us
    pallas_call x1, Pallas kernels, tables(): pl.pallas_call(functools.partial(tables_kernel, scale), out_shape=jax.Sha...  1 us
  transfers between devices with their start and end apart: 10, of which 4 were waited for; matrix products, arithmetic and copies ran while one was open for 3% of the time, Pallas kernels for 14%

profile of v4, /device:TPU:0, one launch (start us, length us, event | category | flops | bytes accessed | tf_op | source)
XLA Modules:
  0.0 30.0 jit_solution(12513617412614650766)
XLA Ops:
  0.0 0.0 copy-start.5
  0.0 0.0 copy-start.4
  0.0 0.0 copy-start.1
  0.0 0.0 copy-start.3
  0.0 0.0 copy-start.2
  0.0 2.1 %pick_references.1 = (bf16[2,8,2048]{2,1,0:T(8,128)(2,1)S(1)}, bf16[2,8,2048]{2,1,0:T(8,128)(2,1)S(1)}) custom-call(s32[8]{0:T(128)} %index_ref.1, bf16[2,2,128,2048]{3,2,1,0:T(8,128)(2,1)} %volt_ref.1), custom_call_target="tpu_custom_call" | custom-call | tf_op jit(solution)/shard_map/pick_references/pallas_call | solution.py:116
  2.1 3.0 %collective-permute-start.3 = (bf16[2,8,2048]{2,1,0:T(8,128)(2,1)S(1)}, bf16[2,8,2048]{2,1,0:T(8,128)(2,1)S(1)}, u32[]{:S(2)}, u32[]{:S(2)}) collective-permute-start(bf16[2,8,2048]{2,1,0:T(8,128)(2,1)S(1)} %get-tuple-element.26.args_0_), channel_id=1, source_target_pairs={{0,1},{1,2},{2,3},{3,0},{4,5},{5,6},{6,7},{7,4},{8,9},{9,10},{10,1... | collective-permute-start | bytes 196616 | tf_op jit(solution)/shard_map/ppermute | solution.py:420
  5.1 2.6 %collective-permute-start.4 = (bf16[2,8,2048]{2,1,0:T(8,128)(2,1)S(1)}, bf16[2,8,2048]{2,1,0:T(8,128)(2,1)S(1)}, u32[]{:S(2)}, u32[]{:S(2)}) collective-permute-start(bf16[2,8,2048]{2,1,0:T(8,128)(2,1)S(1)} %get-tuple-element.26.args_0_), channel_id=1, source_target_pairs={{0,2},{1,3},{2,0},{3,1},{4,6},{5,7},{6,4},{7,5},{8,10},{9,11},{10,... | collective-permute-start | bytes 196616 | tf_op jit(solution)/shard_map/ppermute | solution.py:420
  7.7 1.2 %collective-permute-start.5 = (bf16[2,8,2048]{2,1,0:T(8,128)(2,1)S(1)}, bf16[2,8,2048]{2,1,0:T(8,128)(2,1)S(1)}, u32[]{:S(2)}, u32[]{:S(2)}) collective-permute-start(bf16[2,8,2048]{2,1,0:T(8,128)(2,1)S(1)} %get-tuple-element.26.args_0_), channel_id=1, source_target_pairs={{0,3},{1,0},{2,1},{3,2},{4,7},{5,4},{6,5},{7,6},{8,11},{9,8},{10,9... | collective-permute-start | bytes 196616 | tf_op jit(solution)/shard_map/ppermute | solution.py:420
  8.9 0.0 copy-done.1
  8.9 0.0 copy-done.5
  8.9 0.0 copy-done.4
  8.9 0.0 copy-done.3
  8.9 0.0 copy-done.2
  8.9 0.0 copy-start
  8.9 1.0 %projection_per_sample.1.args_5_ = f32[128,2048]{1,0:T(8,128)S(1)} custom-call(f32[1,256]{1,0:T(1,128)S(1)} %bitcast.7, f32[64,256]{1,0:T(8,128)S(1)} %copy-done.5, f32[256,512]{1,0:T(8,128)S(1)} %copy-done.4, s32[1,2048]{1,0:T(1,128)S(1)} %bitcast.6), custom_call_target="tpu_custom_call" | custom-call | flops 4000000000 | bytes 2000000 | tf_op jit(solution)/shard_map/projection_per_sample/pallas_call | solution.py:198
  9.9 0.1 convert_reduce_fusion
  10.0 0.6 %reduce_max.9 = s32[]{:T(128)} reduce(s32[4]{0:T(128)S(1)} %convert_reduce_fusion, s32[]{:T(128)} %constant.23.clone.1), dimensions={0}, to_apply=%region_1.2 | reduce | flops 3 | bytes 24 | tf_op jit(solution)/shard_map/reduce_max | solution.py:424
  11.3 0.0 collective-permute-done.3.args_1_
  11.3 0.8 %collective-permute-done.4.args_2_ = bf16[2,8,2048]{2,1,0:T(8,128)(2,1)S(1)} collective-permute-done((bf16[2,8,2048]{2,1,0:T(8,128)(2,1)S(1)}, bf16[2,8,2048]{2,1,0:T(8,128)(2,1)S(1)}, u32[]{:S(2)}, u32[]{:S(2)}) %collective-permute-start.4) | collective-permute-done | bytes 65568 | tf_op jit(solution)/shard_map/ppermute | solution.py:420
  12.1 0.3 %collective-permute-done.5.args_3_ = bf16[2,8,2048]{2,1,0:T(8,128)(2,1)S(1)} collective-permute-done((bf16[2,8,2048]{2,1,0:T(8,128)(2,1)S(1)}, bf16[2,8,2048]{2,1,0:T(8,128)(2,1)S(1)}, u32[]{:S(2)}, u32[]{:S(2)}) %collective-permute-start.5) | collective-permute-done | bytes 65568 | tf_op jit(solution)/shard_map/ppermute | solution.py:420
  12.5 0.0 copy-done
  12.5 5.8 %correlate.1 = (f32[2,128,128]{2,1,0:T(8,128)S(1)}, s16[272,128]{1,0:T(8,128)(2,1)S(1)}, s16[272,128]{1,0:T(8,128)(2,1)S(1)}, s16[272,128]{1,0:T(8,128)(2,1)S(1)...) custom-call(s32[8]{0:T(128)S(1)} %copy-done.1, ...), custom_call_target="tpu_custom_call" | custom-call | flops 8600000512 | bytes 5000000 | tf_op jit(solution)/shard_map/correlate/pallas_call | solution.py:339
  18.2 0.1 collective-permute-start.10
  18.3 2.6 %collective-permute-start.11 = (s16[272,128]{1,0:T(8,128)(2,1)S(1)}, s16[272,128]{1,0:T(8,128)(2,1)S(1)}, u32[]{:S(2)}, u32[]{:S(2)}) collective-permute-start(s16[272,128]{1,0:T(8,128)(2,1)S(1)} %get-tuple-element.37), channel_id=1, source_target_pairs={{0,20},{4,16},{8,28},{12,24},{16,4},{20,0},{24,12},{28,8},{1,21},{... | collective-permute-start | bytes 208904 | tf_op jit(solution)/shard_map/ppermute | solution.py:459
  20.9 0.2 collective-permute-start.12
  21.1 1.6 %collective-permute-start.6 = (s16[272,128]{1,0:T(8,128)(2,1)S(1)}, s16[272,128]{1,0:T(8,128)(2,1)S(1)}, u32[]{:S(2)}, u32[]{:S(2)}) collective-permute-start(s16[272,128]{1,0:T(8,128)(2,1)S(1)} %get-tuple-element.32), channel_id=1, source_target_pairs={{0,4},{4,0},{8,12},{12,8},{16,20},{20,16},{24,28},{28,24},{1,5},{5... | collective-permute-start | bytes 208904 | tf_op jit(solution)/shard_map/ppermute | solution.py:459
  22.7 0.1 collective-permute-start.7
  22.8 0.0 collective-permute-done.10.refs_5_
  22.8 1.6 %collective-permute-start.8 = (s16[272,128]{1,0:T(8,128)(2,1)S(1)}, s16[272,128]{1,0:T(8,128)(2,1)S(1)}, u32[]{:S(2)}, u32[]{:S(2)}) collective-permute-start(s16[272,128]{1,0:T(8,128)(2,1)S(1)} %get-tuple-element.34), channel_id=1, source_target_pairs={{0,16},{4,20},{8,24},{12,28},{16,0},{20,4},{24,8},{28,12},{1,17},{... | collective-permute-start | bytes 208904 | tf_op jit(solution)/shard_map/ppermute | solution.py:459
  24.4 0.0 collective-permute-done.11.refs_6_
  24.4 0.3 collective-permute-start.9
  24.7 3.1 %gram_inverse.1.refs_8_ = f32[128,128]{1,0:T(8,128)S(1)} custom-call(f32[1,256]{1,0:T(1,128)S(1)} %bitcast.8, f32[64,256]{1,0:T(8,128)S(1)} %copy-done.5), custom_call_target="tpu_custom_call" | custom-call | flops 5000000000 | bytes 200000 | tf_op jit(solution)/shard_map/gram_inverse/pallas_call | solution.py:220
  27.7 0.0 collective-permute-done.12.refs_7_
  27.7 0.0 collective-permute-done.6.refs_1_
  27.8 0.2 collective-permute-done.7.refs_2_
  27.9 0.0 collective-permute-done.8.refs_3_
  27.9 0.6 %collective-permute-done.9.refs_4_ = s16[272,128]{1,0:T(8,128)(2,1)S(1)} collective-permute-done((s16[272,128]{1,0:T(8,128)(2,1)S(1)}, s16[272,128]{1,0:T(8,128)(2,1)S(1)}, u32[]{:S(2)}, u32[]{:S(2)}) %collective-permute-start.9) | collective-permute-done | bytes 69664 | tf_op jit(solution)/shard_map/ppermute | solution.py:459
  28.5 1.5 %sum_and_solve.1 = f32[16,8,8,128]{3,2,1,0:T(8,128)} custom-call(f32[2,128,128]{2,1,0:T(8,128)S(1)} %get-tuple-element.31.refs_0_, s16[272,128]{1,0:T(8,128)(2,1)S(1)} %collective-permute-done.6.refs_1_, s16[272,128]{1,0:T(8,128)(2,1)S(1)} %collective-permute-done.7.refs_2_, s16[272,128]{1,0:T(8,128)(2,1)S(1)} %collective-permute-done.8.refs_3_, ...), custom_call_target="tpu_custom_call" | custom-call | tf_op jit(solution)/shard_map/sum_and_solve/pallas_call | solution.py:400
  (3 shorter events, 0.0 us)
Async XLA Ops:
  0.0 8.9 %copy-start.5 = (f32[64,256]{1,0:T(8,128)S(1)}, f32[64,256]{1,0:T(8,128)}, u32[]{:S(2)}) copy-start(f32[64,256]{1,0:T(8,128)} %constant.25.clone.zern_ref) | copy-start | bytes 196612
  0.0 8.9 %copy-start.4 = (f32[256,512]{1,0:T(8,128)S(1)}, f32[256,512]{1,0:T(8,128)}, u32[]{:S(2)}) copy-start(f32[256,512]{1,0:T(8,128)} %constant.26.clone.dft_ref) | copy-start | bytes 1572868
  0.0 8.9 %copy-start.1 = (s32[8]{0:T(128)S(1)}, s32[8]{0:T(128)}, u32[]{:S(2)}) copy-start(s32[8]{0:T(128)} %index_ref.1) | copy-start | bytes 100
  0.0 8.9 %copy-start.3 = (f32[256]{0:T(256)S(1)}, f32[256]{0:T(256)}, u32[]{:S(2)}) copy-start(f32[256]{0:T(256)} %param.12) | copy-start | bytes 3076
  0.0 8.9 %copy-start.2 = (s32[2048]{0:T(1024)S(1)}, s32[2048]{0:T(1024)}, u32[]{:S(2)}) copy-start(s32[2048]{0:T(1024)} %param.11) | copy-start | bytes 24580
  2.1 9.2 %collective-permute-start.3 = (bf16[2,8,2048]{2,1,0:T(8,128)(2,1)S(1)}, bf16[2,8,2048]{2,1,0:T(8,128)(2,1)S(1)}, u32[]{:S(2)}, u32[]{:S(2)}) collective-permute-start(bf16[2,8,2048]{2,1,0:T(8,128)(2,1)S(1)} %get-tuple-element.26.args_0_), channel_id=1, source_target_pairs={{0,1},{1,2},{2,3},{3,0},{4,5},{5,6},{6,7},{7,4},{8,9},{9,10},{10,1... | collective-permute-start | bytes 196616 | tf_op jit(solution)/shard_map/ppermute | solution.py:420
  5.1 7.1 %collective-permute-start.4 = (bf16[2,8,2048]{2,1,0:T(8,128)(2,1)S(1)}, bf16[2,8,2048]{2,1,0:T(8,128)(2,1)S(1)}, u32[]{:S(2)}, u32[]{:S(2)}) collective-permute-start(bf16[2,8,2048]{2,1,0:T(8,128)(2,1)S(1)} %get-tuple-element.26.args_0_), channel_id=1, source_target_pairs={{0,2},{1,3},{2,0},{3,1},{4,6},{5,7},{6,4},{7,5},{8,10},{9,11},{10,... | collective-permute-start | bytes 196616 | tf_op jit(solution)/shard_map/ppermute | solution.py:420
  7.7 4.8 %collective-permute-start.5 = (bf16[2,8,2048]{2,1,0:T(8,128)(2,1)S(1)}, bf16[2,8,2048]{2,1,0:T(8,128)(2,1)S(1)}, u32[]{:S(2)}, u32[]{:S(2)}) collective-permute-start(bf16[2,8,2048]{2,1,0:T(8,128)(2,1)S(1)} %get-tuple-element.26.args_0_), channel_id=1, source_target_pairs={{0,3},{1,0},{2,1},{3,2},{4,7},{5,4},{6,5},{7,6},{8,11},{9,8},{10,9... | collective-permute-start | bytes 196616 | tf_op jit(solution)/shard_map/ppermute | solution.py:420
  8.9 3.6 %copy-start = (bf16[2,2,128,2048]{3,2,1,0:T(8,128)(2,1)S(1)}, bf16[2,2,128,2048]{3,2,1,0:T(8,128)(2,1)}, u32[]{:S(2)}) copy-start(bf16[2,2,128,2048]{3,2,1,0:T(8,128)(2,1)} %volt_ref.1) | copy-start | bytes 6291460
  18.2 4.5 %collective-permute-start.10 = (s16[272,128]{1,0:T(8,128)(2,1)S(1)}, s16[272,128]{1,0:T(8,128)(2,1)S(1)}, u32[]{:S(2)}, u32[]{:S(2)}) collective-permute-start(s16[272,128]{1,0:T(8,128)(2,1)S(1)} %get-tuple-element.36), channel_id=1, source_target_pairs={{0,8},{4,12},{8,0},{12,4},{16,24},{20,28},{24,16},{28,20},{1,9},{5... | collective-permute-start | bytes 208904 | tf_op jit(solution)/shard_map/ppermute | solution.py:459
  18.3 6.0 %collective-permute-start.11 = (s16[272,128]{1,0:T(8,128)(2,1)S(1)}, s16[272,128]{1,0:T(8,128)(2,1)S(1)}, u32[]{:S(2)}, u32[]{:S(2)}) collective-permute-start(s16[272,128]{1,0:T(8,128)(2,1)S(1)} %get-tuple-element.37), channel_id=1, source_target_pairs={{0,20},{4,16},{8,28},{12,24},{16,4},{20,0},{24,12},{28,8},{1,21},{... | collective-permute-start | bytes 208904 | tf_op jit(solution)/shard_map/ppermute | solution.py:459
  20.9 6.8 %collective-permute-start.12 = (s16[272,128]{1,0:T(8,128)(2,1)S(1)}, s16[272,128]{1,0:T(8,128)(2,1)S(1)}, u32[]{:S(2)}, u32[]{:S(2)}) collective-permute-start(s16[272,128]{1,0:T(8,128)(2,1)S(1)} %get-tuple-element.38), channel_id=1, source_target_pairs={{0,28},{4,24},{8,20},{12,16},{16,12},{20,8},{24,4},{28,0},{1,29},{... | collective-permute-start | bytes 208904 | tf_op jit(solution)/shard_map/ppermute | solution.py:459
  21.1 6.7 %collective-permute-start.6 = (s16[272,128]{1,0:T(8,128)(2,1)S(1)}, s16[272,128]{1,0:T(8,128)(2,1)S(1)}, u32[]{:S(2)}, u32[]{:S(2)}) collective-permute-start(s16[272,128]{1,0:T(8,128)(2,1)S(1)} %get-tuple-element.32), channel_id=1, source_target_pairs={{0,4},{4,0},{8,12},{12,8},{16,20},{20,16},{24,28},{28,24},{1,5},{5... | collective-permute-start | bytes 208904 | tf_op jit(solution)/shard_map/ppermute | solution.py:459
  22.7 5.3 %collective-permute-start.7 = (s16[272,128]{1,0:T(8,128)(2,1)S(1)}, s16[272,128]{1,0:T(8,128)(2,1)S(1)}, u32[]{:S(2)}, u32[]{:S(2)}) collective-permute-start(s16[272,128]{1,0:T(8,128)(2,1)S(1)} %get-tuple-element.33), channel_id=1, source_target_pairs={{0,12},{4,8},{8,4},{12,0},{16,28},{20,24},{24,20},{28,16},{1,13},{... | collective-permute-start | bytes 208904 | tf_op jit(solution)/shard_map/ppermute | solution.py:459
  22.8 5.1 %collective-permute-start.8 = (s16[272,128]{1,0:T(8,128)(2,1)S(1)}, s16[272,128]{1,0:T(8,128)(2,1)S(1)}, u32[]{:S(2)}, u32[]{:S(2)}) collective-permute-start(s16[272,128]{1,0:T(8,128)(2,1)S(1)} %get-tuple-element.34), channel_id=1, source_target_pairs={{0,16},{4,20},{8,24},{12,28},{16,0},{20,4},{24,8},{28,12},{1,17},{... | collective-permute-start | bytes 208904 | tf_op jit(solution)/shard_map/ppermute | solution.py:459
  24.4 4.1 %collective-permute-start.9 = (s16[272,128]{1,0:T(8,128)(2,1)S(1)}, s16[272,128]{1,0:T(8,128)(2,1)S(1)}, u32[]{:S(2)}, u32[]{:S(2)}) collective-permute-start(s16[272,128]{1,0:T(8,128)(2,1)S(1)} %get-tuple-element.35), channel_id=1, source_target_pairs={{0,24},{4,28},{8,16},{12,20},{16,8},{20,12},{24,0},{28,4},{1,25},{... | collective-permute-start | bytes 208904 | tf_op jit(solution)/shard_map/ppermute | solution.py:459

commit v5 on v4

--- a/solution.py
+++ b/solution.py
@@ -226,6 +226,10 @@
     )(weight.reshape(1, CELLS), jnp.asarray(zernike_rows()))
 
 
+def shift_order(stat_count):
+    return [0, 2, 3, 1] if stat_count == 4 else list(range(stat_count))
+
+
 def correlate_kernel(owners, stat_count, index_ref, volt_ref, *args):
     part_refs, args = args[:stat_count], args[stat_count:]
     extra_ref, table_ref, *out_refs = args[:-7]
@@ -237,7 +241,10 @@
     me = lax.axis_index("stat")
     places, more = [], jnp.int32(0)
     for owner, slot in zip(*owner_and_slot(index_ref, stations)):
-        places.append(((slot // count) * stat_count + lax.rem(me - owner + stat_count, stat_count), lax.rem(slot, count)))
+        shift, place = jnp.bitwise_xor(me, owner), jnp.int32(0)
+        for i, k in enumerate(shift_order(stat_count)):
+            place = jnp.where(shift == k, i, place)
+        places.append(((slot // count) * stat_count + place, lax.rem(slot, count)))
         more = more + slot // count
     for i, part_ref in enumerate(part_refs):
         refs_ref[i] = part_ref[...].astype(jnp.float32)
@@ -274,17 +281,16 @@
                     (ZERN + half, real * table_i - imag * table_r),
                 ):
                     high, low = split(value, 2)
-                    rows = pl.ds(r * 2 * ZERN + at, 16)
-                    left_ref[rows, 0:STEP] = high
-                    left_ref[rows, STEP : 2 * STEP] = low
+                    left_ref[pl.ds(r * 2 * ZERN + at, 16), :] = high
+                    left_ref[pl.ds((refs + r) * 2 * ZERN + at, 16), :] = low
 
     def consume(chan, step, left_ref):
         span = pl.ds(step * STEP, STEP)
         right = jnp.concatenate(
             [volt_ref[chan, k, pl.ds(begin, own), span] for k in range(parts) for begin in begins], axis=0
         )
-        right = jnp.concatenate([right, right], axis=1)
         product = lax.dot_general(left_ref[...], right, ROWS, preferred_element_type=jnp.float32)
+        product = product[: refs * 2 * ZERN] + product[refs * 2 * ZERN :]
         if step == 0:
             total_ref[...] = product
         else:
@@ -307,7 +313,7 @@
                 both = jnp.where(kept, both, rounded)
             stage_ref[pl.ds(r, stations, stride=refs), :] = both.T
         if not owners:
-            out_refs[0][chan] = stage_ref[...]
+            out_refs[0][chan] = stage_ref[: stations * refs, :]
             return
         rows = own * refs
         out_refs[0][chan] = stage_ref[:rows, :]
@@ -345,10 +351,10 @@
         out_shape=shapes,
         scratch_shapes=[
             pltpu.VMEM((2 * len(ref_parts),) + ref_parts[0].shape, jnp.float32),
-            pltpu.VMEM((refs * 2 * ZERN, 2 * STEP), jnp.bfloat16),
-            pltpu.VMEM((refs * 2 * ZERN, 2 * STEP), jnp.bfloat16),
+            pltpu.VMEM((2 * refs * 2 * ZERN, STEP), jnp.bfloat16),
+            pltpu.VMEM((2 * refs * 2 * ZERN, STEP), jnp.bfloat16),
             pltpu.VMEM((refs * 2 * ZERN, parts * stations), jnp.float32),
-            pltpu.VMEM((stations * refs, 2 * ZERN), jnp.float32),
+            pltpu.VMEM(((stations + 1) * refs, 2 * ZERN), jnp.float32),
             pltpu.VMEM(extra.shape, extra.dtype),
             pltpu.SemaphoreType.DMA,
         ],
@@ -368,12 +374,13 @@
 
 
 def collect_kernel(order, shape, *refs):
-    *ins, inverse_ref, out_ref = refs
+    *ins, inverse_ref, out_ref, stage_ref, sems = refs
     ins = [ins[list(order).index(at)] for at in range(len(ins))]
     chan = lax.axis_index("chan")
     chan_count = lax.axis_size("chan")
     tm_count = len(ins) // chan_count
     chans, own, rows, terms = shape
+    copies = []
     for dc in range(chan_count):
         source = jnp.bitwise_xor(chan, dc)
         for c in range(chans):
@@ -391,7 +398,12 @@
                     part = ins[at][c].reshape(own * rows, terms)
                 total = part if total is None else total + part
             solved = jnp.dot(total, inverse_ref[...], precision=HIGHEST, preferred_element_type=jnp.float32)
-            out_ref[:, source * chans + c] = solved.reshape(own, rows, terms)
+            stage_ref[dc, :, c] = solved.reshape(own, rows, terms)
+        to = out_ref.at[:, pl.ds(source * chans, chans)]
+        copies.append(pltpu.make_async_copy(stage_ref.at[dc], to, sems.at[dc]))
+        copies[-1].start()
+    for copy in copies:
+        copy.wait()
 
 
 def collect(pieces, order, inverse, chan_count, shape):
@@ -400,8 +412,12 @@
     return pl.pallas_call(
         functools.partial(collect_kernel, order, shape),
         in_specs=[vmem] * (len(pieces) + 1),
-        out_specs=vmem,
+        out_specs=pl.BlockSpec(memory_space=pltpu.HBM),
         out_shape=jax.ShapeDtypeStruct((stations, chans * chan_count, refs, terms), jnp.float32),
+        scratch_shapes=[
+            pltpu.VMEM((chan_count, stations, chans, refs, terms), jnp.float32),
+            pltpu.SemaphoreType.DMA((chan_count,)),
+        ],
         compiler_params=pltpu.CompilerParams(vmem_limit_bytes=8 * 2**20),
         name="sum_and_solve",
     )(*pieces, inverse)
@@ -416,7 +432,7 @@
     first, second = pick(ref_index, voltages)
 
     def to_all(own):
-        shifts = [[(i, (i + k) % stat_count) for i in range(stat_count)] for k in range(1, stat_count)]
+        shifts = [[(i, i ^ k) for i in range(stat_count)] for k in shift_order(stat_count)[1:]]
         return [own] + [lax.ppermute(own, "stat", pairs) for pairs in shifts]
 
     ref_parts = to_all(first)

time: 30.1 us -> 30 us (level)
  starting transfers between devices: 13.2 us -> 11.9 us
  waiting for transfers between devices: 1.87 us -> 3.05 us
    ppermute x3, starting transfers between devices: 6.77 us -> 5.43 us  [to_all(): return [own] + [lax.ppermute(own, 'stat', pairs) for pairs in shifts]]
    ppermute x3, waiting for transfers between devices: 1.12 us -> 2.31 us  [to_all(): return [own] + [lax.ppermute(own, 'stat', pairs) for pairs in shifts]]
where the time goes in v5:
time: 30 us; the launch traced here: 29.9 us
  Pallas kernels  13.4 us (45%)
  starting transfers between devices  11.9 us (40%)
  waiting for transfers between devices  3.05 us (10%)
  between operations  0.77 us (3%)
  other arithmetic  0.76 us (3%)
    ppermute x7, starting transfers between devices, on_device(): x = lax.ppermute(x, ('chan', 'tm'), pairs)  6.46 us
    pallas_call x1, Pallas kernels, correlate(): pl.pallas_call(functools.partial(correlate_kernel, owners, len(ref_parts)...  5.71 us
    ppermute x3, starting transfers between devices, to_all(): return [own] + [lax.ppermute(own, 'stat', pairs) for pairs in shifts]  5.43 us
    pallas_call x1, Pallas kernels, gram_inverse(): pl.pallas_call(inverse_kernel, out_shape=jax.ShapeDtypeStruct((2 * ZERN,...  3.08 us
    ppermute x3, waiting for transfers between devices, to_all(): return [own] + [lax.ppermute(own, 'stat', pairs) for pairs in shifts]  2.31 us
    pallas_call x1, Pallas kernels, pick(): pl.pallas_call(pick_kernel, in_specs=[pl.BlockSpec(memory_space=pltpu.HBM...  2.2 us
    pallas_call x1, Pallas kernels, collect(): pl.pallas_call(functools.partial(collect_kernel, order, shape), in_specs=...  1.43 us
    pallas_call x1, Pallas kernels, tables(): pl.pallas_call(functools.partial(tables_kernel, scale), out_shape=jax.Sha...  0.99 us
  transfers between devices with their start and end apart: 10, of which 4 were waited for; matrix products, arithmetic and copies ran while one was open for 3% of the time, Pallas kernels for 14%

profile of v5, /device:TPU:0, one launch (start us, length us, event | category | flops | bytes accessed | tf_op | source)
XLA Modules:
  0.0 29.9 jit_solution(14054803420004614830)
XLA Ops:
  0.0 0.0 copy-start.5
  0.0 0.0 copy-start.4
  0.0 0.0 copy-start.1
  0.0 0.0 copy-start.3
  0.0 0.0 copy-start.2
  0.0 2.2 %pick_references.1 = (bf16[2,8,2048]{2,1,0:T(8,128)(2,1)S(1)}, bf16[2,8,2048]{2,1,0:T(8,128)(2,1)S(1)}) custom-call(s32[8]{0:T(128)} %index_ref.1, bf16[2,2,128,2048]{3,2,1,0:T(8,128)(2,1)} %volt_ref.1), custom_call_target="tpu_custom_call" | custom-call | tf_op jit(solution)/shard_map/pick_references/pallas_call | solution.py:116
  2.2 3.9 %collective-permute-start.3 = (bf16[2,8,2048]{2,1,0:T(8,128)(2,1)S(1)}, bf16[2,8,2048]{2,1,0:T(8,128)(2,1)S(1)}, u32[]{:S(2)}, u32[]{:S(2)}) collective-permute-start(bf16[2,8,2048]{2,1,0:T(8,128)(2,1)S(1)} %get-tuple-element.26.args_0_), channel_id=1, source_target_pairs={{0,2},{1,3},{2,0},{3,1},{4,6},{5,7},{6,4},{7,5},{8,10},{9,11},{10,... | collective-permute-start | bytes 196616 | tf_op jit(solution)/shard_map/ppermute | solution.py:436
  6.1 1.1 %collective-permute-start.4 = (bf16[2,8,2048]{2,1,0:T(8,128)(2,1)S(1)}, bf16[2,8,2048]{2,1,0:T(8,128)(2,1)S(1)}, u32[]{:S(2)}, u32[]{:S(2)}) collective-permute-start(bf16[2,8,2048]{2,1,0:T(8,128)(2,1)S(1)} %get-tuple-element.26.args_0_), channel_id=1, source_target_pairs={{0,3},{1,2},{2,1},{3,0},{4,7},{5,6},{6,5},{7,4},{8,11},{9,10},{10,... | collective-permute-start | bytes 196616 | tf_op jit(solution)/shard_map/ppermute | solution.py:436
  7.2 0.5 %collective-permute-start.5 = (bf16[2,8,2048]{2,1,0:T(8,128)(2,1)S(1)}, bf16[2,8,2048]{2,1,0:T(8,128)(2,1)S(1)}, u32[]{:S(2)}, u32[]{:S(2)}) collective-permute-start(bf16[2,8,2048]{2,1,0:T(8,128)(2,1)S(1)} %get-tuple-element.26.args_0_), channel_id=1, source_target_pairs={{0,1},{1,0},{2,3},{3,2},{4,5},{5,4},{6,7},{7,6},{8,9},{9,8},{10,11... | collective-permute-start | bytes 196616 | tf_op jit(solution)/shard_map/ppermute | solution.py:436
  7.7 0.0 copy-done.1
  7.7 0.0 copy-done.5
  7.7 0.0 copy-done.4
  7.7 0.0 copy-done.3
  7.7 0.0 copy-done.2
  7.7 0.0 copy-start
  7.7 1.0 %projection_per_sample.1.args_5_ = f32[128,2048]{1,0:T(8,128)S(1)} custom-call(f32[1,256]{1,0:T(1,128)S(1)} %bitcast.7, f32[64,256]{1,0:T(8,128)S(1)} %copy-done.5, f32[256,512]{1,0:T(8,128)S(1)} %copy-done.4, s32[1,2048]{1,0:T(1,128)S(1)} %bitcast.6), custom_call_target="tpu_custom_call" | custom-call | flops 4000000000 | bytes 2000000 | tf_op jit(solution)/shard_map/projection_per_sample/pallas_call | solution.py:198
  8.7 0.1 convert_reduce_fusion
  8.8 0.6 %reduce_max.9 = s32[]{:T(128)} reduce(s32[4]{0:T(128)S(1)} %convert_reduce_fusion, s32[]{:T(128)} %constant.23.clone.1), dimensions={0}, to_apply=%region_1.2 | reduce | flops 3 | bytes 24 | tf_op jit(solution)/shard_map/reduce_max | solution.py:440
  10.1 0.0 collective-permute-done.3.args_1_
  10.1 2.2 %collective-permute-done.4.args_2_ = bf16[2,8,2048]{2,1,0:T(8,128)(2,1)S(1)} collective-permute-done((bf16[2,8,2048]{2,1,0:T(8,128)(2,1)S(1)}, bf16[2,8,2048]{2,1,0:T(8,128)(2,1)S(1)}, u32[]{:S(2)}, u32[]{:S(2)}) %collective-permute-start.4) | collective-permute-done | bytes 65568 | tf_op jit(solution)/shard_map/ppermute | solution.py:436
  12.3 0.1 collective-permute-done.5.args_3_
  12.4 0.0 copy-done
  12.4 5.7 %correlate.1 = (f32[2,128,128]{2,1,0:T(8,128)S(1)}, s16[272,128]{1,0:T(8,128)(2,1)S(1)}, s16[272,128]{1,0:T(8,128)(2,1)S(1)}, s16[272,128]{1,0:T(8,128)(2,1)S(1)...) custom-call(s32[8]{0:T(128)S(1)} %copy-done.1, ...), custom_call_target="tpu_custom_call" | custom-call | flops 8600000512 | bytes 5000000 | tf_op jit(solution)/shard_map/correlate/pallas_call | solution.py:345
  18.2 0.1 collective-permute-start.10
  18.2 2.7 %collective-permute-start.11 = (s16[272,128]{1,0:T(8,128)(2,1)S(1)}, s16[272,128]{1,0:T(8,128)(2,1)S(1)}, u32[]{:S(2)}, u32[]{:S(2)}) collective-permute-start(s16[272,128]{1,0:T(8,128)(2,1)S(1)} %get-tuple-element.37), channel_id=1, source_target_pairs={{0,20},{4,16},{8,28},{12,24},{16,4},{20,0},{24,12},{28,8},{1,21},{... | collective-permute-start | bytes 208904 | tf_op jit(solution)/shard_map/ppermute | solution.py:475
  20.9 0.1 collective-permute-start.12
  21.0 1.7 %collective-permute-start.6 = (s16[272,128]{1,0:T(8,128)(2,1)S(1)}, s16[272,128]{1,0:T(8,128)(2,1)S(1)}, u32[]{:S(2)}, u32[]{:S(2)}) collective-permute-start(s16[272,128]{1,0:T(8,128)(2,1)S(1)} %get-tuple-element.32), channel_id=1, source_target_pairs={{0,4},{4,0},{8,12},{12,8},{16,20},{20,16},{24,28},{28,24},{1,5},{5... | collective-permute-start | bytes 208904 | tf_op jit(solution)/shard_map/ppermute | solution.py:475
  22.7 0.1 collective-permute-start.7
  22.7 0.0 collective-permute-done.10.refs_5_
  22.7 1.6 %collective-permute-start.8 = (s16[272,128]{1,0:T(8,128)(2,1)S(1)}, s16[272,128]{1,0:T(8,128)(2,1)S(1)}, u32[]{:S(2)}, u32[]{:S(2)}) collective-permute-start(s16[272,128]{1,0:T(8,128)(2,1)S(1)} %get-tuple-element.34), channel_id=1, source_target_pairs={{0,16},{4,20},{8,24},{12,28},{16,0},{20,4},{24,8},{28,12},{1,17},{... | collective-permute-start | bytes 208904 | tf_op jit(solution)/shard_map/ppermute | solution.py:475
  24.3 0.0 collective-permute-done.11.refs_6_
  24.4 0.3 collective-permute-start.9
  24.6 3.1 %gram_inverse.1.refs_8_ = f32[128,128]{1,0:T(8,128)S(1)} custom-call(f32[1,256]{1,0:T(1,128)S(1)} %bitcast.8, f32[64,256]{1,0:T(8,128)S(1)} %copy-done.5), custom_call_target="tpu_custom_call" | custom-call | flops 5000000000 | bytes 200000 | tf_op jit(solution)/shard_map/gram_inverse/pallas_call | solution.py:220
  27.7 0.0 collective-permute-done.12.refs_7_
  27.7 0.0 collective-permute-done.6.refs_1_
  27.8 0.1 collective-permute-done.7.refs_2_
  27.9 0.0 collective-permute-done.8.refs_3_
  27.9 0.6 %collective-permute-done.9.refs_4_ = s16[272,128]{1,0:T(8,128)(2,1)S(1)} collective-permute-done((s16[272,128]{1,0:T(8,128)(2,1)S(1)}, s16[272,128]{1,0:T(8,128)(2,1)S(1)}, u32[]{:S(2)}, u32[]{:S(2)}) %collective-permute-start.9) | collective-permute-done | bytes 69664 | tf_op jit(solution)/shard_map/ppermute | solution.py:475
  28.5 1.4 %sum_and_solve.1 = f32[16,8,8,128]{3,2,1,0:T(8,128)} custom-call(f32[2,128,128]{2,1,0:T(8,128)S(1)} %get-tuple-element.31.refs_0_, s16[272,128]{1,0:T(8,128)(2,1)S(1)} %collective-permute-done.6.refs_1_, s16[272,128]{1,0:T(8,128)(2,1)S(1)} %collective-permute-done.7.refs_2_, s16[272,128]{1,0:T(8,128)(2,1)S(1)} %collective-permute-done.8.refs_3_, ...), custom_call_target="tpu_custom_call" | custom-call | tf_op jit(solution)/shard_map/sum_and_solve/pallas_call | solution.py:412
  (3 shorter events, 0.0 us)
Async XLA Ops:
  0.0 7.7 %copy-start.5 = (f32[64,256]{1,0:T(8,128)S(1)}, f32[64,256]{1,0:T(8,128)}, u32[]{:S(2)}) copy-start(f32[64,256]{1,0:T(8,128)} %constant.25.clone.zern_ref) | copy-start | bytes 196612
  0.0 7.7 %copy-start.4 = (f32[256,512]{1,0:T(8,128)S(1)}, f32[256,512]{1,0:T(8,128)}, u32[]{:S(2)}) copy-start(f32[256,512]{1,0:T(8,128)} %constant.26.clone.dft_ref) | copy-start | bytes 1572868
  0.0 7.7 %copy-start.1 = (s32[8]{0:T(128)S(1)}, s32[8]{0:T(128)}, u32[]{:S(2)}) copy-start(s32[8]{0:T(128)} %index_ref.1) | copy-start | bytes 100
  0.0 7.7 %copy-start.3 = (f32[256]{0:T(256)S(1)}, f32[256]{0:T(256)}, u32[]{:S(2)}) copy-start(f32[256]{0:T(256)} %param.12) | copy-start | bytes 3076
  0.0 7.7 %copy-start.2 = (s32[2048]{0:T(1024)S(1)}, s32[2048]{0:T(1024)}, u32[]{:S(2)}) copy-start(s32[2048]{0:T(1024)} %param.11) | copy-start | bytes 24580
  2.2 7.9 %collective-permute-start.3 = (bf16[2,8,2048]{2,1,0:T(8,128)(2,1)S(1)}, bf16[2,8,2048]{2,1,0:T(8,128)(2,1)S(1)}, u32[]{:S(2)}, u32[]{:S(2)}) collective-permute-start(bf16[2,8,2048]{2,1,0:T(8,128)(2,1)S(1)} %get-tuple-element.26.args_0_), channel_id=1, source_target_pairs={{0,2},{1,3},{2,0},{3,1},{4,6},{5,7},{6,4},{7,5},{8,10},{9,11},{10,... | collective-permute-start | bytes 196616 | tf_op jit(solution)/shard_map/ppermute | solution.py:436
  6.1 6.2 %collective-permute-start.4 = (bf16[2,8,2048]{2,1,0:T(8,128)(2,1)S(1)}, bf16[2,8,2048]{2,1,0:T(8,128)(2,1)S(1)}, u32[]{:S(2)}, u32[]{:S(2)}) collective-permute-start(bf16[2,8,2048]{2,1,0:T(8,128)(2,1)S(1)} %get-tuple-element.26.args_0_), channel_id=1, source_target_pairs={{0,3},{1,2},{2,1},{3,0},{4,7},{5,6},{6,5},{7,4},{8,11},{9,10},{10,... | collective-permute-start | bytes 196616 | tf_op jit(solution)/shard_map/ppermute | solution.py:436
  7.2 5.3 %collective-permute-start.5 = (bf16[2,8,2048]{2,1,0:T(8,128)(2,1)S(1)}, bf16[2,8,2048]{2,1,0:T(8,128)(2,1)S(1)}, u32[]{:S(2)}, u32[]{:S(2)}) collective-permute-start(bf16[2,8,2048]{2,1,0:T(8,128)(2,1)S(1)} %get-tuple-element.26.args_0_), channel_id=1, source_target_pairs={{0,1},{1,0},{2,3},{3,2},{4,5},{5,4},{6,7},{7,6},{8,9},{9,8},{10,11... | collective-permute-start | bytes 196616 | tf_op jit(solution)/shard_map/ppermute | solution.py:436
  7.7 4.7 %copy-start = (bf16[2,2,128,2048]{3,2,1,0:T(8,128)(2,1)S(1)}, bf16[2,2,128,2048]{3,2,1,0:T(8,128)(2,1)}, u32[]{:S(2)}) copy-start(bf16[2,2,128,2048]{3,2,1,0:T(8,128)(2,1)} %volt_ref.1) | copy-start | bytes 6291460
  18.2 4.6 %collective-permute-start.10 = (s16[272,128]{1,0:T(8,128)(2,1)S(1)}, s16[272,128]{1,0:T(8,128)(2,1)S(1)}, u32[]{:S(2)}, u32[]{:S(2)}) collective-permute-start(s16[272,128]{1,0:T(8,128)(2,1)S(1)} %get-tuple-element.36), channel_id=1, source_target_pairs={{0,8},{4,12},{8,0},{12,4},{16,24},{20,28},{24,16},{28,20},{1,9},{5... | collective-permute-start | bytes 208904 | tf_op jit(solution)/shard_map/ppermute | solution.py:475
  18.2 6.1 %collective-permute-start.11 = (s16[272,128]{1,0:T(8,128)(2,1)S(1)}, s16[272,128]{1,0:T(8,128)(2,1)S(1)}, u32[]{:S(2)}, u32[]{:S(2)}) collective-permute-start(s16[272,128]{1,0:T(8,128)(2,1)S(1)} %get-tuple-element.37), channel_id=1, source_target_pairs={{0,20},{4,16},{8,28},{12,24},{16,4},{20,0},{24,12},{28,8},{1,21},{... | collective-permute-start | bytes 208904 | tf_op jit(solution)/shard_map/ppermute | solution.py:475
  20.9 6.8 %collective-permute-start.12 = (s16[272,128]{1,0:T(8,128)(2,1)S(1)}, s16[272,128]{1,0:T(8,128)(2,1)S(1)}, u32[]{:S(2)}, u32[]{:S(2)}) collective-permute-start(s16[272,128]{1,0:T(8,128)(2,1)S(1)} %get-tuple-element.38), channel_id=1, source_target_pairs={{0,28},{4,24},{8,20},{12,16},{16,12},{20,8},{24,4},{28,0},{1,29},{... | collective-permute-start | bytes 208904 | tf_op jit(solution)/shard_map/ppermute | solution.py:475
  21.0 6.7 %collective-permute-start.6 = (s16[272,128]{1,0:T(8,128)(2,1)S(1)}, s16[272,128]{1,0:T(8,128)(2,1)S(1)}, u32[]{:S(2)}, u32[]{:S(2)}) collective-permute-start(s16[272,128]{1,0:T(8,128)(2,1)S(1)} %get-tuple-element.32), channel_id=1, source_target_pairs={{0,4},{4,0},{8,12},{12,8},{16,20},{20,16},{24,28},{28,24},{1,5},{5... | collective-permute-start | bytes 208904 | tf_op jit(solution)/shard_map/ppermute | solution.py:475
  22.7 5.2 %collective-permute-start.7 = (s16[272,128]{1,0:T(8,128)(2,1)S(1)}, s16[272,128]{1,0:T(8,128)(2,1)S(1)}, u32[]{:S(2)}, u32[]{:S(2)}) collective-permute-start(s16[272,128]{1,0:T(8,128)(2,1)S(1)} %get-tuple-element.33), channel_id=1, source_target_pairs={{0,12},{4,8},{8,4},{12,0},{16,28},{20,24},{24,20},{28,16},{1,13},{... | collective-permute-start | bytes 208904 | tf_op jit(solution)/shard_map/ppermute | solution.py:475
  22.7 5.2 %collective-permute-start.8 = (s16[272,128]{1,0:T(8,128)(2,1)S(1)}, s16[272,128]{1,0:T(8,128)(2,1)S(1)}, u32[]{:S(2)}, u32[]{:S(2)}) collective-permute-start(s16[272,128]{1,0:T(8,128)(2,1)S(1)} %get-tuple-element.34), channel_id=1, source_target_pairs={{0,16},{4,20},{8,24},{12,28},{16,0},{20,4},{24,8},{28,12},{1,17},{... | collective-permute-start | bytes 208904 | tf_op jit(solution)/shard_map/ppermute | solution.py:475
  24.4 4.1 %collective-permute-start.9 = (s16[272,128]{1,0:T(8,128)(2,1)S(1)}, s16[272,128]{1,0:T(8,128)(2,1)S(1)}, u32[]{:S(2)}, u32[]{:S(2)}) collective-permute-start(s16[272,128]{1,0:T(8,128)(2,1)S(1)} %get-tuple-element.35), channel_id=1, source_target_pairs={{0,24},{4,28},{8,16},{12,20},{16,8},{20,12},{24,0},{28,4},{1,25},{... | collective-permute-start | bytes 208904 | tf_op jit(solution)/shard_map/ppermute | solution.py:475

commit v6 on v5

--- a/solution.py
+++ b/solution.py
@@ -211,15 +211,17 @@
     )
     inverse = invert(gram)
     zeros = jnp.zeros_like(inverse)
-    out_ref[...] = jnp.concatenate(
+    inverse = jnp.concatenate(
         [jnp.concatenate([inverse, zeros], axis=1), jnp.concatenate([zeros, inverse], axis=1)], axis=0
     )
+    high, low = split(inverse, 2)
+    out_ref[...] = jnp.concatenate([high, high, low], axis=0)
 
 
 def gram_inverse(weight):
     return pl.pallas_call(
         inverse_kernel,
-        out_shape=jax.ShapeDtypeStruct((2 * ZERN, 2 * ZERN), jnp.float32),
+        out_shape=jax.ShapeDtypeStruct((6 * ZERN, 2 * ZERN), jnp.bfloat16),
         name="gram_inverse",
         compiler_params=pltpu.CompilerParams(vmem_limit_bytes=4 * 2**20),
         cost_estimate=pl.CostEstimate(flops=5_000_000_000, bytes_accessed=200_000, transcendentals=0),
@@ -397,7 +399,9 @@
                 else:
                     part = ins[at][c].reshape(own * rows, terms)
                 total = part if total is None else total + part
-            solved = jnp.dot(total, inverse_ref[...], precision=HIGHEST, preferred_element_type=jnp.float32)
+            high, low = split(total, 2)
+            pieces = jnp.concatenate([high, low, high], axis=1)
+            solved = jnp.dot(pieces, inverse_ref[...], preferred_element_type=jnp.float32)
             stage_ref[dc, :, c] = solved.reshape(own, rows, terms)
         to = out_ref.at[:, pl.ds(source * chans, chans)]
         copies.append(pltpu.make_async_copy(stage_ref.at[dc], to, sems.at[dc]))

time: 30 us -> 29.9 us (level)
  Pallas kernels: 13.4 us -> 12.9 us
    ppermute x3, starting transfers between devices: 5.43 us -> 5.84 us  [to_all(): return [own] + [lax.ppermute(own, 'stat', pairs) for pairs in shifts]]
    pallas_call x1, Pallas kernels: 2.2 us -> 1.81 us  [pick(): pl.pallas_call(pick_kernel, in_specs=[pl.BlockSpec(memory_space=pltpu.HBM...]
where the time goes in v6:
time: 29.9 us; the launch traced here: 29.8 us
  Pallas kernels  12.9 us (43%)
  starting transfers between devices  12.2 us (41%)
  waiting for transfers between devices  3.2 us (11%)
  between operations  0.77 us (3%)
  other arithmetic  0.76 us (3%)
    ppermute x7, starting transfers between devices, on_device(): x = lax.ppermute(x, ('chan', 'tm'), pairs)  6.32 us
    ppermute x3, starting transfers between devices, to_all(): return [own] + [lax.ppermute(own, 'stat', pairs) for pairs in shifts]  5.84 us
    pallas_call x1, Pallas kernels, correlate(): pl.pallas_call(functools.partial(correlate_kernel, owners, len(ref_parts)...  5.71 us
    pallas_call x1, Pallas kernels, gram_inverse(): pl.pallas_call(inverse_kernel, out_shape=jax.ShapeDtypeStruct((6 * ZERN,...  3.08 us
    ppermute x3, waiting for transfers between devices, to_all(): return [own] + [lax.ppermute(own, 'stat', pairs) for pairs in shifts]  2.37 us
    pallas_call x1, Pallas kernels, pick(): pl.pallas_call(pick_kernel, in_specs=[pl.BlockSpec(memory_space=pltpu.HBM...  1.81 us
    pallas_call x1, Pallas kernels, collect(): pl.pallas_call(functools.partial(collect_kernel, order, shape), in_specs=...  1.33 us
    pallas_call x1, Pallas kernels, tables(): pl.pallas_call(functools.partial(tables_kernel, scale), out_shape=jax.Sha...  0.99 us
  transfers between devices with their start and end apart: 10, of which 4 were waited for; matrix products, arithmetic and copies ran while one was open for 3% of the time, Pallas kernels for 14%

profile of v6, /device:TPU:0, one launch (start us, length us, event | category | flops | bytes accessed | tf_op | source)
XLA Modules:
  0.0 29.8 jit_solution(4202139896094721368)
XLA Ops:
  0.0 0.0 copy-start.5
  0.0 0.0 copy-start.4
  0.0 0.0 copy-start.1
  0.0 0.0 copy-start.3
  0.0 0.0 copy-start.2
  0.0 1.8 %pick_references.1 = (bf16[2,8,2048]{2,1,0:T(8,128)(2,1)S(1)}, bf16[2,8,2048]{2,1,0:T(8,128)(2,1)S(1)}) custom-call(s32[8]{0:T(128)} %index_ref.1, bf16[2,2,128,2048]{3,2,1,0:T(8,128)(2,1)} %volt_ref.1), custom_call_target="tpu_custom_call" | custom-call | tf_op jit(solution)/shard_map/pick_references/pallas_call | solution.py:116
  1.8 4.2 %collective-permute-start.3 = (bf16[2,8,2048]{2,1,0:T(8,128)(2,1)S(1)}, bf16[2,8,2048]{2,1,0:T(8,128)(2,1)S(1)}, u32[]{:S(2)}, u32[]{:S(2)}) collective-permute-start(bf16[2,8,2048]{2,1,0:T(8,128)(2,1)S(1)} %get-tuple-element.26.args_0_), channel_id=1, source_target_pairs={{0,2},{1,3},{2,0},{3,1},{4,6},{5,7},{6,4},{7,5},{8,10},{9,11},{10,... | collective-permute-start | bytes 196616 | tf_op jit(solution)/shard_map/ppermute | solution.py:440
  6.1 1.5 %collective-permute-start.4 = (bf16[2,8,2048]{2,1,0:T(8,128)(2,1)S(1)}, bf16[2,8,2048]{2,1,0:T(8,128)(2,1)S(1)}, u32[]{:S(2)}, u32[]{:S(2)}) collective-permute-start(bf16[2,8,2048]{2,1,0:T(8,128)(2,1)S(1)} %get-tuple-element.26.args_0_), channel_id=1, source_target_pairs={{0,3},{1,2},{2,1},{3,0},{4,7},{5,6},{6,5},{7,4},{8,11},{9,10},{10,... | collective-permute-start | bytes 196616 | tf_op jit(solution)/shard_map/ppermute | solution.py:440
  7.6 0.1 collective-permute-start.5
  7.7 0.0 copy-done.1
  7.7 0.0 copy-done.5
  7.7 0.0 copy-done.4
  7.7 0.0 copy-done.3
  7.7 0.0 copy-done.2
  7.7 0.0 copy-start
  7.7 1.0 %projection_per_sample.1.args_5_ = f32[128,2048]{1,0:T(8,128)S(1)} custom-call(f32[1,256]{1,0:T(1,128)S(1)} %bitcast.7, f32[64,256]{1,0:T(8,128)S(1)} %copy-done.5, f32[256,512]{1,0:T(8,128)S(1)} %copy-done.4, s32[1,2048]{1,0:T(1,128)S(1)} %bitcast.6), custom_call_target="tpu_custom_call" | custom-call | flops 4000000000 | bytes 2000000 | tf_op jit(solution)/shard_map/projection_per_sample/pallas_call | solution.py:198
  8.7 0.1 convert_reduce_fusion
  8.9 0.6 %reduce_max.9 = s32[]{:T(128)} reduce(s32[4]{0:T(128)S(1)} %convert_reduce_fusion, s32[]{:T(128)} %constant.23.clone.1), dimensions={0}, to_apply=%region_1.2 | reduce | flops 3 | bytes 24 | tf_op jit(solution)/shard_map/reduce_max | solution.py:444
  10.1 0.0 collective-permute-done.3.args_1_
  10.2 2.1 %collective-permute-done.4.args_2_ = bf16[2,8,2048]{2,1,0:T(8,128)(2,1)S(1)} collective-permute-done((bf16[2,8,2048]{2,1,0:T(8,128)(2,1)S(1)}, bf16[2,8,2048]{2,1,0:T(8,128)(2,1)S(1)}, u32[]{:S(2)}, u32[]{:S(2)}) %collective-permute-start.4) | collective-permute-done | bytes 65568 | tf_op jit(solution)/shard_map/ppermute | solution.py:440
  12.3 0.2 collective-permute-done.5.args_3_
  12.5 0.0 copy-done
  12.5 5.7 %correlate.1 = (f32[2,128,128]{2,1,0:T(8,128)S(1)}, s16[272,128]{1,0:T(8,128)(2,1)S(1)}, s16[272,128]{1,0:T(8,128)(2,1)S(1)}, s16[272,128]{1,0:T(8,128)(2,1)S(1)...) custom-call(s32[8]{0:T(128)S(1)} %copy-done.1, ...), custom_call_target="tpu_custom_call" | custom-call | flops 8600000512 | bytes 5000000 | tf_op jit(solution)/shard_map/correlate/pallas_call | solution.py:347
  18.2 0.1 collective-permute-start.10
  18.3 2.5 %collective-permute-start.11 = (s16[272,128]{1,0:T(8,128)(2,1)S(1)}, s16[272,128]{1,0:T(8,128)(2,1)S(1)}, u32[]{:S(2)}, u32[]{:S(2)}) collective-permute-start(s16[272,128]{1,0:T(8,128)(2,1)S(1)} %get-tuple-element.37), channel_id=1, source_target_pairs={{0,20},{4,16},{8,28},{12,24},{16,4},{20,0},{24,12},{28,8},{1,21},{... | collective-permute-start | bytes 208904 | tf_op jit(solution)/shard_map/ppermute | solution.py:479
  20.8 0.2 collective-permute-start.12
  21.1 1.5 %collective-permute-start.6 = (s16[272,128]{1,0:T(8,128)(2,1)S(1)}, s16[272,128]{1,0:T(8,128)(2,1)S(1)}, u32[]{:S(2)}, u32[]{:S(2)}) collective-permute-start(s16[272,128]{1,0:T(8,128)(2,1)S(1)} %get-tuple-element.32), channel_id=1, source_target_pairs={{0,4},{4,0},{8,12},{12,8},{16,20},{20,16},{24,28},{28,24},{1,5},{5... | collective-permute-start | bytes 208904 | tf_op jit(solution)/shard_map/ppermute | solution.py:479
  22.6 0.2 collective-permute-start.7
  22.8 0.0 collective-permute-done.10.refs_5_
  22.8 1.5 %collective-permute-start.8 = (s16[272,128]{1,0:T(8,128)(2,1)S(1)}, s16[272,128]{1,0:T(8,128)(2,1)S(1)}, u32[]{:S(2)}, u32[]{:S(2)}) collective-permute-start(s16[272,128]{1,0:T(8,128)(2,1)S(1)} %get-tuple-element.34), channel_id=1, source_target_pairs={{0,16},{4,20},{8,24},{12,28},{16,0},{20,4},{24,8},{28,12},{1,17},{... | collective-permute-start | bytes 208904 | tf_op jit(solution)/shard_map/ppermute | solution.py:479
  24.3 0.0 collective-permute-done.11.refs_6_
  24.3 0.3 %collective-permute-start.9 = (s16[272,128]{1,0:T(8,128)(2,1)S(1)}, s16[272,128]{1,0:T(8,128)(2,1)S(1)}, u32[]{:S(2)}, u32[]{:S(2)}) collective-permute-start(s16[272,128]{1,0:T(8,128)(2,1)S(1)} %get-tuple-element.35), channel_id=1, source_target_pairs={{0,24},{4,28},{8,16},{12,20},{16,8},{20,12},{24,0},{28,4},{1,25},{... | collective-permute-start | bytes 208904 | tf_op jit(solution)/shard_map/ppermute | solution.py:479
  24.6 3.1 %gram_inverse.1.refs_8_ = bf16[384,128]{1,0:T(8,128)(2,1)S(1)} custom-call(f32[1,256]{1,0:T(1,128)S(1)} %bitcast.8, f32[64,256]{1,0:T(8,128)S(1)} %copy-done.5), custom_call_target="tpu_custom_call" | custom-call | flops 5000000000 | bytes 200000 | tf_op jit(solution)/shard_map/gram_inverse/pallas_call | solution.py:222
  27.7 0.0 collective-permute-done.12.refs_7_
  27.7 0.0 collective-permute-done.6.refs_1_
  27.7 0.2 collective-permute-done.7.refs_2_
  27.9 0.0 collective-permute-done.8.refs_3_
  27.9 0.6 %collective-permute-done.9.refs_4_ = s16[272,128]{1,0:T(8,128)(2,1)S(1)} collective-permute-done((s16[272,128]{1,0:T(8,128)(2,1)S(1)}, s16[272,128]{1,0:T(8,128)(2,1)S(1)}, u32[]{:S(2)}, u32[]{:S(2)}) %collective-permute-start.9) | collective-permute-done | bytes 69664 | tf_op jit(solution)/shard_map/ppermute | solution.py:479
  28.5 1.3 %sum_and_solve.1 = f32[16,8,8,128]{3,2,1,0:T(8,128)} custom-call(f32[2,128,128]{2,1,0:T(8,128)S(1)} %get-tuple-element.31.refs_0_, s16[272,128]{1,0:T(8,128)(2,1)S(1)} %collective-permute-done.6.refs_1_, s16[272,128]{1,0:T(8,128)(2,1)S(1)} %collective-permute-done.7.refs_2_, s16[272,128]{1,0:T(8,128)(2,1)S(1)} %collective-permute-done.8.refs_3_, ...), custom_call_target="tpu_custom_call" | custom-call | tf_op jit(solution)/shard_map/sum_and_solve/pallas_call | solution.py:416
  (3 shorter events, 0.0 us)
Async XLA Ops:
  0.0 7.7 %copy-start.5 = (f32[64,256]{1,0:T(8,128)S(1)}, f32[64,256]{1,0:T(8,128)}, u32[]{:S(2)}) copy-start(f32[64,256]{1,0:T(8,128)} %constant.25.clone.zern_ref) | copy-start | bytes 196612
  0.0 7.7 %copy-start.4 = (f32[256,512]{1,0:T(8,128)S(1)}, f32[256,512]{1,0:T(8,128)}, u32[]{:S(2)}) copy-start(f32[256,512]{1,0:T(8,128)} %constant.26.clone.dft_ref) | copy-start | bytes 1572868
  0.0 7.7 %copy-start.1 = (s32[8]{0:T(128)S(1)}, s32[8]{0:T(128)}, u32[]{:S(2)}) copy-start(s32[8]{0:T(128)} %index_ref.1) | copy-start | bytes 100
  0.0 7.7 %copy-start.3 = (f32[256]{0:T(256)S(1)}, f32[256]{0:T(256)}, u32[]{:S(2)}) copy-start(f32[256]{0:T(256)} %param.12) | copy-start | bytes 3076
  0.0 7.7 %copy-start.2 = (s32[2048]{0:T(1024)S(1)}, s32[2048]{0:T(1024)}, u32[]{:S(2)}) copy-start(s32[2048]{0:T(1024)} %param.11) | copy-start | bytes 24580
  1.8 8.3 %collective-permute-start.3 = (bf16[2,8,2048]{2,1,0:T(8,128)(2,1)S(1)}, bf16[2,8,2048]{2,1,0:T(8,128)(2,1)S(1)}, u32[]{:S(2)}, u32[]{:S(2)}) collective-permute-start(bf16[2,8,2048]{2,1,0:T(8,128)(2,1)S(1)} %get-tuple-element.26.args_0_), channel_id=1, source_target_pairs={{0,2},{1,3},{2,0},{3,1},{4,6},{5,7},{6,4},{7,5},{8,10},{9,11},{10,... | collective-permute-start | bytes 196616 | tf_op jit(solution)/shard_map/ppermute | solution.py:440
  6.1 6.2 %collective-permute-start.4 = (bf16[2,8,2048]{2,1,0:T(8,128)(2,1)S(1)}, bf16[2,8,2048]{2,1,0:T(8,128)(2,1)S(1)}, u32[]{:S(2)}, u32[]{:S(2)}) collective-permute-start(bf16[2,8,2048]{2,1,0:T(8,128)(2,1)S(1)} %get-tuple-element.26.args_0_), channel_id=1, source_target_pairs={{0,3},{1,2},{2,1},{3,0},{4,7},{5,6},{6,5},{7,4},{8,11},{9,10},{10,... | collective-permute-start | bytes 196616 | tf_op jit(solution)/shard_map/ppermute | solution.py:440
  7.6 5.0 %collective-permute-start.5 = (bf16[2,8,2048]{2,1,0:T(8,128)(2,1)S(1)}, bf16[2,8,2048]{2,1,0:T(8,128)(2,1)S(1)}, u32[]{:S(2)}, u32[]{:S(2)}) collective-permute-start(bf16[2,8,2048]{2,1,0:T(8,128)(2,1)S(1)} %get-tuple-element.26.args_0_), channel_id=1, source_target_pairs={{0,1},{1,0},{2,3},{3,2},{4,5},{5,4},{6,7},{7,6},{8,9},{9,8},{10,11... | collective-permute-start | bytes 196616 | tf_op jit(solution)/shard_map/ppermute | solution.py:440
  7.7 4.8 %copy-start = (bf16[2,2,128,2048]{3,2,1,0:T(8,128)(2,1)S(1)}, bf16[2,2,128,2048]{3,2,1,0:T(8,128)(2,1)}, u32[]{:S(2)}) copy-start(bf16[2,2,128,2048]{3,2,1,0:T(8,128)(2,1)} %volt_ref.1) | copy-start | bytes 6291460
  18.2 4.5 %collective-permute-start.10 = (s16[272,128]{1,0:T(8,128)(2,1)S(1)}, s16[272,128]{1,0:T(8,128)(2,1)S(1)}, u32[]{:S(2)}, u32[]{:S(2)}) collective-permute-start(s16[272,128]{1,0:T(8,128)(2,1)S(1)} %get-tuple-element.36), channel_id=1, source_target_pairs={{0,8},{4,12},{8,0},{12,4},{16,24},{20,28},{24,16},{28,20},{1,9},{5... | collective-permute-start | bytes 208904 | tf_op jit(solution)/shard_map/ppermute | solution.py:479
  18.3 6.0 %collective-permute-start.11 = (s16[272,128]{1,0:T(8,128)(2,1)S(1)}, s16[272,128]{1,0:T(8,128)(2,1)S(1)}, u32[]{:S(2)}, u32[]{:S(2)}) collective-permute-start(s16[272,128]{1,0:T(8,128)(2,1)S(1)} %get-tuple-element.37), channel_id=1, source_target_pairs={{0,20},{4,16},{8,28},{12,24},{16,4},{20,0},{24,12},{28,8},{1,21},{... | collective-permute-start | bytes 208904 | tf_op jit(solution)/shard_map/ppermute | solution.py:479
  20.8 6.8 %collective-permute-start.12 = (s16[272,128]{1,0:T(8,128)(2,1)S(1)}, s16[272,128]{1,0:T(8,128)(2,1)S(1)}, u32[]{:S(2)}, u32[]{:S(2)}) collective-permute-start(s16[272,128]{1,0:T(8,128)(2,1)S(1)} %get-tuple-element.38), channel_id=1, source_target_pairs={{0,28},{4,24},{8,20},{12,16},{16,12},{20,8},{24,4},{28,0},{1,29},{... | collective-permute-start | bytes 208904 | tf_op jit(solution)/shard_map/ppermute | solution.py:479
  21.1 6.6 %collective-permute-start.6 = (s16[272,128]{1,0:T(8,128)(2,1)S(1)}, s16[272,128]{1,0:T(8,128)(2,1)S(1)}, u32[]{:S(2)}, u32[]{:S(2)}) collective-permute-start(s16[272,128]{1,0:T(8,128)(2,1)S(1)} %get-tuple-element.32), channel_id=1, source_target_pairs={{0,4},{4,0},{8,12},{12,8},{16,20},{20,16},{24,28},{28,24},{1,5},{5... | collective-permute-start | bytes 208904 | tf_op jit(solution)/shard_map/ppermute | solution.py:479
  22.6 5.3 %collective-permute-start.7 = (s16[272,128]{1,0:T(8,128)(2,1)S(1)}, s16[272,128]{1,0:T(8,128)(2,1)S(1)}, u32[]{:S(2)}, u32[]{:S(2)}) collective-permute-start(s16[272,128]{1,0:T(8,128)(2,1)S(1)} %get-tuple-element.33), channel_id=1, source_target_pairs={{0,12},{4,8},{8,4},{12,0},{16,28},{20,24},{24,20},{28,16},{1,13},{... | collective-permute-start | bytes 208904 | tf_op jit(solution)/shard_map/ppermute | solution.py:479
  22.8 5.1 %collective-permute-start.8 = (s16[272,128]{1,0:T(8,128)(2,1)S(1)}, s16[272,128]{1,0:T(8,128)(2,1)S(1)}, u32[]{:S(2)}, u32[]{:S(2)}) collective-permute-start(s16[272,128]{1,0:T(8,128)(2,1)S(1)} %get-tuple-element.34), channel_id=1, source_target_pairs={{0,16},{4,20},{8,24},{12,28},{16,0},{20,4},{24,8},{28,12},{1,17},{... | collective-permute-start | bytes 208904 | tf_op jit(solution)/shard_map/ppermute | solution.py:479
  24.3 4.2 %collective-permute-start.9 = (s16[272,128]{1,0:T(8,128)(2,1)S(1)}, s16[272,128]{1,0:T(8,128)(2,1)S(1)}, u32[]{:S(2)}, u32[]{:S(2)}) collective-permute-start(s16[272,128]{1,0:T(8,128)(2,1)S(1)} %get-tuple-element.35), channel_id=1, source_target_pairs={{0,24},{4,28},{8,16},{12,20},{16,8},{20,12},{24,0},{28,4},{1,25},{... | collective-permute-start | bytes 208904 | tf_op jit(solution)/shard_map/ppermute | solution.py:479

commit v7 on v6

--- a/solution.py
+++ b/solution.py
@@ -78,7 +78,7 @@
 
 
 def pick_kernel(index_hbm, volt_hbm, *rest):
-    *out_refs, index_ref, volt_ref, rows_ref, index_sem, volt_sem = rest
+    *out_refs, index_ref, volt_ref, rows_ref, group_ref, index_sem, volt_sem = rest
     chans, parts, stations, _ = volt_ref.shape
     count = rows_ref.shape[2] // parts
     index_copy = pltpu.make_async_copy(index_hbm, index_ref, index_sem)
@@ -99,10 +99,11 @@
             for c in range(chans):
                 for k in range(parts):
                     group = volt_ref[c, k, pl.ds(begin, GROUP), :].astype(jnp.float32)
-                    row = lax.broadcasted_iota(jnp.int32, group.shape, 0)
-                    group = jnp.where(row == local - begin, group, 0.0)
+                    group_ref[c, k] = group
+            for c in range(chans):
+                for k in range(parts):
                     to = pl.ds(k * count + lax.rem(slot, count), 1)
-                    rows_ref[slot // count, c, to, :] = jnp.sum(group, axis=0, keepdims=True)
+                    rows_ref[slot // count, c, to, :] = group_ref[c, k, pl.ds(local - begin, 1), :]
 
     for i, out_ref in enumerate(out_refs):
         out_ref[...] = rows_ref[i].astype(jnp.bfloat16)
@@ -122,6 +123,7 @@
             pltpu.SMEM((refs,), jnp.int32),
             pltpu.VMEM(voltages.shape, jnp.bfloat16),
             pltpu.VMEM((2,) + half, jnp.float32),
+            pltpu.VMEM((chans, parts, GROUP, times), jnp.float32),
             pltpu.SemaphoreType.DMA,
             pltpu.SemaphoreType.DMA,
         ],

time: 29.9 us -> 29.7 us (level)
  no operation moved by 1% of the time
where the time goes in v7:
time: 29.7 us; the launch traced here: 29.5 us
  Pallas kernels  12.9 us (43%)
  starting transfers between devices  12.1 us (41%)
  waiting for transfers between devices  2.94 us (10%)
  between operations  0.77 us (3%)
  other arithmetic  0.76 us (3%)
    ppermute x7, starting transfers between devices, on_device(): x = lax.ppermute(x, ('chan', 'tm'), pairs)  6.38 us
    ppermute x3, starting transfers between devices, to_all(): return [own] + [lax.ppermute(own, 'stat', pairs) for pairs in shifts]  5.74 us
    pallas_call x1, Pallas kernels, correlate(): pl.pallas_call(functools.partial(correlate_kernel, owners, len(ref_parts)...  5.71 us
    pallas_call x1, Pallas kernels, gram_inverse(): pl.pallas_call(inverse_kernel, out_shape=jax.ShapeDtypeStruct((6 * ZERN,...  3.08 us
    ppermute x3, waiting for transfers between devices, to_all(): return [own] + [lax.ppermute(own, 'stat', pairs) for pairs in shifts]  2.2 us
    pallas_call x1, Pallas kernels, pick(): pl.pallas_call(pick_kernel, in_specs=[pl.BlockSpec(memory_space=pltpu.HBM...  1.82 us
    pallas_call x1, Pallas kernels, collect(): pl.pallas_call(functools.partial(collect_kernel, order, shape), in_specs=...  1.33 us
    pallas_call x1, Pallas kernels, tables(): pl.pallas_call(functools.partial(tables_kernel, scale), out_shape=jax.Sha...  0.99 us
  transfers between devices with their start and end apart: 10, of which 4 were waited for; matrix products, arithmetic and copies ran while one was open for 3% of the time, Pallas kernels for 14%

profile of v7, /device:TPU:0, one launch (start us, length us, event | category | flops | bytes accessed | tf_op | source)
XLA Modules:
  0.0 29.5 jit_solution(7301154402760074980)
XLA Ops:
  0.0 0.0 copy-start.5
  0.0 0.0 copy-start.4
  0.0 0.0 copy-start.1
  0.0 0.0 copy-start.3
  0.0 0.0 copy-start.2
  0.0 1.8 %pick_references.1 = (bf16[2,8,2048]{2,1,0:T(8,128)(2,1)S(1)}, bf16[2,8,2048]{2,1,0:T(8,128)(2,1)S(1)}) custom-call(s32[8]{0:T(128)} %index_ref.1, bf16[2,2,128,2048]{3,2,1,0:T(8,128)(2,1)} %volt_ref.1), custom_call_target="tpu_custom_call" | custom-call | tf_op jit(solution)/shard_map/pick_references/pallas_call | solution.py:117
  1.8 4.0 %collective-permute-start.3 = (bf16[2,8,2048]{2,1,0:T(8,128)(2,1)S(1)}, bf16[2,8,2048]{2,1,0:T(8,128)(2,1)S(1)}, u32[]{:S(2)}, u32[]{:S(2)}) collective-permute-start(bf16[2,8,2048]{2,1,0:T(8,128)(2,1)S(1)} %get-tuple-element.26.args_0_), channel_id=1, source_target_pairs={{0,2},{1,3},{2,0},{3,1},{4,6},{5,7},{6,4},{7,5},{8,10},{9,11},{10,... | collective-permute-start | bytes 196616 | tf_op jit(solution)/shard_map/ppermute | solution.py:442
  5.9 1.4 %collective-permute-start.4 = (bf16[2,8,2048]{2,1,0:T(8,128)(2,1)S(1)}, bf16[2,8,2048]{2,1,0:T(8,128)(2,1)S(1)}, u32[]{:S(2)}, u32[]{:S(2)}) collective-permute-start(bf16[2,8,2048]{2,1,0:T(8,128)(2,1)S(1)} %get-tuple-element.26.args_0_), channel_id=1, source_target_pairs={{0,3},{1,2},{2,1},{3,0},{4,7},{5,6},{6,5},{7,4},{8,11},{9,10},{10,... | collective-permute-start | bytes 196616 | tf_op jit(solution)/shard_map/ppermute | solution.py:442
  7.3 0.3 collective-permute-start.5
  7.6 0.0 copy-done.1
  7.6 0.0 copy-done.5
  7.6 0.0 copy-done.4
  7.6 0.0 copy-done.3
  7.6 0.0 copy-done.2
  7.6 0.0 copy-start
  7.6 1.0 %projection_per_sample.1.args_5_ = f32[128,2048]{1,0:T(8,128)S(1)} custom-call(f32[1,256]{1,0:T(1,128)S(1)} %bitcast.7, f32[64,256]{1,0:T(8,128)S(1)} %copy-done.5, f32[256,512]{1,0:T(8,128)S(1)} %copy-done.4, s32[1,2048]{1,0:T(1,128)S(1)} %bitcast.6), custom_call_target="tpu_custom_call" | custom-call | flops 4000000000 | bytes 2000000 | tf_op jit(solution)/shard_map/projection_per_sample/pallas_call | solution.py:200
  8.6 0.1 convert_reduce_fusion
  8.8 0.6 %reduce_max.9 = s32[]{:T(128)} reduce(s32[4]{0:T(128)S(1)} %convert_reduce_fusion, s32[]{:T(128)} %constant.23.clone.1), dimensions={0}, to_apply=%region_1.2 | reduce | flops 3 | bytes 24 | tf_op jit(solution)/shard_map/reduce_max | solution.py:446
  10.1 0.0 collective-permute-done.3.args_1_
  10.1 2.0 %collective-permute-done.4.args_2_ = bf16[2,8,2048]{2,1,0:T(8,128)(2,1)S(1)} collective-permute-done((bf16[2,8,2048]{2,1,0:T(8,128)(2,1)S(1)}, bf16[2,8,2048]{2,1,0:T(8,128)(2,1)S(1)}, u32[]{:S(2)}, u32[]{:S(2)}) %collective-permute-start.4) | collective-permute-done | bytes 65568 | tf_op jit(solution)/shard_map/ppermute | solution.py:442
  12.1 0.2 collective-permute-done.5.args_3_
  12.3 0.0 copy-done
  12.3 5.7 %correlate.1 = (f32[2,128,128]{2,1,0:T(8,128)S(1)}, s16[272,128]{1,0:T(8,128)(2,1)S(1)}, s16[272,128]{1,0:T(8,128)(2,1)S(1)}, s16[272,128]{1,0:T(8,128)(2,1)S(1)...) custom-call(s32[8]{0:T(128)S(1)} %copy-done.1, ...), custom_call_target="tpu_custom_call" | custom-call | flops 8600000512 | bytes 5000000 | tf_op jit(solution)/shard_map/correlate/pallas_call | solution.py:349
  18.0 0.1 collective-permute-start.10
  18.1 2.6 %collective-permute-start.11 = (s16[272,128]{1,0:T(8,128)(2,1)S(1)}, s16[272,128]{1,0:T(8,128)(2,1)S(1)}, u32[]{:S(2)}, u32[]{:S(2)}) collective-permute-start(s16[272,128]{1,0:T(8,128)(2,1)S(1)} %get-tuple-element.37), channel_id=1, source_target_pairs={{0,20},{4,16},{8,28},{12,24},{16,4},{20,0},{24,12},{28,8},{1,21},{... | collective-permute-start | bytes 208904 | tf_op jit(solution)/shard_map/ppermute | solution.py:481
  20.6 0.2 collective-permute-start.12
  20.8 1.6 %collective-permute-start.6 = (s16[272,128]{1,0:T(8,128)(2,1)S(1)}, s16[272,128]{1,0:T(8,128)(2,1)S(1)}, u32[]{:S(2)}, u32[]{:S(2)}) collective-permute-start(s16[272,128]{1,0:T(8,128)(2,1)S(1)} %get-tuple-element.32), channel_id=1, source_target_pairs={{0,4},{4,0},{8,12},{12,8},{16,20},{20,16},{24,28},{28,24},{1,5},{5... | collective-permute-start | bytes 208904 | tf_op jit(solution)/shard_map/ppermute | solution.py:481
  22.4 0.1 collective-permute-start.7
  22.5 0.0 collective-permute-done.10.refs_5_
  22.5 1.6 %collective-permute-start.8 = (s16[272,128]{1,0:T(8,128)(2,1)S(1)}, s16[272,128]{1,0:T(8,128)(2,1)S(1)}, u32[]{:S(2)}, u32[]{:S(2)}) collective-permute-start(s16[272,128]{1,0:T(8,128)(2,1)S(1)} %get-tuple-element.34), channel_id=1, source_target_pairs={{0,16},{4,20},{8,24},{12,28},{16,0},{20,4},{24,8},{28,12},{1,17},{... | collective-permute-start | bytes 208904 | tf_op jit(solution)/shard_map/ppermute | solution.py:481
  24.1 0.0 collective-permute-done.11.refs_6_
  24.1 0.3 %collective-permute-start.9 = (s16[272,128]{1,0:T(8,128)(2,1)S(1)}, s16[272,128]{1,0:T(8,128)(2,1)S(1)}, u32[]{:S(2)}, u32[]{:S(2)}) collective-permute-start(s16[272,128]{1,0:T(8,128)(2,1)S(1)} %get-tuple-element.35), channel_id=1, source_target_pairs={{0,24},{4,28},{8,16},{12,20},{16,8},{20,12},{24,0},{28,4},{1,25},{... | collective-permute-start | bytes 208904 | tf_op jit(solution)/shard_map/ppermute | solution.py:481
  24.4 3.1 %gram_inverse.1.refs_8_ = bf16[384,128]{1,0:T(8,128)(2,1)S(1)} custom-call(f32[1,256]{1,0:T(1,128)S(1)} %bitcast.8, f32[64,256]{1,0:T(8,128)S(1)} %copy-done.5), custom_call_target="tpu_custom_call" | custom-call | flops 5000000000 | bytes 200000 | tf_op jit(solution)/shard_map/gram_inverse/pallas_call | solution.py:224
  27.5 0.0 collective-permute-done.12.refs_7_
  27.5 0.0 collective-permute-done.6.refs_1_
  27.5 0.2 collective-permute-done.7.refs_2_
  27.7 0.0 collective-permute-done.8.refs_3_
  27.7 0.5 %collective-permute-done.9.refs_4_ = s16[272,128]{1,0:T(8,128)(2,1)S(1)} collective-permute-done((s16[272,128]{1,0:T(8,128)(2,1)S(1)}, s16[272,128]{1,0:T(8,128)(2,1)S(1)}, u32[]{:S(2)}, u32[]{:S(2)}) %collective-permute-start.9) | collective-permute-done | bytes 69664 | tf_op jit(solution)/shard_map/ppermute | solution.py:481
  28.2 1.3 %sum_and_solve.1 = f32[16,8,8,128]{3,2,1,0:T(8,128)} custom-call(f32[2,128,128]{2,1,0:T(8,128)S(1)} %get-tuple-element.31.refs_0_, s16[272,128]{1,0:T(8,128)(2,1)S(1)} %collective-permute-done.6.refs_1_, s16[272,128]{1,0:T(8,128)(2,1)S(1)} %collective-permute-done.7.refs_2_, s16[272,128]{1,0:T(8,128)(2,1)S(1)} %collective-permute-done.8.refs_3_, ...), custom_call_target="tpu_custom_call" | custom-call | tf_op jit(solution)/shard_map/sum_and_solve/pallas_call | solution.py:418
  (3 shorter events, 0.0 us)
Async XLA Ops:
  0.0 7.6 %copy-start.5 = (f32[64,256]{1,0:T(8,128)S(1)}, f32[64,256]{1,0:T(8,128)}, u32[]{:S(2)}) copy-start(f32[64,256]{1,0:T(8,128)} %constant.25.clone.zern_ref) | copy-start | bytes 196612
  0.0 7.6 %copy-start.4 = (f32[256,512]{1,0:T(8,128)S(1)}, f32[256,512]{1,0:T(8,128)}, u32[]{:S(2)}) copy-start(f32[256,512]{1,0:T(8,128)} %constant.26.clone.dft_ref) | copy-start | bytes 1572868
  0.0 7.6 %copy-start.1 = (s32[8]{0:T(128)S(1)}, s32[8]{0:T(128)}, u32[]{:S(2)}) copy-start(s32[8]{0:T(128)} %index_ref.1) | copy-start | bytes 100
  0.0 7.6 %copy-start.3 = (f32[256]{0:T(256)S(1)}, f32[256]{0:T(256)}, u32[]{:S(2)}) copy-start(f32[256]{0:T(256)} %param.12) | copy-start | bytes 3076
  0.0 7.6 %copy-start.2 = (s32[2048]{0:T(1024)S(1)}, s32[2048]{0:T(1024)}, u32[]{:S(2)}) copy-start(s32[2048]{0:T(1024)} %param.11) | copy-start | bytes 24580
  1.8 8.2 %collective-permute-start.3 = (bf16[2,8,2048]{2,1,0:T(8,128)(2,1)S(1)}, bf16[2,8,2048]{2,1,0:T(8,128)(2,1)S(1)}, u32[]{:S(2)}, u32[]{:S(2)}) collective-permute-start(bf16[2,8,2048]{2,1,0:T(8,128)(2,1)S(1)} %get-tuple-element.26.args_0_), channel_id=1, source_target_pairs={{0,2},{1,3},{2,0},{3,1},{4,6},{5,7},{6,4},{7,5},{8,10},{9,11},{10,... | collective-permute-start | bytes 196616 | tf_op jit(solution)/shard_map/ppermute | solution.py:442
  5.9 6.2 %collective-permute-start.4 = (bf16[2,8,2048]{2,1,0:T(8,128)(2,1)S(1)}, bf16[2,8,2048]{2,1,0:T(8,128)(2,1)S(1)}, u32[]{:S(2)}, u32[]{:S(2)}) collective-permute-start(bf16[2,8,2048]{2,1,0:T(8,128)(2,1)S(1)} %get-tuple-element.26.args_0_), channel_id=1, source_target_pairs={{0,3},{1,2},{2,1},{3,0},{4,7},{5,6},{6,5},{7,4},{8,11},{9,10},{10,... | collective-permute-start | bytes 196616 | tf_op jit(solution)/shard_map/ppermute | solution.py:442
  7.3 5.0 %collective-permute-start.5 = (bf16[2,8,2048]{2,1,0:T(8,128)(2,1)S(1)}, bf16[2,8,2048]{2,1,0:T(8,128)(2,1)S(1)}, u32[]{:S(2)}, u32[]{:S(2)}) collective-permute-start(bf16[2,8,2048]{2,1,0:T(8,128)(2,1)S(1)} %get-tuple-element.26.args_0_), channel_id=1, source_target_pairs={{0,1},{1,0},{2,3},{3,2},{4,5},{5,4},{6,7},{7,6},{8,9},{9,8},{10,11... | collective-permute-start | bytes 196616 | tf_op jit(solution)/shard_map/ppermute | solution.py:442
  7.6 4.6 %copy-start = (bf16[2,2,128,2048]{3,2,1,0:T(8,128)(2,1)S(1)}, bf16[2,2,128,2048]{3,2,1,0:T(8,128)(2,1)}, u32[]{:S(2)}) copy-start(bf16[2,2,128,2048]{3,2,1,0:T(8,128)(2,1)} %volt_ref.1) | copy-start | bytes 6291460
  18.0 4.5 %collective-permute-start.10 = (s16[272,128]{1,0:T(8,128)(2,1)S(1)}, s16[272,128]{1,0:T(8,128)(2,1)S(1)}, u32[]{:S(2)}, u32[]{:S(2)}) collective-permute-start(s16[272,128]{1,0:T(8,128)(2,1)S(1)} %get-tuple-element.36), channel_id=1, source_target_pairs={{0,8},{4,12},{8,0},{12,4},{16,24},{20,28},{24,16},{28,20},{1,9},{5... | collective-permute-start | bytes 208904 | tf_op jit(solution)/shard_map/ppermute | solution.py:481
  18.1 6.0 %collective-permute-start.11 = (s16[272,128]{1,0:T(8,128)(2,1)S(1)}, s16[272,128]{1,0:T(8,128)(2,1)S(1)}, u32[]{:S(2)}, u32[]{:S(2)}) collective-permute-start(s16[272,128]{1,0:T(8,128)(2,1)S(1)} %get-tuple-element.37), channel_id=1, source_target_pairs={{0,20},{4,16},{8,28},{12,24},{16,4},{20,0},{24,12},{28,8},{1,21},{... | collective-permute-start | bytes 208904 | tf_op jit(solution)/shard_map/ppermute | solution.py:481
  20.6 6.8 %collective-permute-start.12 = (s16[272,128]{1,0:T(8,128)(2,1)S(1)}, s16[272,128]{1,0:T(8,128)(2,1)S(1)}, u32[]{:S(2)}, u32[]{:S(2)}) collective-permute-start(s16[272,128]{1,0:T(8,128)(2,1)S(1)} %get-tuple-element.38), channel_id=1, source_target_pairs={{0,28},{4,24},{8,20},{12,16},{16,12},{20,8},{24,4},{28,0},{1,29},{... | collective-permute-start | bytes 208904 | tf_op jit(solution)/shard_map/ppermute | solution.py:481
  20.8 6.7 %collective-permute-start.6 = (s16[272,128]{1,0:T(8,128)(2,1)S(1)}, s16[272,128]{1,0:T(8,128)(2,1)S(1)}, u32[]{:S(2)}, u32[]{:S(2)}) collective-permute-start(s16[272,128]{1,0:T(8,128)(2,1)S(1)} %get-tuple-element.32), channel_id=1, source_target_pairs={{0,4},{4,0},{8,12},{12,8},{16,20},{20,16},{24,28},{28,24},{1,5},{5... | collective-permute-start | bytes 208904 | tf_op jit(solution)/shard_map/ppermute | solution.py:481
  22.4 5.3 %collective-permute-start.7 = (s16[272,128]{1,0:T(8,128)(2,1)S(1)}, s16[272,128]{1,0:T(8,128)(2,1)S(1)}, u32[]{:S(2)}, u32[]{:S(2)}) collective-permute-start(s16[272,128]{1,0:T(8,128)(2,1)S(1)} %get-tuple-element.33), channel_id=1, source_target_pairs={{0,12},{4,8},{8,4},{12,0},{16,28},{20,24},{24,20},{28,16},{1,13},{... | collective-permute-start | bytes 208904 | tf_op jit(solution)/shard_map/ppermute | solution.py:481
  22.5 5.1 %collective-permute-start.8 = (s16[272,128]{1,0:T(8,128)(2,1)S(1)}, s16[272,128]{1,0:T(8,128)(2,1)S(1)}, u32[]{:S(2)}, u32[]{:S(2)}) collective-permute-start(s16[272,128]{1,0:T(8,128)(2,1)S(1)} %get-tuple-element.34), channel_id=1, source_target_pairs={{0,16},{4,20},{8,24},{12,28},{16,0},{20,4},{24,8},{28,12},{1,17},{... | collective-permute-start | bytes 208904 | tf_op jit(solution)/shard_map/ppermute | solution.py:481
  24.1 4.1 %collective-permute-start.9 = (s16[272,128]{1,0:T(8,128)(2,1)S(1)}, s16[272,128]{1,0:T(8,128)(2,1)S(1)}, u32[]{:S(2)}, u32[]{:S(2)}) collective-permute-start(s16[272,128]{1,0:T(8,128)(2,1)S(1)} %get-tuple-element.35), channel_id=1, source_target_pairs={{0,24},{4,28},{8,16},{12,20},{16,8},{20,12},{24,0},{28,4},{1,25},{... | collective-permute-start | bytes 208904 | tf_op jit(solution)/shard_map/ppermute | solution.py:481
